TPU v7x, 32 devices: a whole 2x2x4 slice. The times are simulated.
32 devices in a mesh: groups: 2 (over x), img: 16 (over z, y, core).
Axes of the slice: x: 2, y: 2, z: 4, core: 2. Of those that a mesh axis runs over, the one named last changes fastest.
Arguments:
- images: bfloat16 [256, 4608], P(('groups', 'img')), parts along dimension 0, may hold values from -64 to 64
- class_refs: bfloat16 [96, 4608], P('groups', 'img'), parts along dimension 0, may hold values from -0.6 to 0.6
- sigma2: float32 [32, 16], P('groups'), parts along dimension 0, may hold values from 0.5 to 18
- ctf_group: int32 [256], P(('groups', 'img')), parts along dimension 0, may hold values from 0 to 15, as said below
- defocus_bin: int32 [256], P(('groups', 'img')), parts along dimension 0, may hold values from 0 to 31
Outputs:
- new_refs: float32 [96, 4608], P('groups', 'img'), parts along dimension 0
There are 2 independent parts, one for each index of `groups`. A program takes and returns all parts, laid end to end along the dimension named above; each array names one. Nothing has to cross between parts.
Inputs may be any that keep to these rules, and one draw needn't show every extreme that they name: `ctf_group`: never falls from one image to the next; every group appears.
All inputs are finite; a program needn't handle non-finite values.
Results may differ from a plain program's by a relative error of at most 0.0084.
Values may be sent and summed in bfloat16 or wider, within the bound.
No kernel may reach another device: no remote copies, remote signals or barrier semaphores. Data moves between devices by JAX's collectives and lax.ppermute only.
A program may use at most 128 MiB of HBM per device.

v0:
```python
import functools
import math

import jax
import jax.numpy as jnp
import numpy as np
from jax import lax
from jax.experimental import pallas as pl
from jax.experimental.pallas import tpu as pltpu
from jax.sharding import PartitionSpec as P

CLASSES = 48
ROT = 36
SHELLS = 16
ANG = 144
REACH = 3
SHIFTS = 49
BINS = 32
NGROUP = 16

STEP = ANG // ROT
CHANS = 2 * SHELLS
BLOCKS = CHANS // 2
BLOCK_COLS = 2 * ANG
LANES = CHANS * STEP
FREQS = ROT // 2 + 1
ROWS8 = 8
S_PAD = SHIFTS + 1
ROWS = S_PAD * ROWS8
LIVE = SHIFTS * ROWS8
COLS = 512
KPAD = 64
PAY = (FREQS + 1) * ROWS8
BF = jnp.bfloat16
F32 = jnp.float32
VMEM_LIMIT = 56 * 1024 * 1024


def block_order():
    return [m for m in range(0, BLOCKS, 2)] + [m for m in range(1, BLOCKS, 2)]


def lane_channel():
    chan, off = [], []
    for m in block_order():
        for cc in range(2):
            for d in range(STEP):
                chan.append(2 * m + cc)
                off.append(d)
    return np.array(chan), np.array(off)


def radius_of():
    return (np.arange(SHELLS, dtype=np.float64) + 1.0) / (2.0 * SHELLS)


def ctf_lanes():
    chan, _ = lane_channel()
    radius = (jnp.arange(SHELLS, dtype=F32) + 1.0) / (2.0 * SHELLS)
    defocus = 1.0 + jnp.arange(BINS, dtype=F32) / BINS
    table = -jnp.sin(80.0 * defocus[:, None] * radius[None, :] ** 2 + 0.1)
    return table[:, chan % SHELLS]


def shell_expand():
    chan, _ = lane_channel()
    return (np.arange(SHELLS)[:, None] == (chan % SHELLS)[None, :]).astype(np.float32)


def pixel_perm():
    table = np.zeros((BLOCK_COLS, BLOCK_COLS), np.float32)
    for b in range(ROT):
        for cc in range(2):
            for d in range(STEP):
                table[b * 8 + cc * STEP + d, cc * ANG + STEP * b + d] = 1.0
    return table


def phase_lanes():
    chan, off = lane_channel()
    shell = chan % SHELLS
    sign = np.where(chan < SHELLS, -1.0, 1.0)
    offsets = np.arange(2 * REACH + 1, dtype=np.float64) - REACH
    sx = np.repeat(offsets, 2 * REACH + 1)
    sy = np.tile(offsets, 2 * REACH + 1)
    angle = 2.0 * math.pi * (STEP * np.arange(ROT)[:, None] + off[None, :]) / ANG
    phase = (
        2.0
        * math.pi
        * radius_of()[shell][None, None, :]
        * (np.cos(angle)[None] * sx[:, None, None] + np.sin(angle)[None] * sy[:, None, None])
    )
    cos_t = np.zeros((S_PAD, ROT, LANES), np.float32)
    sin_t = np.zeros((S_PAD, ROT, LANES), np.float32)
    cos_t[:SHIFTS] = np.cos(phase)
    sin_t[:SHIFTS] = np.sin(phase) * sign[None, None, :]
    return cos_t, sin_t


def refs_transform():
    table = np.zeros((FREQS, 2, 2, STEP, 2, ANG), np.float64)
    for q in range(FREQS):
        scale = (1.0 if q in (0, ROT // 2) else 2.0) / ROT
        for d in range(STEP):
            b = np.arange(ROT)
            turn = 2.0 * math.pi * ((q * b) % ROT) / ROT
            for cc in range(2):
                table[q, 0, cc, d, cc, STEP * b + d] = scale * np.cos(turn)
                if q not in (0, ROT // 2):
                    table[q, 1, cc, d, cc, STEP * b + d] = -scale * np.sin(turn)
    return table.reshape(FREQS * 16, BLOCK_COLS)


def power_rows():
    table = np.zeros((2, STEP, 2, ANG), np.float32)
    for cc in range(2):
        table[cc, 0, cc, :] = -0.5
    return table.reshape(8, BLOCK_COLS)


def inverse_transform():
    real = np.zeros((FREQS + 1, 2, STEP, 2, ANG), np.float64)
    imag = np.zeros((FREQS + 1, 2, STEP, 2, ANG), np.float64)
    pick = np.zeros((FREQS + 1, 2, STEP, 2, ANG), np.float64)
    b = np.arange(ROT)
    for q in range(FREQS):
        scale = (1.0 if q in (0, ROT // 2) else 2.0) / ROT
        turn = 2.0 * math.pi * ((q * b) % ROT) / ROT
        for cc in range(2):
            for d in range(STEP):
                real[q, cc, d, cc, STEP * b + d] = scale * np.cos(turn)
                if q not in (0, ROT // 2):
                    imag[q, cc, d, cc, STEP * b + d] = -scale * np.sin(turn)
    for cc in range(2):
        for d in range(2):
            pick[0, cc, d, cc, :] = 1.0
    shape = (PAY, BLOCK_COLS)
    return [t.reshape(shape).astype(np.float32) for t in (real, imag, pick)]


C1, C2 = math.cos(2 * math.pi / 9), math.cos(4 * math.pi / 9)
S1, S3, S4 = math.sin(2 * math.pi / 9), math.sin(6 * math.pi / 9), math.sin(8 * math.pi / 9)


def nine_cos(x0, s1, s2, s3, s4):
    u = s1 + s2 + s4
    v = x0 + s3
    base = x0 - 0.5 * s3
    a, b, c = s1 - s4, s2 - s4, s1 - s2
    p1 = C1 * a + C2 * b
    p2 = C2 * c - C1 * b
    return u + v, base + p1, base + p2, v - 0.5 * u, base - (p1 + p2)


def nine_sin(d1, d2, d3, d4):
    p, q, r = d1 + d2, d2 + d4, d1 - d4
    h = S3 * d3
    e1 = S1 * p + S4 * q
    e2 = S1 * r + S4 * p
    return e1 + h, e2 - h, S3 * (d1 - d2 + d4), (e2 - e1) + h


def nine_real(x):
    r = nine_cos(x[0], x[1] + x[8], x[2] + x[7], x[3] + x[6], x[4] + x[5])
    i = nine_sin(x[1] - x[8], x[2] - x[7], x[3] - x[6], x[4] - x[5])
    return r, (None,) + i


def crt(k1, k2):
    for k in range(ROT):
        if k % 4 == k1 and k % 9 == k2:
            return k
    return None


def forward36(x):
    re, im = [None] * FREQS, [None] * FREQS
    y0, y2, ya, yb = [], [], [], []
    for n2 in range(9):
        v = [x[(9 * n1 + 4 * n2) % ROT] for n1 in range(4)]
        t0, t1 = v[0] + v[2], v[1] + v[3]
        y0.append(t0 + t1)
        y2.append(t0 - t1)
        ya.append(v[0] - v[2])
        yb.append(v[3] - v[1])

    def put(k, real, imag):
        if k <= ROT // 2:
            re[k], im[k] = real, imag
        else:
            re[ROT - k], im[ROT - k] = real, -imag

    for k1, y in ((0, y0), (2, y2)):
        r, i = nine_real(y)
        k = crt(k1, 0)
        re[k] = r[0]
        for k2 in range(1, 5):
            k = crt(k1, k2)
            if k <= ROT // 2:
                re[k], im[k] = r[k2], -i[k2]
            else:
                re[ROT - k], im[ROT - k] = r[k2], i[k2]
    ra, ia = nine_real(ya)
    rb, ib = nine_real(yb)
    put(crt(1, 0), ra[0], rb[0])
    for k2 in range(1, 5):
        put(crt(1, k2), ra[k2] + ib[k2], rb[k2] - ia[k2])
        put(crt(1, 9 - k2), ra[k2] - ib[k2], rb[k2] + ia[k2])
    return re, im


def inverse36(re, im):
    def entry(k):
        if k <= ROT // 2:
            return re[k], im[k], 1
        return re[ROT - k], im[ROT - k], -1

    ys = []
    for k1 in (0, 2):
        real, imag = [entry(crt(k1, 0))[0]], [None]
        for k2 in range(1, 5):
            a, b, sign = entry(crt(k1, k2))
            real.append(a)
            imag.append(b if sign > 0 else -b)
        r = nine_cos(*real)
        i = (None,) + nine_sin(*imag[1:])
        y = [None] * 9
        y[0] = r[0]
        for n in range(1, 5):
            y[n], y[9 - n] = r[n] - i[n], r[n] + i[n]
        ys.append(y)
    xr, xi = [], []
    for k2 in range(9):
        a, b, sign = entry(crt(1, k2))
        xr.append(a)
        xi.append(b if sign > 0 else -b)
    rr, ir = nine_real(xr)
    ri, ii = nine_real(xi)
    ya, yb = [None] * 9, [None] * 9
    ya[0], yb[0] = rr[0], ri[0]
    for n in range(1, 5):
        ya[n], ya[9 - n] = rr[n] - ii[n], rr[n] + ii[n]
        yb[n], yb[9 - n] = ri[n] + ir[n], ri[n] - ir[n]
    x = [None] * ROT
    for n2 in range(9):
        t0, t1 = ys[0][n2] + ys[1][n2], ys[0][n2] - ys[1][n2]
        for n1, value in enumerate((t0 + ya[n2], t1 - yb[n2], t0 - ya[n2], t1 + yb[n2])):
            x[(9 * n1 + 4 * n2) % ROT] = value
    return x


def features_kernel(
    grp_ref, bin_ref, img_ref, sig_ref, ctf_ref, exp_ref, perm_ref, cos_ref, sin_ref,
    fh_ref, fl_ref, noise_ref, pix_ref, swp_ref,
):
    noise_ref[...] = jnp.dot(
        sig_ref[...], exp_ref[...], precision=lax.Precision.HIGHEST, preferred_element_type=F32
    )
    ctf = jnp.concatenate([ctf_ref[pl.ds(bin_ref[i], 1), :] for i in range(ROWS8)], axis=0)
    noise = jnp.concatenate([noise_ref[pl.ds(grp_ref[i], 1), :] for i in range(ROWS8)], axis=0)
    filt = ctf / noise
    weight = ctf * ctf / noise

    img = img_ref[...].astype(F32)
    stack = jnp.concatenate(
        [img[:, BLOCK_COLS * m : BLOCK_COLS * (m + 1)] for m in block_order()], axis=0
    ).astype(BF)
    turned = lax.dot_general(
        perm_ref[...], stack, (((1,), (1,)), ((), ())), preferred_element_type=F32
    )
    sub = lax.broadcasted_iota(jnp.int32, (ROWS8, LANES), 0)
    lane = lax.broadcasted_iota(jnp.int32, (ROWS8, LANES), 1)
    for b in range(ROT):
        y = turned[b * 8 : (b + 1) * 8]
        for t in (1, 2, 4):
            up = pltpu.roll(pltpu.roll(y, t, 0), LANES - t, 1)
            down = pltpu.roll(pltpu.roll(y, 8 - t, 0), t, 1)
            row_bit, lane_bit = (sub & t) != 0, (lane & t) != 0
            y = jnp.where(row_bit == lane_bit, y, jnp.where(row_bit, up, down))
        y = y * filt
        pix_ref[b] = y
        swp_ref[b] = jnp.where(
            (lane & 32) == 0, pltpu.roll(y, LANES - 32, 1), pltpu.roll(y, 32, 1)
        )

    off = lane & (STEP - 1)
    weight_hi = weight.astype(BF).astype(F32)
    slot = jnp.where(off == 0, weight, jnp.where(off == 1, weight - weight_hi, 0.0))
    slot = jnp.concatenate([slot, slot], axis=0)
    nothing = jnp.zeros_like(slot)

    def pair(sp, _):
        x = []
        for b in range(ROT):
            halves = []
            for h in range(2):
                c = cos_ref[2 * sp + h, b : b + 1, :]
                s = sin_ref[2 * sp + h, b : b + 1, :]
                halves.append(pix_ref[b] * c + swp_ref[b] * s)
            x.append(jnp.concatenate(halves, axis=0).astype(BF).astype(F32))
        re, im = forward36(x)
        im[0], im[ROT // 2] = slot, nothing
        rows = pl.ds(pl.multiple_of(sp * 16, 16), 16)
        for q in range(FREQS):
            for part, value in ((0, re[q]), (1, im[q])):
                hi = value.astype(BF)
                fh_ref[q, rows, part * LANES : (part + 1) * LANES] = hi
                fl_ref[q, rows, part * LANES : (part + 1) * LANES] = (
                    value - hi.astype(F32)
                ).astype(BF)
        return 0

    lax.fori_loop(0, S_PAD // 2, pair, 0)


def make_features(images, sigma2, ctf_group, defocus_bin):
    cos_t, sin_t = phase_lanes()
    vm = pl.BlockSpec(memory_space=pltpu.VMEM)
    sm = pl.BlockSpec(memory_space=pltpu.SMEM)
    shape = jax.ShapeDtypeStruct((FREQS, ROWS, 2 * LANES), BF)
    return pl.pallas_call(
        features_kernel,
        out_shape=(shape, shape),
        in_specs=[sm, sm] + [vm] * 7,
        out_specs=(vm, vm),
        scratch_shapes=[
            pltpu.VMEM((NGROUP, LANES), F32),
            pltpu.VMEM((ROT, ROWS8, LANES), F32),
            pltpu.VMEM((ROT, ROWS8, LANES), F32),
        ],
        compiler_params=pltpu.CompilerParams(vmem_limit_bytes=VMEM_LIMIT),
        name="features",
    )(
        ctf_group, defocus_bin, images, sigma2, ctf_lanes(), jnp.asarray(shell_expand()),
        jnp.asarray(pixel_perm(), BF), jnp.asarray(cos_t), jnp.asarray(sin_t),
    )


def nt(left, right):
    return lax.dot_general(left, right, (((1,), (1,)), ((), ())), preferred_element_type=F32)


def posterior_kernel(
    ref_ref, fh_ref, fl_ref, mth_ref, mtl_ref, pow_ref, out_ref, x_ref, d_ref, c_ref, p_ref, num_ref
):
    lane = lax.broadcasted_iota(jnp.int32, (CLASSES, LANES), 1)
    lane8 = lax.broadcasted_iota(jnp.int32, (8, LANES), 1)

    for m in range(BLOCKS):
        x_ref[m * KPAD : m * KPAD + CLASSES, :] = ref_ref[m]
        x_ref[m * KPAD + CLASSES : (m + 1) * KPAD, :] = jnp.zeros((KPAD - CLASSES, BLOCK_COLS), BF)
    x = x_ref[...]
    d_ref[...] = nt(mth_ref[...], x) + nt(mtl_ref[...], x)
    square = jnp.square(x.astype(F32))
    square_hi = square.astype(BF)
    square_lo = (square - square_hi.astype(F32)).astype(BF)
    d_ref[8:16, :] = nt(pow_ref[...], square_hi) + nt(pow_ref[...], square_lo)

    c_ref[:, :, COLS - LANES :] = jnp.zeros((2 * FREQS, CLASSES, LANES), F32)
    for q in range(FREQS):
        tile = jnp.concatenate(
            [
                d_ref[q * 16 + part * 8 : q * 16 + part * 8 + 8, t * LANES : (t + 1) * LANES]
                for part in range(2)
                for t in range(BLOCKS // 2)
            ],
            axis=0,
        )
        tile = tile.T
        even, odd = tile[:CLASSES], tile[KPAD : KPAD + CLASSES]
        real = jnp.where(lane < 64, even, pltpu.roll(odd, 64, 1))
        imag = jnp.where(lane < 64, pltpu.roll(even, 64, 1), odd)
        left = jnp.concatenate(
            [jnp.concatenate([real, imag], axis=1), jnp.concatenate([-imag, real], axis=1)], axis=0
        )
        hi = left.astype(BF)
        lo = (left - hi.astype(F32)).astype(BF)
        first = nt(jnp.concatenate([hi, lo], axis=0), fh_ref[q])
        second = nt(hi, fl_ref[q])
        total = first[: 2 * CLASSES] + first[2 * CLASSES :] + second
        c_ref[2 * q, :, :ROWS] = total[:CLASSES]
        c_ref[2 * q + 1, :, :ROWS] = total[CLASSES:]

    tiles_k = CLASSES // 8

    def where_of(i):
        col = pl.multiple_of((i // tiles_k) * LANES, LANES)
        row = pl.multiple_of((i % tiles_k) * 8, 8)
        return pl.ds(row, 8), pl.ds(col, LANES), col

    def to_scores(i, top):
        rows, cols, col = where_of(i)
        re = [c_ref[2 * q, rows, cols] for q in range(FREQS)]
        im = [None] + [c_ref[2 * q + 1, rows, cols] for q in range(1, FREQS - 1)] + [None]
        re[0] = jnp.where(lane8 + col < LIVE, re[0], -1e30)
        x = inverse36(re, im)
        for r in range(ROT):
            c_ref[r, rows, cols] = x[r]
        peak = x[0]
        for r in range(1, ROT):
            peak = jnp.maximum(peak, x[r])
        return jnp.maximum(top, peak)

    count = tiles_k * (COLS // LANES)
    top = lax.fori_loop(0, count, to_scores, jnp.full((8, LANES), -1e30, F32))

    def fold(v, op):
        for t in (4, 2, 1):
            v = op(v, pltpu.roll(v, t, 0))
        for t in (64, 32, 16, 8):
            v = op(v, pltpu.roll(v, t, 1))
        return v

    top = fold(top, jnp.maximum)

    def to_posterior(i, total):
        rows, cols, _ = where_of(i)
        x = [jnp.exp(c_ref[r, rows, cols] - top) for r in range(ROT)]
        re, im = forward36(x)
        for q in range(FREQS):
            c_ref[2 * q, rows, cols] = re[q]
            if im[q] is not None:
                c_ref[2 * q + 1, rows, cols] = im[q]
            else:
                c_ref[2 * q + 1, rows, cols] = jnp.zeros_like(re[q])
        return total + re[0]

    total = lax.fori_loop(0, count, to_posterior, jnp.zeros((8, LANES), F32))
    inverse = 1.0 / fold(total, jnp.add)
    scale = jnp.concatenate([inverse[:1]] * (COLS // LANES), axis=1)

    num_ref[FREQS] = jnp.zeros((LANES, LANES), F32)
    empty = jnp.zeros((KPAD - CLASSES, LANES), F32)
    for q in range(FREQS):
        p_ref[:CLASSES, :] = (c_ref[2 * q] * scale).astype(BF)
        p_ref[CLASSES:, :] = (c_ref[2 * q + 1] * scale).astype(BF)
        o = jnp.dot(p_ref[:, :ROWS], fh_ref[q], preferred_element_type=F32)
        real = o[:CLASSES, :LANES] + o[CLASSES:, LANES:]
        imag = o[:CLASSES, LANES:] - o[CLASSES:, :LANES]
        num_ref[q] = jnp.concatenate([real, empty, imag, empty], axis=0).T
    for pos, m in enumerate(block_order()):
        block = num_ref[:, pos * 8 : (pos + 1) * 8, :]
        out_ref[m] = block.reshape(PAY, LANES).astype(BF)


def make_payload(refs, feat_hi, feat_lo):
    mt = refs_transform()
    mt_hi = mt.astype(np.float32).astype(jnp.bfloat16)
    mt_lo = (mt - mt_hi.astype(np.float64)).astype(np.float32).astype(jnp.bfloat16)
    vm = pl.BlockSpec(memory_space=pltpu.VMEM)
    return pl.pallas_call(
        posterior_kernel,
        out_shape=jax.ShapeDtypeStruct((BLOCKS, PAY, LANES), BF),
        in_specs=[vm] * 6,
        out_specs=vm,
        scratch_shapes=[
            pltpu.VMEM((BLOCKS * KPAD, BLOCK_COLS), BF),
            pltpu.VMEM((FREQS * 16, BLOCKS * KPAD), F32),
            pltpu.VMEM((2 * FREQS, CLASSES, COLS), F32),
            pltpu.VMEM((2 * CLASSES, COLS), BF),
            pltpu.VMEM((FREQS + 1, LANES, LANES), F32),
        ],
        compiler_params=pltpu.CompilerParams(vmem_limit_bytes=VMEM_LIMIT),
        name="posterior",
    )(refs, feat_hi, feat_lo, jnp.asarray(mt_hi), jnp.asarray(mt_lo), jnp.asarray(power_rows(), BF))


def final_kernel(pay_ref, re_ref, im_ref, pick_ref, out_ref):
    total = jnp.sum(pay_ref[...].astype(F32), axis=0)
    turned = total.T
    real, imag = turned[:CLASSES], turned[KPAD : KPAD + CLASSES]
    dot = functools.partial(
        jnp.dot, precision=lax.Precision.HIGHEST, preferred_element_type=F32
    )
    numer = dot(real, re_ref[...]) + dot(imag, im_ref[...])
    out_ref[...] = numer / (dot(imag, pick_ref[...]) + 1.0)


def finish(pieces):
    re_t, im_t, pick = inverse_transform()
    vm = pl.BlockSpec(memory_space=pltpu.VMEM)
    return pl.pallas_call(
        final_kernel,
        out_shape=jax.ShapeDtypeStruct((CLASSES, BLOCK_COLS), F32),
        in_specs=[vm] * 4,
        out_specs=vm,
        compiler_params=pltpu.CompilerParams(vmem_limit_bytes=VMEM_LIMIT),
        name="finish",
    )(pieces, jnp.asarray(re_t), jnp.asarray(im_t), jnp.asarray(pick))


def on_device(images, class_refs, sigma2, ctf_group, defocus_bin):
    devices = lax.axis_size("img")
    share = class_refs.shape[1]
    me = lax.axis_index("img")
    direct = devices == BLOCKS and share == BLOCK_COLS
    if direct:
        own = jnp.broadcast_to(class_refs[None], (devices,) + class_refs.shape)
        refs = lax.all_to_all(own, "img", 0, 0)
    else:
        whole = lax.all_gather(class_refs, "img", axis=1, tiled=True)
        refs = whole.reshape(CLASSES, BLOCKS, BLOCK_COLS).transpose(1, 0, 2)
    pay = None
    for first in range(0, images.shape[0], ROWS8):
        part = slice(first, first + ROWS8)
        hi, lo = make_features(images[part], sigma2, ctf_group[part], defocus_bin[part])
        one = make_payload(refs, hi, lo)
        pay = one if pay is None else pay + one
    if direct:
        return finish(lax.all_to_all(pay, "img", 0, 0))
    summed = lax.psum(pay.astype(F32), "img")
    start = me * share
    block = lax.dynamic_index_in_dim(summed, start // BLOCK_COLS, 0, keepdims=True)
    return lax.dynamic_slice_in_dim(finish(block), start % BLOCK_COLS, share, 1)


def solution(mesh):
    in_specs = (
        P(("groups", "img"), None),
        P("groups", "img"),
        P("groups", None),
        P(("groups", "img")),
        P(("groups", "img")),
    )
    out_specs = P("groups", "img")
    return jax.shard_map(
        on_device, mesh=mesh, in_specs=in_specs, out_specs=out_specs, check_vma=False
    )
```

profile of v0, /device:TPU:0, one launch (start us, length us, event | category | flops | bytes accessed | tf_op | source)
XLA Modules:
  0.0 64.8 jit_solution(11959264624270126241)
XLA Ops:
  0.0 1.7 %broadcast_in_dim.4 = bf16[16,48,288]{2,1,0:T(8,128)(2,1)} broadcast(bf16[48,288]{1,0:T(8,128)(2,1)} %param.18), dimensions={1,2} | broadcast | bytes 470016 | tf_op jit(solution)/shard_map/broadcast_in_dim | solution.py:498
  1.7 7.4 %all-to-all-start = ((bf16[16,48,288]{2,1,0:T(8,128)(2,1)}), bf16[16,48,288]{2,1,0:T(8,128)(2,1)S(1)}, u32[]{:S(2)}, u32[]{:S(2)}) async-start(bf16[16,48,288]{2,1,0:T(8,128)(2,1)} %broadcast_in_dim.4), calls=%async_computation | async-start | bytes 1179648 | tf_op jit(solution)/shard_map/all_to_all | solution.py:499
  9.1 0.7 %pad_clamp_fusion = s32[1024]{0:T(1024)S(1)} fusion(s32[128]{0:T(128)} %constant.54), kind=kLoop, calls=%fused_computation.2 | loop fusion | flops 1024 | bytes 4608 | tf_op jit(solution)/shard_map/gather | solution.py:62
  9.8 0.1 sine_negate_fusion
  9.9 0.6 gather_fusion
  10.5 0.7 %copy.18 = f32[128,32]{0,1:T(8,128)} copy(f32[128,32]{1,0:T(8,128)S(1)} %gather_fusion) | data formatting | bytes 32768 | tf_op jit(solution)/shard_map/gather | solution.py:62
  11.2 9.7 %features.1 = (bf16[19,400,256]{2,1,0:T(8,128)(2,1)}, bf16[19,400,256]{2,1,0:T(8,128)(2,1)}) custom-call(s32[8]{0:T(128)} %grp_ref.1, s32[8]{0:T(128)} %bin_ref.1, bf16[8,4608]{1,0:T(8,128)(2,1)} %img_ref.1, f32[16,16]{1,0:T(8,128)} %sig_ref.1, f32[32,128]{1,0:T(8,128)} %bitcast.1, f32[16,128]{1,0:T(8,128)} %constant.40.clone.exp_ref, ...), custom_call_target="tpu_custom_call" | custom-call | tf_op jit(solution)/shard_map/features/pallas_call | solution.py:321
  21.0 3.7 %all-to-all-done.ref_ref = bf16[16,48,288]{2,1,0:T(8,128)(2,1)S(1)} async-done(((bf16[16,48,288]{2,1,0:T(8,128)(2,1)}), bf16[16,48,288]{2,1,0:T(8,128)(2,1)S(1)}, u32[]{:S(2)}, u32[]{:S(2)}) %all-to-all-start) | async-done | bytes 442400 | tf_op jit(solution)/shard_map/all_to_all | solution.py:499
  24.6 0.0 copy-start
  24.6 0.9 %copy-done = bf16[16,48,288]{2,1,0:T(8,128)(2,1)} copy-done((bf16[16,48,288]{2,1,0:T(8,128)(2,1)}, bf16[16,48,288]{2,1,0:T(8,128)(2,1)S(1)}, u32[]{:S(2)}) %copy-start) | copy-done | bytes 442392
  25.5 13.9 %posterior.1 = bf16[16,160,128]{2,1,0:T(8,128)(2,1)} custom-call(bf16[16,48,288]{2,1,0:T(8,128)(2,1)} %copy-done, bf16[19,400,256]{2,1,0:T(8,128)(2,1)} %get-tuple-element.7.fh_ref, bf16[19,400,256]{2,1,0:T(8,128)(2,1)} %get-tuple-element.8.fl_ref, bf16[304,288]{1,0:T(8,128)(2,1)} %constant.44.clone.mth_ref, bf16[304,288]{1,0:T(8,128)(2,1)} %constant.45.clone.mtl_ref, ...), custom_call_target="tpu_custom_call" | custom-call | tf_op jit(solution)/shard_map/posterior/pallas_call | solution.py:451
  39.4 22.8 %all_to_all.10.pay_ref = bf16[16,160,128]{2,1,0:T(8,128)(2,1)} all-to-all(bf16[16,160,128]{2,1,0:T(8,128)(2,1)} %posterior.1), channel_id=1, replica_groups=mesh['groups'=2,'img'=16] {'img'}, dimensions={0} | all-to-all | bytes 1310720 | tf_op jit(solution)/shard_map/all_to_all | solution.py:510
  62.1 2.7 %finish.1 = f32[48,288]{1,0:T(8,128)} custom-call(bf16[16,160,128]{2,1,0:T(8,128)(2,1)} %all_to_all.10.pay_ref, f32[160,288]{1,0:T(8,128)} %constant.47.clone.re_ref, f32[160,288]{1,0:T(8,128)} %constant.48.clone.im_ref, f32[160,288]{1,0:T(8,128)} %constant.49.clone.pick_ref), custom_call_target="tpu_custom_call" | custom-call | tf_op jit(solution)/shard_map/finish/pallas_call | solution.py:482
  (2 shorter events, 0.0 us)
Async XLA Ops:
  1.7 22.9 %all-to-all-start = ((bf16[16,48,288]{2,1,0:T(8,128)(2,1)}), bf16[16,48,288]{2,1,0:T(8,128)(2,1)S(1)}, u32[]{:S(2)}, u32[]{:S(2)}) async-start(bf16[16,48,288]{2,1,0:T(8,128)(2,1)} %broadcast_in_dim.4), calls=%async_computation | async-start | bytes 1179648 | tf_op jit(solution)/shard_map/all_to_all | solution.py:499
  24.6 0.9 %copy-start = (bf16[16,48,288]{2,1,0:T(8,128)(2,1)}, bf16[16,48,288]{2,1,0:T(8,128)(2,1)S(1)}, u32[]{:S(2)}) copy-start(bf16[16,48,288]{2,1,0:T(8,128)(2,1)S(1)} %all-to-all-done.ref_ref) | copy-start | bytes 1327108
where the time goes:
time: 65.3 us; the launch traced here: 64.8 us
  Pallas kernels  26.3 us (40%)
  blocking collectives  22.8 us (35%)
  starting transfers between devices  7.39 us (11%)
  local copies, waits for them, and re-layouts  3.86 us (6%)
  waiting for transfers between devices  3.67 us (6%)
  other arithmetic  0.8 us (1%)
    all_to_all x1, blocking collectives, on_device(): return finish(lax.all_to_all(pay, 'img', 0, 0))  22.8 us
    pallas_call x1, Pallas kernels, make_payload(): pl.pallas_call(posterior_kernel, out_shape=jax.ShapeDtypeStruct((BLOCKS,...  13.9 us
    pallas_call x1, Pallas kernels, make_features(): pl.pallas_call(features_kernel, out_shape=(shape, shape), in_specs=[sm, s...  9.74 us
    all_to_all x1, starting transfers between devices, on_device(): refs = lax.all_to_all(own, 'img', 0, 0)  7.39 us
    all_to_all x1, waiting for transfers between devices, on_device(): refs = lax.all_to_all(own, 'img', 0, 0)  3.67 us
    pallas_call x1, Pallas kernels, finish(): pl.pallas_call(final_kernel, out_shape=jax.ShapeDtypeStruct((CLASSES, BLO...  2.72 us
    broadcast_in_dim x1, local copies, waits for them, and re-layouts, on_device(): own = jnp.broadcast_to(class_refs[None], (devices,) + class_refs.shape)  1.68 us
    gather x2, local copies, waits for them, and re-layouts, ctf_lanes(): return table[:, chan % SHELLS]  1.33 us
  transfers between devices with their start and end apart: 1, of which 1 were waited for; matrix products, arithmetic and copies ran while one was open for 3% of the time, Pallas kernels for 15%

commit v1 on v0

--- a/solution.py
+++ b/solution.py
@@ -29,11 +29,16 @@
 ROWS = S_PAD * ROWS8
 LIVE = SHIFTS * ROWS8
 COLS = 512
+PAIRS_A = 16
+ROWS_A = 16 * PAIRS_A
+ROWS_B = ROWS - ROWS_A
 KPAD = 64
-PAY = (FREQS + 1) * ROWS8
+QUADS = (FREQS + 1) // 4
+TILES = 3 * QUADS
+PAY = TILES * ROWS8
 BF = jnp.bfloat16
 F32 = jnp.float32
-VMEM_LIMIT = 56 * 1024 * 1024
+MIB = 1024 * 1024
 
 
 def block_order():
@@ -56,10 +61,9 @@
 
 def ctf_lanes():
     chan, _ = lane_channel()
-    radius = (jnp.arange(SHELLS, dtype=F32) + 1.0) / (2.0 * SHELLS)
-    defocus = 1.0 + jnp.arange(BINS, dtype=F32) / BINS
-    table = -jnp.sin(80.0 * defocus[:, None] * radius[None, :] ** 2 + 0.1)
-    return table[:, chan % SHELLS]
+    defocus = 1.0 + np.arange(BINS, dtype=np.float64) / BINS
+    table = -np.sin(80.0 * defocus[:, None] * radius_of()[None, :] ** 2 + 0.1)
+    return table[:, chan % SHELLS].astype(np.float32)
 
 
 def shell_expand():
@@ -94,7 +98,7 @@
     sin_t = np.zeros((S_PAD, ROT, LANES), np.float32)
     cos_t[:SHIFTS] = np.cos(phase)
     sin_t[:SHIFTS] = np.sin(phase) * sign[None, None, :]
-    return cos_t, sin_t
+    return np.concatenate([cos_t, sin_t], axis=1)
 
 
 def refs_transform():
@@ -111,17 +115,9 @@
     return table.reshape(FREQS * 16, BLOCK_COLS)
 
 
-def power_rows():
-    table = np.zeros((2, STEP, 2, ANG), np.float32)
-    for cc in range(2):
-        table[cc, 0, cc, :] = -0.5
-    return table.reshape(8, BLOCK_COLS)
-
-
 def inverse_transform():
     real = np.zeros((FREQS + 1, 2, STEP, 2, ANG), np.float64)
     imag = np.zeros((FREQS + 1, 2, STEP, 2, ANG), np.float64)
-    pick = np.zeros((FREQS + 1, 2, STEP, 2, ANG), np.float64)
     b = np.arange(ROT)
     for q in range(FREQS):
         scale = (1.0 if q in (0, ROT // 2) else 2.0) / ROT
@@ -131,11 +127,14 @@
                 real[q, cc, d, cc, STEP * b + d] = scale * np.cos(turn)
                 if q not in (0, ROT // 2):
                     imag[q, cc, d, cc, STEP * b + d] = -scale * np.sin(turn)
-    for cc in range(2):
-        for d in range(2):
-            pick[0, cc, d, cc, :] = 1.0
-    shape = (PAY, BLOCK_COLS)
-    return [t.reshape(shape).astype(np.float32) for t in (real, imag, pick)]
+    shape = (QUADS, 4, ROWS8, BLOCK_COLS)
+    return [t.reshape(shape).transpose(1, 0, 2, 3).reshape(4 * QUADS * ROWS8, BLOCK_COLS) for t in (real, imag)]
+
+
+def split(table):
+    hi = table.astype(np.float32).astype(jnp.bfloat16)
+    lo = (table - hi.astype(np.float64)).astype(np.float32).astype(jnp.bfloat16)
+    return hi, lo
 
 
 C1, C2 = math.cos(2 * math.pi / 9), math.cos(4 * math.pi / 9)
@@ -249,10 +248,50 @@
     return x
 
 
-def features_kernel(
-    grp_ref, bin_ref, img_ref, sig_ref, ctf_ref, exp_ref, perm_ref, cos_ref, sin_ref,
-    fh_ref, fl_ref, noise_ref, pix_ref, swp_ref,
+def transform_pairs(table_ref, pix_ref, slot_ref, fh_ref, fl_ref, count):
+    slot = jnp.concatenate([slot_ref[...]] * 2, axis=0)
+    nothing = jnp.zeros_like(slot)
+
+    def pair(sp, _):
+        x = []
+        for b in range(ROT):
+            halves = []
+            for h in range(2):
+                c = table_ref[2 * sp + h, b : b + 1, :]
+                s = table_ref[2 * sp + h, ROT + b : ROT + b + 1, :]
+                halves.append(pix_ref[0, b] * c + pix_ref[1, b] * s)
+            x.append(jnp.concatenate(halves, axis=0).astype(BF).astype(F32))
+        re, im = forward36(x)
+        im[0], im[ROT // 2] = slot, nothing
+        rows = pl.ds(pl.multiple_of(sp * 16, 16), 16)
+        for q in range(FREQS):
+            for part, value in ((0, re[q]), (1, im[q])):
+                hi = value.astype(BF)
+                fh_ref[q, rows, part * LANES : (part + 1) * LANES] = hi
+                fl_ref[q, rows, part * LANES : (part + 1) * LANES] = (
+                    value - hi.astype(F32)
+                ).astype(BF)
+        return 0
+
+    lax.fori_loop(0, count, pair, 0)
+
+
+def first_kernel(
+    grp_hbm, bin_hbm, img_hbm, sig_hbm, ctf_hbm, exp_hbm, perm_hbm, table_hbm,
+    fh_ref, fl_ref, pix_ref, slot_ref, rest_ref,
+    grp_ref, bin_ref, img_ref, sig_ref, ctf_ref, exp_ref, perm_ref, table_ref, noise_ref, sems,
 ):
+    moves = [
+        (grp_hbm, grp_ref), (bin_hbm, bin_ref), (img_hbm, img_ref), (sig_hbm, sig_ref),
+        (ctf_hbm, ctf_ref), (exp_hbm, exp_ref), (perm_hbm, perm_ref),
+        (table_hbm.at[pl.ds(0, 2 * PAIRS_A)], table_ref),
+        (table_hbm.at[pl.ds(2 * PAIRS_A, S_PAD - 2 * PAIRS_A)], rest_ref),
+    ]
+    copies = [pltpu.make_async_copy(a, b, sems.at[i]) for i, (a, b) in enumerate(moves)]
+    for copy in copies:
+        copy.start()
+    for copy in copies[:7]:
+        copy.wait()
     noise_ref[...] = jnp.dot(
         sig_ref[...], exp_ref[...], precision=lax.Precision.HIGHEST, preferred_element_type=F32
     )
@@ -278,62 +317,99 @@
             row_bit, lane_bit = (sub & t) != 0, (lane & t) != 0
             y = jnp.where(row_bit == lane_bit, y, jnp.where(row_bit, up, down))
         y = y * filt
-        pix_ref[b] = y
-        swp_ref[b] = jnp.where(
+        pix_ref[0, b] = y
+        pix_ref[1, b] = jnp.where(
             (lane & 32) == 0, pltpu.roll(y, LANES - 32, 1), pltpu.roll(y, 32, 1)
         )
 
     off = lane & (STEP - 1)
     weight_hi = weight.astype(BF).astype(F32)
-    slot = jnp.where(off == 0, weight, jnp.where(off == 1, weight - weight_hi, 0.0))
-    slot = jnp.concatenate([slot, slot], axis=0)
-    nothing = jnp.zeros_like(slot)
-
-    def pair(sp, _):
-        x = []
-        for b in range(ROT):
-            halves = []
-            for h in range(2):
-                c = cos_ref[2 * sp + h, b : b + 1, :]
-                s = sin_ref[2 * sp + h, b : b + 1, :]
-                halves.append(pix_ref[b] * c + swp_ref[b] * s)
-            x.append(jnp.concatenate(halves, axis=0).astype(BF).astype(F32))
-        re, im = forward36(x)
-        im[0], im[ROT // 2] = slot, nothing
-        rows = pl.ds(pl.multiple_of(sp * 16, 16), 16)
-        for q in range(FREQS):
-            for part, value in ((0, re[q]), (1, im[q])):
-                hi = value.astype(BF)
-                fh_ref[q, rows, part * LANES : (part + 1) * LANES] = hi
-                fl_ref[q, rows, part * LANES : (part + 1) * LANES] = (
-                    value - hi.astype(F32)
-                ).astype(BF)
-        return 0
-
-    lax.fori_loop(0, S_PAD // 2, pair, 0)
-
-
-def make_features(images, sigma2, ctf_group, defocus_bin):
-    cos_t, sin_t = phase_lanes()
-    vm = pl.BlockSpec(memory_space=pltpu.VMEM)
-    sm = pl.BlockSpec(memory_space=pltpu.SMEM)
-    shape = jax.ShapeDtypeStruct((FREQS, ROWS, 2 * LANES), BF)
+    slot_ref[...] = jnp.where(off == 0, weight, jnp.where(off == 1, weight - weight_hi, 0.0))
+    copies[7].wait()
+    transform_pairs(table_ref, pix_ref, slot_ref, fh_ref, fl_ref, PAIRS_A)
+    copies[8].wait()
+
+
+def second_kernel(
+    table_ref, pix_ref, slot_ref, mt_hbm, back_hbm, fh_ref, fl_ref, mt_ref, back_ref, sems
+):
+    copies = [
+        pltpu.make_async_copy(mt_hbm, mt_ref, sems.at[0]),
+        pltpu.make_async_copy(back_hbm, back_ref, sems.at[1]),
+    ]
+    for copy in copies:
+        copy.start()
+    transform_pairs(table_ref, pix_ref, slot_ref, fh_ref, fl_ref, S_PAD // 2 - PAIRS_A)
+    for copy in copies:
+        copy.wait()
+
+
+VM = pl.BlockSpec(memory_space=pltpu.VMEM)
+HB = pl.BlockSpec(memory_space=pltpu.HBM)
+
+
+def in_hbm(*arrays):
+    return [pltpu.with_memory_space_constraint(a, pltpu.HBM) for a in arrays]
+
+
+def cost(micros):
+    return pl.CostEstimate(flops=int(micros * 1e9), bytes_accessed=int(micros * 3e6), transcendentals=0)
+
+
+def first_features(images, sigma2, ctf_group, defocus_bin):
+    feat = jax.ShapeDtypeStruct((FREQS, ROWS_A, 2 * LANES), BF)
+    tail = S_PAD - 2 * PAIRS_A
     return pl.pallas_call(
-        features_kernel,
-        out_shape=(shape, shape),
-        in_specs=[sm, sm] + [vm] * 7,
-        out_specs=(vm, vm),
+        first_kernel,
+        out_shape=(
+            feat,
+            feat,
+            jax.ShapeDtypeStruct((2, ROT, ROWS8, LANES), F32),
+            jax.ShapeDtypeStruct((ROWS8, LANES), F32),
+            jax.ShapeDtypeStruct((tail, 2 * ROT, LANES), F32),
+        ),
+        in_specs=[HB] * 8,
+        out_specs=[VM] * 5,
         scratch_shapes=[
+            pltpu.SMEM((ROWS8,), jnp.int32),
+            pltpu.SMEM((ROWS8,), jnp.int32),
+            pltpu.VMEM(images.shape, BF),
+            pltpu.VMEM(sigma2.shape, F32),
+            pltpu.VMEM((BINS, LANES), F32),
             pltpu.VMEM((NGROUP, LANES), F32),
-            pltpu.VMEM((ROT, ROWS8, LANES), F32),
-            pltpu.VMEM((ROT, ROWS8, LANES), F32),
+            pltpu.VMEM((BLOCK_COLS, BLOCK_COLS), BF),
+            pltpu.VMEM((2 * PAIRS_A, 2 * ROT, LANES), F32),
+            pltpu.VMEM((NGROUP, LANES), F32),
+            pltpu.SemaphoreType.DMA((9,)),
         ],
-        compiler_params=pltpu.CompilerParams(vmem_limit_bytes=VMEM_LIMIT),
-        name="features",
-    )(
-        ctf_group, defocus_bin, images, sigma2, ctf_lanes(), jnp.asarray(shell_expand()),
-        jnp.asarray(pixel_perm(), BF), jnp.asarray(cos_t), jnp.asarray(sin_t),
-    )
+        compiler_params=pltpu.CompilerParams(vmem_limit_bytes=20 * MIB),
+        cost_estimate=cost(4.5),
+        name="features_first",
+    )(*in_hbm(
+        ctf_group, defocus_bin, images, sigma2, jnp.asarray(ctf_lanes()),
+        jnp.asarray(shell_expand()), jnp.asarray(pixel_perm(), BF), jnp.asarray(phase_lanes()),
+    ))
+
+
+def second_features(table, pix, slot):
+    feat = jax.ShapeDtypeStruct((FREQS, ROWS_B, 2 * LANES), BF)
+    mt = np.stack(split(refs_transform()))
+    back = np.stack([half for part in inverse_transform() for half in split(part)])
+    return pl.pallas_call(
+        second_kernel,
+        out_shape=(
+            feat,
+            feat,
+            jax.ShapeDtypeStruct(mt.shape, BF),
+            jax.ShapeDtypeStruct(back.shape, BF),
+        ),
+        in_specs=[VM] * 3 + [HB] * 2,
+        out_specs=[VM] * 4,
+        scratch_shapes=[pltpu.SemaphoreType.DMA((2,))],
+        compiler_params=pltpu.CompilerParams(vmem_limit_bytes=16 * MIB),
+        cost_estimate=cost(2.5),
+        name="features_second",
+    )(table, pix, slot, *in_hbm(jnp.asarray(mt), jnp.asarray(back)))
 
 
 def nt(left, right):
@@ -341,20 +417,27 @@
 
 
 def posterior_kernel(
-    ref_ref, fh_ref, fl_ref, mth_ref, mtl_ref, pow_ref, out_ref, x_ref, d_ref, c_ref, p_ref, num_ref
+    direct, r0_ref, r1_ref, r2_ref, r3_ref, fha_ref, fla_ref, fhb_ref, flb_ref, mt_ref,
+    out_ref, x_ref, d_ref, c_ref, p_ref, num_ref,
 ):
     lane = lax.broadcasted_iota(jnp.int32, (CLASSES, LANES), 1)
     lane8 = lax.broadcasted_iota(jnp.int32, (8, LANES), 1)
 
-    for m in range(BLOCKS):
-        x_ref[m * KPAD : m * KPAD + CLASSES, :] = ref_ref[m]
-        x_ref[m * KPAD + CLASSES : (m + 1) * KPAD, :] = jnp.zeros((KPAD - CLASSES, BLOCK_COLS), BF)
+    me = lax.axis_index("img") if direct else 0
+    blank = jnp.zeros((KPAD - CLASSES, BLOCK_COLS), BF)
+    for group, ref in enumerate((r0_ref, r1_ref, r2_ref, r3_ref)):
+        for f in range(BLOCKS // 4):
+            row = pl.multiple_of((me ^ (4 * f + group)) * KPAD, KPAD)
+            x_ref[pl.ds(row, KPAD), :] = jnp.concatenate([ref[f], blank], axis=0)
     x = x_ref[...]
-    d_ref[...] = nt(mth_ref[...], x) + nt(mtl_ref[...], x)
+    d_ref[...] = nt(mt_ref[0], x) + nt(mt_ref[1], x)
     square = jnp.square(x.astype(F32))
     square_hi = square.astype(BF)
     square_lo = (square - square_hi.astype(F32)).astype(BF)
-    d_ref[8:16, :] = nt(pow_ref[...], square_hi) + nt(pow_ref[...], square_lo)
+    e = lax.broadcasted_iota(jnp.int32, (8, BLOCK_COLS), 0)
+    col = lax.broadcasted_iota(jnp.int32, (8, BLOCK_COLS), 1)
+    power = jnp.where(e == jnp.where(col < ANG, 0, STEP), -0.5, 0.0).astype(BF)
+    d_ref[8:16, :] = nt(power, square_hi) + nt(power, square_lo)
 
     c_ref[:, :, COLS - LANES :] = jnp.zeros((2 * FREQS, CLASSES, LANES), F32)
     for q in range(FREQS):
@@ -375,11 +458,12 @@
         )
         hi = left.astype(BF)
         lo = (left - hi.astype(F32)).astype(BF)
-        first = nt(jnp.concatenate([hi, lo], axis=0), fh_ref[q])
-        second = nt(hi, fl_ref[q])
-        total = first[: 2 * CLASSES] + first[2 * CLASSES :] + second
-        c_ref[2 * q, :, :ROWS] = total[:CLASSES]
-        c_ref[2 * q + 1, :, :ROWS] = total[CLASSES:]
+        both = jnp.concatenate([hi, lo], axis=0)
+        for fh, fl, span in ((fha_ref, fla_ref, slice(0, ROWS_A)), (fhb_ref, flb_ref, slice(ROWS_A, ROWS))):
+            first = nt(both, fh[q])
+            total = first[: 2 * CLASSES] + first[2 * CLASSES :] + nt(hi, fl[q])
+            c_ref[2 * q, :, span] = total[:CLASSES]
+            c_ref[2 * q + 1, :, span] = total[CLASSES:]
 
     tiles_k = CLASSES // 8
 
@@ -429,64 +513,101 @@
     inverse = 1.0 / fold(total, jnp.add)
     scale = jnp.concatenate([inverse[:1]] * (COLS // LANES), axis=1)
 
-    num_ref[FREQS] = jnp.zeros((LANES, LANES), F32)
-    empty = jnp.zeros((KPAD - CLASSES, LANES), F32)
-    for q in range(FREQS):
+    def product(q):
         p_ref[:CLASSES, :] = (c_ref[2 * q] * scale).astype(BF)
         p_ref[CLASSES:, :] = (c_ref[2 * q + 1] * scale).astype(BF)
-        o = jnp.dot(p_ref[:, :ROWS], fh_ref[q], preferred_element_type=F32)
+        o = jnp.dot(p_ref[:, :ROWS_A], fha_ref[q], preferred_element_type=F32)
+        o += jnp.dot(p_ref[:, ROWS_A:ROWS], fhb_ref[q], preferred_element_type=F32)
         real = o[:CLASSES, :LANES] + o[CLASSES:, LANES:]
         imag = o[:CLASSES, LANES:] - o[CLASSES:, :LANES]
-        num_ref[q] = jnp.concatenate([real, empty, imag, empty], axis=0).T
-    for pos, m in enumerate(block_order()):
-        block = num_ref[:, pos * 8 : (pos + 1) * 8, :]
-        out_ref[m] = block.reshape(PAY, LANES).astype(BF)
-
-
-def make_payload(refs, feat_hi, feat_lo):
-    mt = refs_transform()
-    mt_hi = mt.astype(np.float32).astype(jnp.bfloat16)
-    mt_lo = (mt - mt_hi.astype(np.float64)).astype(np.float32).astype(jnp.bfloat16)
-    vm = pl.BlockSpec(memory_space=pltpu.VMEM)
+        return jnp.concatenate([real, imag], axis=0)
+
+    third = 2 * CLASSES // 3
+    for quad in range(QUADS):
+        if 4 * quad + 3 < FREQS:
+            extra = product(4 * quad + 3)
+        else:
+            extra = jnp.zeros((2 * CLASSES, LANES), F32)
+        for slot in range(3):
+            tile = [product(4 * quad + slot), extra[slot * third : (slot + 1) * third]]
+            num_ref[slot * QUADS + quad] = jnp.concatenate(tile, axis=0).T
+    core, chip = me % 2, me // 2
+    for half in range(2):
+        side = (1 - core) if half == 0 else core
+        for e in range(BLOCKS // 2):
+            row = pl.multiple_of(side * (LANES // 2) + (chip ^ e) * ROWS8, ROWS8)
+            out_ref[half, e] = num_ref[:, pl.ds(row, 8), :].reshape(PAY, LANES).astype(BF)
+
+
+def make_payload(direct, refs, feat_a, feat_b, mt):
     return pl.pallas_call(
-        posterior_kernel,
-        out_shape=jax.ShapeDtypeStruct((BLOCKS, PAY, LANES), BF),
-        in_specs=[vm] * 6,
-        out_specs=vm,
+        functools.partial(posterior_kernel, direct),
+        out_shape=jax.ShapeDtypeStruct((2, BLOCKS // 2, PAY, LANES), BF),
+        in_specs=[VM] * 9,
+        out_specs=VM,
         scratch_shapes=[
             pltpu.VMEM((BLOCKS * KPAD, BLOCK_COLS), BF),
             pltpu.VMEM((FREQS * 16, BLOCKS * KPAD), F32),
             pltpu.VMEM((2 * FREQS, CLASSES, COLS), F32),
             pltpu.VMEM((2 * CLASSES, COLS), BF),
-            pltpu.VMEM((FREQS + 1, LANES, LANES), F32),
+            pltpu.VMEM((TILES, LANES, LANES), F32),
         ],
-        compiler_params=pltpu.CompilerParams(vmem_limit_bytes=VMEM_LIMIT),
+        compiler_params=pltpu.CompilerParams(vmem_limit_bytes=24 * MIB),
+        cost_estimate=cost(10.0),
         name="posterior",
-    )(refs, feat_hi, feat_lo, jnp.asarray(mt_hi), jnp.asarray(mt_lo), jnp.asarray(power_rows(), BF))
-
-
-def final_kernel(pay_ref, re_ref, im_ref, pick_ref, out_ref):
-    total = jnp.sum(pay_ref[...].astype(F32), axis=0)
+    )(*refs, *feat_a, *feat_b, mt)
+
+
+def final_kernel(keep_ref, got_ref, back_ref, out_ref):
+    total = keep_ref[...] + got_ref[...].astype(F32)
     turned = total.T
-    real, imag = turned[:CLASSES], turned[KPAD : KPAD + CLASSES]
-    dot = functools.partial(
-        jnp.dot, precision=lax.Precision.HIGHEST, preferred_element_type=F32
+    width = QUADS * ROWS8
+    third = 2 * CLASSES // 3
+    last = jnp.concatenate(
+        [turned[2 * CLASSES :, slot * width : (slot + 1) * width] for slot in range(3)], axis=0
     )
-    numer = dot(real, re_ref[...]) + dot(imag, im_ref[...])
-    out_ref[...] = numer / (dot(imag, pick_ref[...]) + 1.0)
-
-
-def finish(pieces):
-    re_t, im_t, pick = inverse_transform()
-    vm = pl.BlockSpec(memory_space=pltpu.VMEM)
+    numer = jnp.zeros((CLASSES, BLOCK_COLS), F32)
+    for part in range(2):
+        rows = slice(part * CLASSES, (part + 1) * CLASSES)
+        for value, first in ((turned[rows], 0), (last[rows], 3 * width)):
+            span = slice(first, first + value.shape[1])
+            hi = value.astype(BF)
+            lo = (value - hi.astype(F32)).astype(BF)
+            dot = functools.partial(jnp.dot, preferred_element_type=F32)
+            table_hi, table_lo = back_ref[2 * part, span], back_ref[2 * part + 1, span]
+            numer += dot(hi, table_hi) + dot(lo, table_hi) + dot(hi, table_lo)
+    weights = turned[CLASSES : 2 * CLASSES]
+    column = lax.broadcasted_iota(jnp.int32, (CLASSES, BLOCK_COLS), 1)
+    first = weights[:, 0:1] + weights[:, 1:2]
+    second = weights[:, STEP : STEP + 1] + weights[:, STEP + 1 : STEP + 2]
+    out_ref[...] = numer / (jnp.where(column < ANG, first, second) + 1.0)
+
+
+def finish(keep, got, back):
     return pl.pallas_call(
         final_kernel,
         out_shape=jax.ShapeDtypeStruct((CLASSES, BLOCK_COLS), F32),
-        in_specs=[vm] * 4,
-        out_specs=vm,
-        compiler_params=pltpu.CompilerParams(vmem_limit_bytes=VMEM_LIMIT),
+        in_specs=[VM] * 3,
+        out_specs=VM,
+        compiler_params=pltpu.CompilerParams(vmem_limit_bytes=8 * MIB),
+        cost_estimate=cost(1.0),
         name="finish",
-    )(pieces, jnp.asarray(re_t), jnp.asarray(im_t), jnp.asarray(pick))
+    )(keep, got, back)
+
+
+def swap(value, distance):
+    pairs = [(i, i ^ distance) for i in range(lax.axis_size("img"))]
+    return lax.ppermute(value, "img", pairs)
+
+
+def reduce_direct(pay):
+    pairs = pay[1].astype(F32) + swap(pay[0], 1).astype(F32)
+    pairs = pairs.reshape((BLOCKS // 4, 2) + pairs.shape[1:])
+    parts = [swap(pairs[f].astype(BF), 4 * f) for f in range(1, BLOCKS // 4)]
+    total = pairs[0]
+    for part in parts:
+        total = total + part.astype(F32)
+    return total[0], swap(total[1].astype(BF), 2)
 
 
 def on_device(images, class_refs, sigma2, ctf_group, defocus_bin):
@@ -495,23 +616,36 @@
     me = lax.axis_index("img")
     direct = devices == BLOCKS and share == BLOCK_COLS
     if direct:
-        own = jnp.broadcast_to(class_refs[None], (devices,) + class_refs.shape)
-        refs = lax.all_to_all(own, "img", 0, 0)
+        line = [swap(class_refs, 4 * f) for f in range(1, BLOCKS // 4)]
     else:
         whole = lax.all_gather(class_refs, "img", axis=1, tiled=True)
-        refs = whole.reshape(CLASSES, BLOCKS, BLOCK_COLS).transpose(1, 0, 2)
+        blocks = whole.reshape(CLASSES, BLOCKS // 4, 4, BLOCK_COLS).transpose(2, 1, 0, 3)
+        refs = [blocks[g] for g in range(4)]
     pay = None
     for first in range(0, images.shape[0], ROWS8):
         part = slice(first, first + ROWS8)
-        hi, lo = make_features(images[part], sigma2, ctf_group[part], defocus_bin[part])
-        one = make_payload(refs, hi, lo)
+        fha, fla, pix, slot, rest = first_features(
+            images[part], sigma2, ctf_group[part], defocus_bin[part]
+        )
+        if direct and first == 0:
+            line, fha = lax.optimization_barrier((line, fha))
+            line = jnp.stack([class_refs] + line)
+            across = swap(line, 2)
+        fhb, flb, mt, back = second_features(rest, pix, slot)
+        if direct and first == 0:
+            across, fhb = lax.optimization_barrier((across, fhb))
+            refs = [line, swap(line, 1), across, swap(across, 1)]
+        one = make_payload(direct, refs, (fha, fla), (fhb, flb), mt)
         pay = one if pay is None else pay + one
     if direct:
-        return finish(lax.all_to_all(pay, "img", 0, 0))
+        return finish(*reduce_direct(pay), back)
     summed = lax.psum(pay.astype(F32), "img")
     start = me * share
-    block = lax.dynamic_index_in_dim(summed, start // BLOCK_COLS, 0, keepdims=True)
-    return lax.dynamic_slice_in_dim(finish(block), start % BLOCK_COLS, share, 1)
+    block = start // BLOCK_COLS
+    mine = summed[1 - block % 2, block // 2]
+    return lax.dynamic_slice_in_dim(
+        finish(mine, jnp.zeros_like(mine, BF), back), start % BLOCK_COLS, share, 1
+    )
 
 
 def solution(mesh):

time: 65.3 us -> 44.2 us (0.68)
  blocking collectives: 22.8 us -> 0 us
  waiting for transfers between devices: 3.67 us -> 13.1 us
  Pallas kernels: 26.3 us -> 17.2 us
  starting transfers between devices: 7.39 us -> 13.5 us
  local copies, waits for them, and re-layouts: 3.86 us -> 0.05 us
  other arithmetic: 0.8 us -> 0.14 us
    all_to_all x1 -> x0, blocking collectives: 22.8 us -> none  [on_device(): return finish(lax.all_to_all(pay, 'img', 0, 0))]
    ppermute x0 -> x11, starting transfers between devices: none -> 13.5 us  [swap(): return lax.ppermute(value, 'img', pairs)]
    ppermute x0 -> x11, waiting for transfers between devices: none -> 13.1 us  [swap(): return lax.ppermute(value, 'img', pairs)]
    pallas_call x2 -> x3, Pallas kernels: 23.6 us -> 16.1 us  [the longest x1 9.79 us: make_payload(): pl.pallas_call(functools.partial(posterior_kernel, direct), out_shape=jax...]
    all_to_all x1 -> x0, starting transfers between devices: 7.39 us -> none  [on_device(): refs = lax.all_to_all(own, 'img', 0, 0)]
    all_to_all x1 -> x0, waiting for transfers between devices: 3.67 us -> none  [on_device(): refs = lax.all_to_all(own, 'img', 0, 0)]
    broadcast_in_dim x1 -> x0, local copies, waits for them, and re-layouts: 1.68 us -> none  [on_device(): own = jnp.broadcast_to(class_refs[None], (devices,) + class_refs.shape)]
    pallas_call x1, Pallas kernels: 2.72 us -> 1.08 us  [finish(): pl.pallas_call(final_kernel, out_shape=jax.ShapeDtypeStruct((CLASSES, BLO...]
  transfers between devices with their start and end apart: 1 -> 11, of which waited for: 1 -> 8; matrix products, arithmetic and copies ran while one was open for 3% -> 0% of each run, Pallas kernels for 15% -> 14%
where the time goes in v1:
time: 44.2 us; the launch traced here: 44.1 us
  Pallas kernels  17.2 us (39%)
  starting transfers between devices  13.5 us (31%)
  waiting for transfers between devices  13.1 us (30%)
    ppermute x11, starting transfers between devices, swap(): return lax.ppermute(value, 'img', pairs)  13.5 us
    ppermute x11, waiting for transfers between devices, swap(): return lax.ppermute(value, 'img', pairs)  13.1 us
    pallas_call x1, Pallas kernels, make_payload(): pl.pallas_call(functools.partial(posterior_kernel, direct), out_shape=jax...  9.79 us
    pallas_call x1, Pallas kernels, first_features(): pl.pallas_call(first_kernel, out_shape=(feat, feat, jax.ShapeDtypeStruct(...  4.63 us
    pallas_call x1, Pallas kernels, second_features(): pl.pallas_call(second_kernel, out_shape=(feat, feat, jax.ShapeDtypeStruct...  1.65 us
    pallas_call x1, Pallas kernels, finish(): pl.pallas_call(final_kernel, out_shape=jax.ShapeDtypeStruct((CLASSES, BLO...  1.08 us
  transfers between devices with their start and end apart: 11, of which 8 were waited for; matrix products, arithmetic and copies ran while one was open for 0% of the time, Pallas kernels for 14%

profile of v1, /device:TPU:0, one launch (start us, length us, event | category | flops | bytes accessed | tf_op | source)
XLA Modules:
  0.0 44.1 jit_solution(15625965721715099697)
XLA Ops:
  0.0 0.0 copy-start
  0.0 3.0 %collective-permute-start = (bf16[48,288]{1,0:T(8,128)(2,1)}, bf16[48,288]{1,0:T(8,128)(2,1)S(1)}, u32[]{:S(2)}, u32[]{:S(2)}) collective-permute-start(bf16[48,288]{1,0:T(8,128)(2,1)} %param.12), channel_id=1, source_target_pairs={{0,4},{1,5},{2,6},{3,7},{4,0},{5,1},{6,2},{7,3},{8,12},{9,13},{10,... | collective-permute-start | bytes 82952 | tf_op jit(solution)/shard_map/ppermute | solution.py:600
  3.0 2.6 %collective-permute-start.1 = (bf16[48,288]{1,0:T(8,128)(2,1)}, bf16[48,288]{1,0:T(8,128)(2,1)S(1)}, u32[]{:S(2)}, u32[]{:S(2)}) collective-permute-start(bf16[48,288]{1,0:T(8,128)(2,1)} %param.12), channel_id=1, source_target_pairs={{0,8},{1,9},{2,10},{3,11},{4,12},{5,13},{6,14},{7,15},{8,0},{9,1},... | collective-permute-start | bytes 82952 | tf_op jit(solution)/shard_map/ppermute | solution.py:600
  5.6 0.0 collective-permute-start.2
  5.6 4.6 %features_first.1 = (bf16[19,256,256]{2,1,0:T(8,128)(2,1)S(1)}, bf16[19,256,256]{2,1,0:T(8,128)(2,1)S(1)}, f32[2,36,8,128]{3,2,1,0:T(8,128)S(1)}, f32[8,128]{1,0:T(8,128)S(1)}, f32[18,72,128]{2,1,0:T(8,128)S(1)}) custom-call(s32[8]{0:T(128)} %grp_hbm.1, s32[8]{0:T(128)} %bin_hbm.1, bf16[8,4608]{1,0:T(8,128)(2,1)} %img_hbm.1, f32[16,16]{1,0:T(8,128)} %sig_hbm.1, ...), custom_call_target="tpu_custom_call" | custom-call | flops 4499999744 | bytes 13500000 | tf_op jit(solution)/shard_map/features_first/pallas_call | solution.py:362
  10.3 0.0 collective-permute-done
  10.3 0.0 collective-permute-done.1
  10.3 1.3 %collective-permute-done.2 = bf16[48,288]{1,0:T(8,128)(2,1)S(1)} collective-permute-done((bf16[48,288]{1,0:T(8,128)(2,1)}, bf16[48,288]{1,0:T(8,128)(2,1)S(1)}, u32[]{:S(2)}, u32[]{:S(2)}) %collective-permute-start.2) | collective-permute-done | bytes 27680 | tf_op jit(solution)/shard_map/ppermute | solution.py:600
  11.6 0.0 copy-done
  11.6 1.6 %collective-permute-start.4 = (bf16[4,48,288]{2,1,0:T(8,128)(2,1)S(1)}, bf16[4,48,288]{2,1,0:T(8,128)(2,1)S(1)}, u32[]{:S(2)}, u32[]{:S(2)}) collective-permute-start(bf16[4,48,288]{2,1,0:T(8,128)(2,1)S(1)} %pad_maximum_fusion.r0_ref), channel_id=1, source_target_pairs={{0,2},{1,3},{2,0},{3,1},{4,6},{5,7},{6,4},{7,5},{8,10},{9,11},{10,... | collective-permute-start | bytes 331784 | tf_op jit(solution)/shard_map/ppermute | solution.py:600
  13.2 1.6 %features_second.1 = (bf16[19,144,256]{2,1,0:T(8,128)(2,1)S(1)}, bf16[19,144,256]{2,1,0:T(8,128)(2,1)S(1)}, bf16[2,304,288]{2,1,0:T(8,128)(2,1)S(1)}, bf16[4,160,288]{2,1,0:T(8,128)(2,1)S(1)}) custom-call(f32[18,72,128]{2,1,0:T(8,128)S(1)} %get-tuple-element.24.table_ref, f32[2,36,8,128]{3,2,1,0:T(8,128)S(1)} %get-tuple-element.25.pix_ref, ...), custom_call_target="tpu_custom_call" | custom-call | flops 2500000000 | bytes 7500000 | tf_op jit(solution)/shard_map/features_second/pallas_call | solution.py:398
  14.9 0.1 collective-permute-start.3
  15.0 1.9 %collective-permute-done.4.r2_ref = bf16[4,48,288]{2,1,0:T(8,128)(2,1)S(1)} collective-permute-done((bf16[4,48,288]{2,1,0:T(8,128)(2,1)S(1)}, bf16[4,48,288]{2,1,0:T(8,128)(2,1)S(1)}, u32[]{:S(2)}, u32[]{:S(2)}) %collective-permute-start.4) | collective-permute-done | bytes 110624 | tf_op jit(solution)/shard_map/ppermute | solution.py:600
  16.8 0.0 collective-permute-start.5
  16.8 0.0 collective-permute-done.3.r1_ref
  16.8 1.4 %collective-permute-done.5.r3_ref = bf16[4,48,288]{2,1,0:T(8,128)(2,1)S(1)} collective-permute-done((bf16[4,48,288]{2,1,0:T(8,128)(2,1)S(1)}, bf16[4,48,288]{2,1,0:T(8,128)(2,1)S(1)}, u32[]{:S(2)}, u32[]{:S(2)}) %collective-permute-start.5) | collective-permute-done | bytes 110624 | tf_op jit(solution)/shard_map/ppermute | solution.py:600
  18.2 9.8 %posterior.1 = bf16[2,8,120,128]{3,2,1,0:T(8,128)(2,1)S(1)} custom-call(bf16[4,48,288]{2,1,0:T(8,128)(2,1)S(1)} %pad_maximum_fusion.r0_ref, bf16[4,48,288]{2,1,0:T(8,128)(2,1)S(1)} %collective-permute-done.3.r1_ref, bf16[4,48,288]{2,1,0:T(8,128)(2,1)S(1)} %collective-permute-done.4.r2_ref, bf16[4,48,288]{2,1,0:T(8,128)(2,1)S(1)} %collective-permute-done.5.r3_ref, ...), custom_call_target="tpu_custom_call" | custom-call | flops 10000000000 | bytes 30000000 | tf_op jit(solution)/shard_map/posterior/pallas_call | solution.py:543
  28.0 0.2 collective-permute-start.6
  28.3 1.4 %collective-permute-done.6 = bf16[8,120,128]{2,1,0:T(8,128)(2,1)S(1)} collective-permute-done((bf16[8,120,128]{2,1,0:T(8,128)(2,1)S(1)}, bf16[8,120,128]{2,1,0:T(8,128)(2,1)S(1)}, u32[]{:S(2)}, u32[]{:S(2)}) %collective-permute-start.6) | collective-permute-done | bytes 245792 | tf_op jit(solution)/shard_map/ppermute | solution.py:600
  29.6 0.1 fusion.3
  29.7 0.1 collective-permute-start.7
  29.8 3.1 %collective-permute-start.8 = (bf16[2,120,128]{2,1,0:T(8,128)(2,1)S(1)}, bf16[2,120,128]{2,1,0:T(8,128)(2,1)S(1)}, u32[]{:S(2)}, u32[]{:S(2)}) collective-permute-start(bf16[2,120,128]{2,1,0:T(8,128)(2,1)S(1)} %get-tuple-element.39), channel_id=1, source_target_pairs={{0,8},{1,9},{2,10},{3,11},{4,12},{5,13},{6,14},{7,15},{8,0},{9,1},... | collective-permute-start | bytes 184328 | tf_op jit(solution)/shard_map/ppermute | solution.py:600
  32.9 1.3 %collective-permute-start.9 = (bf16[2,120,128]{2,1,0:T(8,128)(2,1)S(1)}, bf16[2,120,128]{2,1,0:T(8,128)(2,1)S(1)}, u32[]{:S(2)}, u32[]{:S(2)}) collective-permute-start(bf16[2,120,128]{2,1,0:T(8,128)(2,1)S(1)} %get-tuple-element.38), channel_id=1, source_target_pairs={{0,12},{1,13},{2,14},{3,15},{4,8},{5,9},{6,10},{7,11},{8,4},{9,5},... | collective-permute-start | bytes 184328 | tf_op jit(solution)/shard_map/ppermute | solution.py:600
  34.2 0.8 %collective-permute-done.7 = bf16[2,120,128]{2,1,0:T(8,128)(2,1)S(1)} collective-permute-done((bf16[2,120,128]{2,1,0:T(8,128)(2,1)S(1)}, bf16[2,120,128]{2,1,0:T(8,128)(2,1)S(1)}, u32[]{:S(2)}, u32[]{:S(2)}) %collective-permute-start.7) | collective-permute-done | bytes 61472 | tf_op jit(solution)/shard_map/ppermute | solution.py:600
  34.9 1.8 %collective-permute-done.8 = bf16[2,120,128]{2,1,0:T(8,128)(2,1)S(1)} collective-permute-done((bf16[2,120,128]{2,1,0:T(8,128)(2,1)S(1)}, bf16[2,120,128]{2,1,0:T(8,128)(2,1)S(1)}, u32[]{:S(2)}, u32[]{:S(2)}) %collective-permute-start.8) | collective-permute-done | bytes 61472 | tf_op jit(solution)/shard_map/ppermute | solution.py:600
  36.8 2.2 %collective-permute-done.9 = bf16[2,120,128]{2,1,0:T(8,128)(2,1)S(1)} collective-permute-done((bf16[2,120,128]{2,1,0:T(8,128)(2,1)S(1)}, bf16[2,120,128]{2,1,0:T(8,128)(2,1)S(1)}, u32[]{:S(2)}, u32[]{:S(2)}) %collective-permute-start.9) | collective-permute-done | bytes 61472 | tf_op jit(solution)/shard_map/ppermute | solution.py:600
  39.1 1.6 %collective-permute-start.10 = (bf16[120,128]{1,0:T(8,128)(2,1)S(1)}, bf16[120,128]{1,0:T(8,128)(2,1)S(1)}, u32[]{:S(2)}, u32[]{:S(2)}) collective-permute-start(bf16[120,128]{1,0:T(8,128)(2,1)S(1)} %fusion.2), channel_id=1, source_target_pairs={{0,2},{1,3},{2,0},{3,1},{4,6},{5,7},{6,4},{7,5},{8,10},{9,11},{10,... | collective-permute-start | bytes 92168 | tf_op jit(solution)/shard_map/ppermute | solution.py:600
  40.6 2.4 %collective-permute-done.10.got_ref = bf16[120,128]{1,0:T(8,128)(2,1)S(1)} collective-permute-done((bf16[120,128]{1,0:T(8,128)(2,1)S(1)}, bf16[120,128]{1,0:T(8,128)(2,1)S(1)}, u32[]{:S(2)}, u32[]{:S(2)}) %collective-permute-start.10) | collective-permute-done | bytes 30752 | tf_op jit(solution)/shard_map/ppermute | solution.py:600
  43.0 1.1 %finish.1 = f32[48,288]{1,0:T(8,128)} custom-call(f32[120,128]{1,0:T(8,128)S(1)} %slice_bitcast_fusion.2.keep_ref, bf16[120,128]{1,0:T(8,128)(2,1)S(1)} %collective-permute-done.10.got_ref, bf16[4,160,288]{2,1,0:T(8,128)(2,1)S(1)} %get-tuple-element.34.back_ref), custom_call_target="tpu_custom_call" | custom-call | flops 1000000000 | bytes 3000000 | tf_op jit(solution)/shard_map/finish/pallas_call | solution.py:587
  (6 shorter events, 0.1 us)
Async XLA Ops:
  0.0 11.6 %copy-start = (bf16[48,288]{1,0:T(8,128)(2,1)S(1)}, bf16[48,288]{1,0:T(8,128)(2,1)}, u32[]{:S(2)}) copy-start(bf16[48,288]{1,0:T(8,128)(2,1)} %param.12) | copy-start | bytes 82948
  0.0 10.3 %collective-permute-start = (bf16[48,288]{1,0:T(8,128)(2,1)}, bf16[48,288]{1,0:T(8,128)(2,1)S(1)}, u32[]{:S(2)}, u32[]{:S(2)}) collective-permute-start(bf16[48,288]{1,0:T(8,128)(2,1)} %param.12), channel_id=1, source_target_pairs={{0,4},{1,5},{2,6},{3,7},{4,0},{5,1},{6,2},{7,3},{8,12},{9,13},{10,... | collective-permute-start | bytes 82952 | tf_op jit(solution)/shard_map/ppermute | solution.py:600
  3.0 7.2 %collective-permute-start.1 = (bf16[48,288]{1,0:T(8,128)(2,1)}, bf16[48,288]{1,0:T(8,128)(2,1)S(1)}, u32[]{:S(2)}, u32[]{:S(2)}) collective-permute-start(bf16[48,288]{1,0:T(8,128)(2,1)} %param.12), channel_id=1, source_target_pairs={{0,8},{1,9},{2,10},{3,11},{4,12},{5,13},{6,14},{7,15},{8,0},{9,1},... | collective-permute-start | bytes 82952 | tf_op jit(solution)/shard_map/ppermute | solution.py:600
  5.6 6.0 %collective-permute-start.2 = (bf16[48,288]{1,0:T(8,128)(2,1)}, bf16[48,288]{1,0:T(8,128)(2,1)S(1)}, u32[]{:S(2)}, u32[]{:S(2)}) collective-permute-start(bf16[48,288]{1,0:T(8,128)(2,1)} %param.12), channel_id=1, source_target_pairs={{0,12},{1,13},{2,14},{3,15},{4,8},{5,9},{6,10},{7,11},{8,4},{9,5},... | collective-permute-start | bytes 82952 | tf_op jit(solution)/shard_map/ppermute | solution.py:600
  11.6 5.2 %collective-permute-start.4 = (bf16[4,48,288]{2,1,0:T(8,128)(2,1)S(1)}, bf16[4,48,288]{2,1,0:T(8,128)(2,1)S(1)}, u32[]{:S(2)}, u32[]{:S(2)}) collective-permute-start(bf16[4,48,288]{2,1,0:T(8,128)(2,1)S(1)} %pad_maximum_fusion.r0_ref), channel_id=1, source_target_pairs={{0,2},{1,3},{2,0},{3,1},{4,6},{5,7},{6,4},{7,5},{8,10},{9,11},{10,... | collective-permute-start | bytes 331784 | tf_op jit(solution)/shard_map/ppermute | solution.py:600
  14.9 2.0 %collective-permute-start.3 = (bf16[4,48,288]{2,1,0:T(8,128)(2,1)S(1)}, bf16[4,48,288]{2,1,0:T(8,128)(2,1)S(1)}, u32[]{:S(2)}, u32[]{:S(2)}) collective-permute-start(bf16[4,48,288]{2,1,0:T(8,128)(2,1)S(1)} %pad_maximum_fusion.r0_ref), channel_id=1, source_target_pairs={{0,1},{1,0},{2,3},{3,2},{4,5},{5,4},{6,7},{7,6},{8,9},{9,8},{10,11... | collective-permute-start | bytes 331784 | tf_op jit(solution)/shard_map/ppermute | solution.py:600
  16.8 1.4 %collective-permute-start.5 = (bf16[4,48,288]{2,1,0:T(8,128)(2,1)S(1)}, bf16[4,48,288]{2,1,0:T(8,128)(2,1)S(1)}, u32[]{:S(2)}, u32[]{:S(2)}) collective-permute-start(bf16[4,48,288]{2,1,0:T(8,128)(2,1)S(1)} %collective-permute-done.4.r2_ref), channel_id=1, source_target_pairs={{0,1},{1,0},{2,3},{3,2},{4,5},{5,4},{6,7},{7,6},{8,9},{9,8},{10,11... | collective-permute-start | bytes 331784 | tf_op jit(solution)/shard_map/ppermute | solution.py:600
  28.0 1.6 %collective-permute-start.6 = (bf16[8,120,128]{2,1,0:T(8,128)(2,1)S(1)}, bf16[8,120,128]{2,1,0:T(8,128)(2,1)S(1)}, u32[]{:S(2)}, u32[]{:S(2)}) collective-permute-start(bf16[8,120,128]{2,1,0:T(8,128)(2,1)S(1)} %slice_bitcast_fusion), channel_id=1, source_target_pairs={{0,1},{1,0},{2,3},{3,2},{4,5},{5,4},{6,7},{7,6},{8,9},{9,8},{10,11... | collective-permute-start | bytes 737288 | tf_op jit(solution)/shard_map/ppermute | solution.py:600
  29.7 5.2 %collective-permute-start.7 = (bf16[2,120,128]{2,1,0:T(8,128)(2,1)S(1)}, bf16[2,120,128]{2,1,0:T(8,128)(2,1)S(1)}, u32[]{:S(2)}, u32[]{:S(2)}) collective-permute-start(bf16[2,120,128]{2,1,0:T(8,128)(2,1)S(1)} %get-tuple-element.37), channel_id=1, source_target_pairs={{0,4},{1,5},{2,6},{3,7},{4,0},{5,1},{6,2},{7,3},{8,12},{9,13},{10,... | collective-permute-start | bytes 184328 | tf_op jit(solution)/shard_map/ppermute | solution.py:600
  29.8 7.0 %collective-permute-start.8 = (bf16[2,120,128]{2,1,0:T(8,128)(2,1)S(1)}, bf16[2,120,128]{2,1,0:T(8,128)(2,1)S(1)}, u32[]{:S(2)}, u32[]{:S(2)}) collective-permute-start(bf16[2,120,128]{2,1,0:T(8,128)(2,1)S(1)} %get-tuple-element.39), channel_id=1, source_target_pairs={{0,8},{1,9},{2,10},{3,11},{4,12},{5,13},{6,14},{7,15},{8,0},{9,1},... | collective-permute-start | bytes 184328 | tf_op jit(solution)/shard_map/ppermute | solution.py:600
  32.9 6.1 %collective-permute-start.9 = (bf16[2,120,128]{2,1,0:T(8,128)(2,1)S(1)}, bf16[2,120,128]{2,1,0:T(8,128)(2,1)S(1)}, u32[]{:S(2)}, u32[]{:S(2)}) collective-permute-start(bf16[2,120,128]{2,1,0:T(8,128)(2,1)S(1)} %get-tuple-element.38), channel_id=1, source_target_pairs={{0,12},{1,13},{2,14},{3,15},{4,8},{5,9},{6,10},{7,11},{8,4},{9,5},... | collective-permute-start | bytes 184328 | tf_op jit(solution)/shard_map/ppermute | solution.py:600
  39.1 4.0 %collective-permute-start.10 = (bf16[120,128]{1,0:T(8,128)(2,1)S(1)}, bf16[120,128]{1,0:T(8,128)(2,1)S(1)}, u32[]{:S(2)}, u32[]{:S(2)}) collective-permute-start(bf16[120,128]{1,0:T(8,128)(2,1)S(1)} %fusion.2), channel_id=1, source_target_pairs={{0,2},{1,3},{2,0},{3,1},{4,6},{5,7},{6,4},{7,5},{8,10},{9,11},{10,... | collective-permute-start | bytes 92168 | tf_op jit(solution)/shard_map/ppermute | solution.py:600

commit v2 on v1

--- a/solution.py
+++ b/solution.py
@@ -25,18 +25,21 @@
 LANES = CHANS * STEP
 FREQS = ROT // 2 + 1
 ROWS8 = 8
-S_PAD = SHIFTS + 1
+S_STEP = 4
+S_PAD = -(-SHIFTS // S_STEP) * S_STEP
 ROWS = S_PAD * ROWS8
 LIVE = SHIFTS * ROWS8
 COLS = 512
-PAIRS_A = 16
-ROWS_A = 16 * PAIRS_A
-ROWS_B = ROWS - ROWS_A
+STEPS_A = 3
+GROUP = 256
+TAIL = 3 * LANES
+TAIL_ROWS = 16
 KPAD = 64
 QUADS = (FREQS + 1) // 4
 TILES = 3 * QUADS
 PAY = TILES * ROWS8
 BF = jnp.bfloat16
+F8 = jnp.float8_e5m2
 F32 = jnp.float32
 MIB = 1024 * 1024
 
@@ -248,32 +251,39 @@
     return x
 
 
-def transform_pairs(table_ref, pix_ref, slot_ref, fh_ref, fl_ref, count):
+def transform_steps(table_ref, pix_ref, slot_ref, fh_ref, fl_ref, first, count):
     slot = jnp.concatenate([slot_ref[...]] * 2, axis=0)
     nothing = jnp.zeros_like(slot)
 
-    def pair(sp, _):
-        x = []
-        for b in range(ROT):
-            halves = []
-            for h in range(2):
-                c = table_ref[2 * sp + h, b : b + 1, :]
-                s = table_ref[2 * sp + h, ROT + b : ROT + b + 1, :]
-                halves.append(pix_ref[0, b] * c + pix_ref[1, b] * s)
-            x.append(jnp.concatenate(halves, axis=0).astype(BF).astype(F32))
-        re, im = forward36(x)
-        im[0], im[ROT // 2] = slot, nothing
-        rows = pl.ds(pl.multiple_of(sp * 16, 16), 16)
-        for q in range(FREQS):
-            for part, value in ((0, re[q]), (1, im[q])):
-                hi = value.astype(BF)
-                fh_ref[q, rows, part * LANES : (part + 1) * LANES] = hi
-                fl_ref[q, rows, part * LANES : (part + 1) * LANES] = (
-                    value - hi.astype(F32)
-                ).astype(BF)
+    def step(i, _):
+        parts = []
+        for pair in range(S_STEP // 2):
+            x = []
+            for b in range(ROT):
+                halves = []
+                for h in range(2):
+                    at = S_STEP * i + 2 * pair + h
+                    c = table_ref[at, b : b + 1, :]
+                    s = table_ref[at, ROT + b : ROT + b + 1, :]
+                    halves.append(pix_ref[0, b] * c + pix_ref[1, b] * s)
+                x.append(jnp.concatenate(halves, axis=0).astype(BF).astype(F32))
+            re, im = forward36(x)
+            im[0], im[ROT // 2] = slot, nothing
+            row = pl.multiple_of((first + i) * S_STEP * ROWS8 + 16 * pair, 16)
+            low = []
+            for q in range(FREQS):
+                for part, value in ((0, re[q]), (1, im[q])):
+                    hi = value.astype(BF)
+                    fh_ref[q, pl.ds(row, 16), part * LANES : (part + 1) * LANES] = hi
+                    low.append(value - hi.astype(F32))
+            parts.append(low)
+        rows = pl.ds(pl.multiple_of((first + i) * S_STEP * ROWS8, S_STEP * ROWS8), S_STEP * ROWS8)
+        for n, low in enumerate(zip(*parts)):
+            cols = slice((n % 2) * LANES, (n % 2 + 1) * LANES)
+            fl_ref[n // 2, rows, cols] = jnp.concatenate(low, axis=0).astype(F8)
         return 0
 
-    lax.fori_loop(0, count, pair, 0)
+    lax.fori_loop(0, count, step, 0)
 
 
 def first_kernel(
@@ -284,8 +294,8 @@
     moves = [
         (grp_hbm, grp_ref), (bin_hbm, bin_ref), (img_hbm, img_ref), (sig_hbm, sig_ref),
         (ctf_hbm, ctf_ref), (exp_hbm, exp_ref), (perm_hbm, perm_ref),
-        (table_hbm.at[pl.ds(0, 2 * PAIRS_A)], table_ref),
-        (table_hbm.at[pl.ds(2 * PAIRS_A, S_PAD - 2 * PAIRS_A)], rest_ref),
+        (table_hbm.at[pl.ds(0, S_STEP * STEPS_A)], table_ref),
+        (table_hbm.at[pl.ds(S_STEP * STEPS_A, S_PAD - S_STEP * STEPS_A)], rest_ref),
     ]
     copies = [pltpu.make_async_copy(a, b, sems.at[i]) for i, (a, b) in enumerate(moves)]
     for copy in copies:
@@ -324,22 +334,26 @@
 
     off = lane & (STEP - 1)
     weight_hi = weight.astype(BF).astype(F32)
-    slot_ref[...] = jnp.where(off == 0, weight, jnp.where(off == 1, weight - weight_hi, 0.0))
+    slot_ref[...] = jnp.where(off == 0, weight_hi, jnp.where(off == 1, weight - weight_hi, 0.0))
     copies[7].wait()
-    transform_pairs(table_ref, pix_ref, slot_ref, fh_ref, fl_ref, PAIRS_A)
+    transform_steps(table_ref, pix_ref, slot_ref, fh_ref, fl_ref, 0, STEPS_A)
     copies[8].wait()
 
 
 def second_kernel(
-    table_ref, pix_ref, slot_ref, mt_hbm, back_hbm, fh_ref, fl_ref, mt_ref, back_ref, sems
+    fh_in, fl_in, table_ref, pix_ref, slot_ref, mt_hbm, back_hbm,
+    fh_ref, fl_ref, mt_ref, back_ref, sems,
 ):
+    del fh_in, fl_in
     copies = [
         pltpu.make_async_copy(mt_hbm, mt_ref, sems.at[0]),
         pltpu.make_async_copy(back_hbm, back_ref, sems.at[1]),
     ]
     for copy in copies:
         copy.start()
-    transform_pairs(table_ref, pix_ref, slot_ref, fh_ref, fl_ref, S_PAD // 2 - PAIRS_A)
+    transform_steps(
+        table_ref, pix_ref, slot_ref, fh_ref, fl_ref, STEPS_A, S_PAD // S_STEP - STEPS_A
+    )
     for copy in copies:
         copy.wait()
 
@@ -357,13 +371,13 @@
 
 
 def first_features(images, sigma2, ctf_group, defocus_bin):
-    feat = jax.ShapeDtypeStruct((FREQS, ROWS_A, 2 * LANES), BF)
-    tail = S_PAD - 2 * PAIRS_A
+    feat = (FREQS, ROWS, 2 * LANES)
+    tail = S_PAD - S_STEP * STEPS_A
     return pl.pallas_call(
         first_kernel,
         out_shape=(
-            feat,
-            feat,
+            jax.ShapeDtypeStruct(feat, BF),
+            jax.ShapeDtypeStruct(feat, F8),
             jax.ShapeDtypeStruct((2, ROT, ROWS8, LANES), F32),
             jax.ShapeDtypeStruct((ROWS8, LANES), F32),
             jax.ShapeDtypeStruct((tail, 2 * ROT, LANES), F32),
@@ -378,7 +392,7 @@
             pltpu.VMEM((BINS, LANES), F32),
             pltpu.VMEM((NGROUP, LANES), F32),
             pltpu.VMEM((BLOCK_COLS, BLOCK_COLS), BF),
-            pltpu.VMEM((2 * PAIRS_A, 2 * ROT, LANES), F32),
+            pltpu.VMEM((S_STEP * STEPS_A, 2 * ROT, LANES), F32),
             pltpu.VMEM((NGROUP, LANES), F32),
             pltpu.SemaphoreType.DMA((9,)),
         ],
@@ -391,25 +405,25 @@
     ))
 
 
-def second_features(table, pix, slot):
-    feat = jax.ShapeDtypeStruct((FREQS, ROWS_B, 2 * LANES), BF)
+def second_features(hi, lo, table, pix, slot):
     mt = np.stack(split(refs_transform()))
     back = np.stack([half for part in inverse_transform() for half in split(part)])
     return pl.pallas_call(
         second_kernel,
         out_shape=(
-            feat,
-            feat,
+            jax.ShapeDtypeStruct(hi.shape, BF),
+            jax.ShapeDtypeStruct(lo.shape, F8),
             jax.ShapeDtypeStruct(mt.shape, BF),
             jax.ShapeDtypeStruct(back.shape, BF),
         ),
-        in_specs=[VM] * 3 + [HB] * 2,
+        in_specs=[VM] * 5 + [HB] * 2,
         out_specs=[VM] * 4,
         scratch_shapes=[pltpu.SemaphoreType.DMA((2,))],
+        input_output_aliases={0: 0, 1: 1},
         compiler_params=pltpu.CompilerParams(vmem_limit_bytes=16 * MIB),
         cost_estimate=cost(2.5),
         name="features_second",
-    )(table, pix, slot, *in_hbm(jnp.asarray(mt), jnp.asarray(back)))
+    )(hi, lo, table, pix, slot, *in_hbm(jnp.asarray(mt), jnp.asarray(back)))
 
 
 def nt(left, right):
@@ -417,30 +431,43 @@
 
 
 def posterior_kernel(
-    direct, r0_ref, r1_ref, r2_ref, r3_ref, fha_ref, fla_ref, fhb_ref, flb_ref, mt_ref,
-    out_ref, x_ref, d_ref, c_ref, p_ref, num_ref,
+    direct, near_ref, rest_ref, near1_ref, rest1_ref, fh_ref, fl_ref, mt_ref,
+    out_ref, x_ref, d_ref, a_ref, e_ref, ca_ref, cb_ref, ct_ref, sa_ref, sb_ref, st_ref,
+    pa_ref, pb_ref, pt_ref, q_ref, num_ref,
 ):
     lane = lax.broadcasted_iota(jnp.int32, (CLASSES, LANES), 1)
     lane8 = lax.broadcasted_iota(jnp.int32, (8, LANES), 1)
+    row8 = lax.broadcasted_iota(jnp.int32, (8, LANES), 0)
 
     me = lax.axis_index("img") if direct else 0
     blank = jnp.zeros((KPAD - CLASSES, BLOCK_COLS), BF)
-    for group, ref in enumerate((r0_ref, r1_ref, r2_ref, r3_ref)):
-        for f in range(BLOCKS // 4):
-            row = pl.multiple_of((me ^ (4 * f + group)) * KPAD, KPAD)
-            x_ref[pl.ds(row, KPAD), :] = jnp.concatenate([ref[f], blank], axis=0)
+    for side, refs in enumerate(((near_ref, rest_ref), (near1_ref, rest1_ref))):
+        for entry in range(BLOCKS // 2):
+            values = refs[0][entry] if entry < 2 else refs[1][entry - 2]
+            block = me ^ (2 * (entry // 2) + 8 * (entry % 2) + side)
+            row = pl.multiple_of(block * KPAD, KPAD)
+            x_ref[pl.ds(row, KPAD), :] = jnp.concatenate([values, blank], axis=0)
     x = x_ref[...]
     d_ref[...] = nt(mt_ref[0], x) + nt(mt_ref[1], x)
-    square = jnp.square(x.astype(F32))
-    square_hi = square.astype(BF)
-    square_lo = (square - square_hi.astype(F32)).astype(BF)
-    e = lax.broadcasted_iota(jnp.int32, (8, BLOCK_COLS), 0)
-    col = lax.broadcasted_iota(jnp.int32, (8, BLOCK_COLS), 1)
-    power = jnp.where(e == jnp.where(col < ANG, 0, STEP), -0.5, 0.0).astype(BF)
-    d_ref[8:16, :] = nt(power, square_hi) + nt(power, square_lo)
-
-    c_ref[:, :, COLS - LANES :] = jnp.zeros((2 * FREQS, CLASSES, LANES), F32)
-    for q in range(FREQS):
+
+    for t in range(BLOCKS // 2):
+        cols = slice(t * LANES, (t + 1) * LANES)
+        edge = jnp.zeros((8, LANES), F32)
+        inner = jnp.zeros((8, LANES), F32)
+        for q in range(FREQS):
+            re = d_ref[q * 16 : q * 16 + 8, cols]
+            if q in (0, ROT // 2):
+                edge += re * re
+            else:
+                im = d_ref[q * 16 + 8 : q * 16 + 16, cols]
+                inner += re * re + im * im
+        power = -0.5 * (ROT * edge + (ROT // 2) * inner)
+        power += pltpu.roll(power, 7, 0)
+        power += pltpu.roll(power, 6, 0)
+        power = jnp.where((row8 & (STEP - 1)) == 0, power, 0.0)
+        d_ref[8:16, cols] = power + pltpu.roll(power, 1, 0)
+
+    def operand(q):
         tile = jnp.concatenate(
             [
                 d_ref[q * 16 + part * 8 : q * 16 + part * 8 + 8, t * LANES : (t + 1) * LANES]
@@ -453,40 +480,65 @@
         even, odd = tile[:CLASSES], tile[KPAD : KPAD + CLASSES]
         real = jnp.where(lane < 64, even, pltpu.roll(odd, 64, 1))
         imag = jnp.where(lane < 64, pltpu.roll(even, 64, 1), odd)
-        left = jnp.concatenate(
-            [jnp.concatenate([real, imag], axis=1), jnp.concatenate([-imag, real], axis=1)], axis=0
-        )
-        hi = left.astype(BF)
-        lo = (left - hi.astype(F32)).astype(BF)
-        both = jnp.concatenate([hi, lo], axis=0)
-        for fh, fl, span in ((fha_ref, fla_ref, slice(0, ROWS_A)), (fhb_ref, flb_ref, slice(ROWS_A, ROWS))):
-            first = nt(both, fh[q])
-            total = first[: 2 * CLASSES] + first[2 * CLASSES :] + nt(hi, fl[q])
-            c_ref[2 * q, :, span] = total[:CLASSES]
-            c_ref[2 * q + 1, :, span] = total[CLASSES:]
+        real_hi, imag_hi = real.astype(BF), imag.astype(BF)
+        real_lo = (real - real_hi.astype(F32)).astype(BF)
+        imag_lo = (imag - imag_hi.astype(F32)).astype(BF)
+        for first, re, im in ((0, real_hi, imag_hi), (2 * CLASSES, real_lo, imag_lo)):
+            a_ref[q, first : first + CLASSES, :LANES] = re
+            a_ref[q, first : first + CLASSES, LANES:] = im
+            a_ref[q, first + CLASSES : first + 2 * CLASSES, :LANES] = -im
+            a_ref[q, first + CLASSES : first + 2 * CLASSES, LANES:] = re
+        left = [jnp.concatenate([real, imag], axis=1), jnp.concatenate([-imag, real], axis=1)]
+        e_ref[q] = jnp.concatenate(left, axis=0).astype(F8)
 
     tiles_k = CLASSES // 8
 
-    def where_of(i):
-        col = pl.multiple_of((i // tiles_k) * LANES, LANES)
-        row = pl.multiple_of((i % tiles_k) * 8, 8)
-        return pl.ds(row, 8), pl.ds(col, LANES), col
-
-    def to_scores(i, top):
-        rows, cols, col = where_of(i)
+    def cross(q, rows):
+        both = a_ref[q]
+        first = nt(both, fh_ref[q, rows])
+        return first[: 2 * CLASSES] + first[2 * CLASSES :] + nt(e_ref[q], fl_ref[q, rows])
+
+    def cross_first(q):
+        total = cross(q, slice(0, GROUP))
+        if q + 1 < FREQS:
+            operand(q + 1)
+        ca_ref[2 * q] = total[:CLASSES]
+        ca_ref[2 * q + 1] = total[CLASSES:]
+
+    def cross_second(q):
+        total = cross(q, slice(GROUP, ROWS))
+        cb_ref[2 * q] = total[:CLASSES, : TAIL - GROUP]
+        cb_ref[2 * q + 1] = total[CLASSES:, : TAIL - GROUP]
+        last = total[:, TAIL - GROUP : TAIL - GROUP + TAIL_ROWS]
+        last = jnp.concatenate([last, jnp.zeros((2 * CLASSES, LANES - TAIL_ROWS), F32)], axis=1)
+        for part in range(2):
+            packed = last[part * CLASSES : part * CLASSES + 8]
+            for kt in range(1, tiles_k):
+                row = part * CLASSES + kt * 8
+                packed += pltpu.roll(last[row : row + 8], kt * TAIL_ROWS, 1)
+            ct_ref[2 * q + part] = packed
+
+    def tiles_of(c_ref, s_ref, p_ref):
+        return [
+            (c_ref, s_ref, p_ref, slice(row, row + 8), slice(col, col + LANES))
+            for col in range(0, c_ref.shape[2], LANES)
+            for row in range(0, c_ref.shape[1], 8)
+        ]
+
+    packed_live = ((lane8 & (TAIL_ROWS - 1)) < LIVE - TAIL) & (lane8 < tiles_k * TAIL_ROWS)
+
+    def to_scores(where, top):
+        c_ref, s_ref, _, rows, cols = where
         re = [c_ref[2 * q, rows, cols] for q in range(FREQS)]
         im = [None] + [c_ref[2 * q + 1, rows, cols] for q in range(1, FREQS - 1)] + [None]
-        re[0] = jnp.where(lane8 + col < LIVE, re[0], -1e30)
+        if c_ref is ct_ref:
+            re[0] = jnp.where(packed_live, re[0], -1e30)
         x = inverse36(re, im)
         for r in range(ROT):
-            c_ref[r, rows, cols] = x[r]
-        peak = x[0]
-        for r in range(1, ROT):
-            peak = jnp.maximum(peak, x[r])
-        return jnp.maximum(top, peak)
-
-    count = tiles_k * (COLS // LANES)
-    top = lax.fori_loop(0, count, to_scores, jnp.full((8, LANES), -1e30, F32))
+            s_ref[r, rows, cols] = x[r]
+        while len(x) > 1:
+            x = [jnp.maximum(*x[i : i + 2]) if i + 1 < len(x) else x[i] for i in range(0, len(x), 2)]
+        return x[0] if top is None else jnp.maximum(top, x[0])
 
     def fold(v, op):
         for t in (4, 2, 1):
@@ -495,67 +547,119 @@
             v = op(v, pltpu.roll(v, t, 1))
         return v
 
-    top = fold(top, jnp.maximum)
-
-    def to_posterior(i, total):
-        rows, cols, _ = where_of(i)
-        x = [jnp.exp(c_ref[r, rows, cols] - top) for r in range(ROT)]
+    def to_posterior(where, top, total):
+        _, s_ref, p_ref, rows, cols = where
+        x = [jnp.exp(s_ref[r, rows, cols] - top) for r in range(ROT)]
         re, im = forward36(x)
         for q in range(FREQS):
-            c_ref[2 * q, rows, cols] = re[q]
+            p_ref[2 * q, rows, cols] = re[q]
             if im[q] is not None:
-                c_ref[2 * q + 1, rows, cols] = im[q]
-            else:
-                c_ref[2 * q + 1, rows, cols] = jnp.zeros_like(re[q])
-        return total + re[0]
-
-    total = lax.fori_loop(0, count, to_posterior, jnp.zeros((8, LANES), F32))
-    inverse = 1.0 / fold(total, jnp.add)
-    scale = jnp.concatenate([inverse[:1]] * (COLS // LANES), axis=1)
-
-    def product(q):
-        p_ref[:CLASSES, :] = (c_ref[2 * q] * scale).astype(BF)
-        p_ref[CLASSES:, :] = (c_ref[2 * q + 1] * scale).astype(BF)
-        o = jnp.dot(p_ref[:, :ROWS_A], fha_ref[q], preferred_element_type=F32)
-        o += jnp.dot(p_ref[:, ROWS_A:ROWS], fhb_ref[q], preferred_element_type=F32)
+                p_ref[2 * q + 1, rows, cols] = im[q]
+        return re[0] if total is None else total + re[0]
+
+    operand(0)
+    for q in range(FREQS):
+        cross_first(q)
+    tiles_a = tiles_of(ca_ref, sa_ref, pa_ref)
+    top_a = total_a = None
+    todo = list(range(FREQS))
+    for step, where in enumerate(tiles_a):
+        top_a = to_scores(where, top_a)
+        while todo and todo[0] * 2 * len(tiles_a) < (step + 1) * FREQS:
+            cross_second(todo.pop(0))
+    top_a = fold(top_a, jnp.maximum)
+    for step, where in enumerate(tiles_a):
+        total_a = to_posterior(where, top_a, total_a)
+        while todo and todo[0] * 2 * len(tiles_a) < (len(tiles_a) + step + 1) * FREQS:
+            cross_second(todo.pop(0))
+    for q in todo:
+        cross_second(q)
+    tiles_b = tiles_of(cb_ref, sb_ref, pb_ref) + tiles_of(ct_ref, st_ref, pt_ref)
+    top_b = total_b = None
+    for where in tiles_b:
+        top_b = to_scores(where, top_b)
+    top_b = fold(top_b, jnp.maximum)
+    for where in tiles_b:
+        total_b = to_posterior(where, top_b, total_b)
+    top = jnp.maximum(top_a, top_b)
+    part_a, part_b = jnp.exp(top_a - top), jnp.exp(top_b - top)
+    inverse = 1.0 / (part_a * fold(total_a, jnp.add) + part_b * fold(total_b, jnp.add))
+    scale_a, scale_b = (part_a * inverse)[:1], (part_b * inverse)[:1]
+
+    def scaled(q):
+        for part in range(2):
+            rows = slice(part * CLASSES, (part + 1) * CLASSES)
+            if part == 1 and q in (0, ROT // 2):
+                q_ref[q, rows, :] = jnp.zeros((CLASSES, COLS), BF)
+                continue
+            slot = 2 * q + part
+            for col in range(0, GROUP, LANES):
+                value = pa_ref[slot, :, col : col + LANES] * scale_a
+                q_ref[q, rows, col : col + LANES] = value.astype(BF)
+            q_ref[q, rows, GROUP:TAIL] = (pb_ref[slot] * scale_b).astype(BF)
+            packed = jnp.where(packed_live, pt_ref[slot] * scale_b, 0.0)
+            last = [packed] + [
+                pltpu.roll(packed, LANES - kt * TAIL_ROWS, 1) for kt in range(1, tiles_k)
+            ]
+            last = jnp.where(lane < TAIL_ROWS, jnp.concatenate(last, axis=0), 0.0)
+            q_ref[q, rows, TAIL:] = last.astype(BF)
+
+    third = 2 * CLASSES // 3
+    order = [4 * quad + slot for quad in range(QUADS) for slot in (3, 0, 1, 2)]
+    order = [q for q in order if q < FREQS]
+    extra = jnp.zeros((2 * CLASSES, LANES), F32)
+    scaled(order[0])
+    for n, q in enumerate(order):
+        o = jnp.dot(q_ref[q, :, :ROWS], fh_ref[q], preferred_element_type=F32)
+        if n + 1 < len(order):
+            scaled(order[n + 1])
         real = o[:CLASSES, :LANES] + o[CLASSES:, LANES:]
         imag = o[:CLASSES, LANES:] - o[CLASSES:, :LANES]
-        return jnp.concatenate([real, imag], axis=0)
-
-    third = 2 * CLASSES // 3
-    for quad in range(QUADS):
-        if 4 * quad + 3 < FREQS:
-            extra = product(4 * quad + 3)
-        else:
+        both = jnp.concatenate([real, imag], axis=0)
+        quad, slot = q // 4, q % 4
+        if slot == 3:
+            extra = both
+            continue
+        if 4 * quad + 3 >= FREQS:
             extra = jnp.zeros((2 * CLASSES, LANES), F32)
-        for slot in range(3):
-            tile = [product(4 * quad + slot), extra[slot * third : (slot + 1) * third]]
-            num_ref[slot * QUADS + quad] = jnp.concatenate(tile, axis=0).T
+        tile = [both, extra[slot * third : (slot + 1) * third]]
+        num_ref[slot * QUADS + quad] = jnp.concatenate(tile, axis=0).T
     core, chip = me % 2, me // 2
     for half in range(2):
         side = (1 - core) if half == 0 else core
         for e in range(BLOCKS // 2):
-            row = pl.multiple_of(side * (LANES // 2) + (chip ^ e) * ROWS8, ROWS8)
+            row = side * (LANES // 2) + (chip ^ (e // 2 + 4 * (e % 2))) * ROWS8
+            row = pl.multiple_of(row, ROWS8)
             out_ref[half, e] = num_ref[:, pl.ds(row, 8), :].reshape(PAY, LANES).astype(BF)
 
 
-def make_payload(direct, refs, feat_a, feat_b, mt):
+def make_payload(direct, refs, feat_hi, feat_lo, mt):
     return pl.pallas_call(
         functools.partial(posterior_kernel, direct),
         out_shape=jax.ShapeDtypeStruct((2, BLOCKS // 2, PAY, LANES), BF),
-        in_specs=[VM] * 9,
+        in_specs=[VM] * 7,
         out_specs=VM,
         scratch_shapes=[
             pltpu.VMEM((BLOCKS * KPAD, BLOCK_COLS), BF),
             pltpu.VMEM((FREQS * 16, BLOCKS * KPAD), F32),
-            pltpu.VMEM((2 * FREQS, CLASSES, COLS), F32),
-            pltpu.VMEM((2 * CLASSES, COLS), BF),
+            pltpu.VMEM((FREQS, 4 * CLASSES, 2 * LANES), BF),
+            pltpu.VMEM((FREQS, 2 * CLASSES, 2 * LANES), F8),
+            pltpu.VMEM((2 * FREQS, CLASSES, GROUP), F32),
+            pltpu.VMEM((2 * FREQS, CLASSES, TAIL - GROUP), F32),
+            pltpu.VMEM((2 * FREQS, 8, LANES), F32),
+            pltpu.VMEM((ROT, CLASSES, GROUP), F32),
+            pltpu.VMEM((ROT, CLASSES, TAIL - GROUP), F32),
+            pltpu.VMEM((ROT, 8, LANES), F32),
+            pltpu.VMEM((2 * FREQS, CLASSES, GROUP), F32),
+            pltpu.VMEM((2 * FREQS, CLASSES, TAIL - GROUP), F32),
+            pltpu.VMEM((2 * FREQS, 8, LANES), F32),
+            pltpu.VMEM((FREQS, 2 * CLASSES, COLS), BF),
             pltpu.VMEM((TILES, LANES, LANES), F32),
         ],
-        compiler_params=pltpu.CompilerParams(vmem_limit_bytes=24 * MIB),
+        compiler_params=pltpu.CompilerParams(vmem_limit_bytes=28 * MIB),
         cost_estimate=cost(10.0),
         name="posterior",
-    )(*refs, *feat_a, *feat_b, mt)
+    )(*refs, feat_hi, feat_lo, mt)
 
 
 def final_kernel(keep_ref, got_ref, back_ref, out_ref):
@@ -602,12 +706,12 @@
 
 def reduce_direct(pay):
     pairs = pay[1].astype(F32) + swap(pay[0], 1).astype(F32)
-    pairs = pairs.reshape((BLOCKS // 4, 2) + pairs.shape[1:])
-    parts = [swap(pairs[f].astype(BF), 4 * f) for f in range(1, BLOCKS // 4)]
+    pairs = pairs.reshape((4, BLOCKS // 8) + pairs.shape[1:])
+    parts = [swap(pairs[g].astype(BF), 2 * g) for g in (1, 2, 3)]
     total = pairs[0]
     for part in parts:
         total = total + part.astype(F32)
-    return total[0], swap(total[1].astype(BF), 2)
+    return total[0], swap(total[1].astype(BF), 8)
 
 
 def on_device(images, class_refs, sigma2, ctf_group, defocus_bin):
@@ -616,33 +720,37 @@
     me = lax.axis_index("img")
     direct = devices == BLOCKS and share == BLOCK_COLS
     if direct:
-        line = [swap(class_refs, 4 * f) for f in range(1, BLOCKS // 4)]
+        near = swap(class_refs, 8)
     else:
         whole = lax.all_gather(class_refs, "img", axis=1, tiled=True)
-        blocks = whole.reshape(CLASSES, BLOCKS // 4, 4, BLOCK_COLS).transpose(2, 1, 0, 3)
-        refs = [blocks[g] for g in range(4)]
+        blocks = whole.reshape(CLASSES, BLOCKS, BLOCK_COLS).transpose(1, 0, 2)
+        order = [2 * (e // 2) + 8 * (e % 2) for e in range(BLOCKS // 2)]
+        sides = [jnp.stack([blocks[m + side] for m in order]) for side in range(2)]
+        refs = [part for side in sides for part in (side[:2], side[2:])]
     pay = None
     for first in range(0, images.shape[0], ROWS8):
         part = slice(first, first + ROWS8)
-        fha, fla, pix, slot, rest = first_features(
+        hi, lo, pix, slot, table = first_features(
             images[part], sigma2, ctf_group[part], defocus_bin[part]
         )
         if direct and first == 0:
-            line, fha = lax.optimization_barrier((line, fha))
-            line = jnp.stack([class_refs] + line)
-            across = swap(line, 2)
-        fhb, flb, mt, back = second_features(rest, pix, slot)
+            near, hi = lax.optimization_barrier((near, hi))
+            near = jnp.stack([class_refs, near])
+            rest = [swap(near, 2 * g) for g in (1, 2, 3)]
+        hi, lo, mt, back = second_features(hi, lo, table, pix, slot)
         if direct and first == 0:
-            across, fhb = lax.optimization_barrier((across, fhb))
-            refs = [line, swap(line, 1), across, swap(across, 1)]
-        one = make_payload(direct, refs, (fha, fla), (fhb, flb), mt)
+            rest, hi = lax.optimization_barrier((rest, hi))
+            rest = jnp.concatenate(rest)
+            refs = [near, rest, swap(near, 1), swap(rest, 1)]
+        one = make_payload(direct, refs, hi, lo, mt)
         pay = one if pay is None else pay + one
     if direct:
         return finish(*reduce_direct(pay), back)
     summed = lax.psum(pay.astype(F32), "img")
     start = me * share
     block = start // BLOCK_COLS
-    mine = summed[1 - block % 2, block // 2]
+    chip = block // 2
+    mine = summed[1 - block % 2, 2 * (chip % 4) + chip // 4]
     return lax.dynamic_slice_in_dim(
         finish(mine, jnp.zeros_like(mine, BF), back), start % BLOCK_COLS, share, 1
     )

time: 44.2 us -> 39.6 us (0.90)
  waiting for transfers between devices: 13.1 us -> 9.76 us
  Pallas kernels: 17.2 us -> 14.8 us
  starting transfers between devices: 13.5 us -> 14.5 us
    ppermute x11, waiting for transfers between devices: 13.1 us -> 9.76 us  [swap(): return lax.ppermute(value, 'img', pairs)]
    pallas_call x1, Pallas kernels: 9.79 us -> 7.35 us  [make_payload(): pl.pallas_call(functools.partial(posterior_kernel, direct), out_shape=jax...]
    ppermute x11, starting transfers between devices: 13.5 us -> 14.5 us  [swap(): return lax.ppermute(value, 'img', pairs)]
  transfers between devices with their start and end apart: 11 -> 11, of which waited for: 8 -> 7; matrix products, arithmetic and copies ran while one was open for 0% -> 0% of each run, Pallas kernels for 14% -> 16%
where the time goes in v2:
time: 39.6 us; the launch traced here: 39.4 us
  Pallas kernels  14.8 us (37%)
  starting transfers between devices  14.5 us (37%)
  waiting for transfers between devices  9.76 us (25%)
    ppermute x11, starting transfers between devices, swap(): return lax.ppermute(value, 'img', pairs)  14.5 us
    ppermute x11, waiting for transfers between devices, swap(): return lax.ppermute(value, 'img', pairs)  9.76 us
    pallas_call x1, Pallas kernels, make_payload(): pl.pallas_call(functools.partial(posterior_kernel, direct), out_shape=jax...  7.35 us
    pallas_call x1, Pallas kernels, second_features(): pl.pallas_call(second_kernel, out_shape=(jax.ShapeDtypeStruct(hi.shape, B...  3.54 us
    pallas_call x1, Pallas kernels, first_features(): pl.pallas_call(first_kernel, out_shape=(jax.ShapeDtypeStruct(feat, BF), j...  2.82 us
    pallas_call x1, Pallas kernels, finish(): pl.pallas_call(final_kernel, out_shape=jax.ShapeDtypeStruct((CLASSES, BLO...  1.08 us
  transfers between devices with their start and end apart: 11, of which 7 were waited for; matrix products, arithmetic and copies ran while one was open for 0% of the time, Pallas kernels for 16%

profile of v2, /device:TPU:0, one launch (start us, length us, event | category | flops | bytes accessed | tf_op | source)
XLA Modules:
  0.0 39.4 jit_solution(4182222576051065963)
XLA Ops:
  0.0 0.0 copy-start
  0.0 4.0 %collective-permute-start = (bf16[48,288]{1,0:T(8,128)(2,1)}, bf16[48,288]{1,0:T(8,128)(2,1)S(1)}, u32[]{:S(2)}, u32[]{:S(2)}) collective-permute-start(bf16[48,288]{1,0:T(8,128)(2,1)} %param.12), channel_id=1, source_target_pairs={{0,8},{1,9},{2,10},{3,11},{4,12},{5,13},{6,14},{7,15},{8,0},{9,1},... | collective-permute-start | bytes 82952 | tf_op jit(solution)/shard_map/ppermute | solution.py:704
  4.0 2.8 %features_first.1 = (bf16[19,416,256]{2,1,0:T(8,128)(2,1)S(1)}, f8e5m2[19,416,256]{2,1,0:T(32,128)(4,1)S(1)}, f32[2,36,8,128]{3,2,1,0:T(8,128)S(1)}, f32[8,128]{1,0:T(8,128)S(1)}, f32[40,72,128]{2,1,0:T(8,128)S(1)}) custom-call(s32[8]{0:T(128)} %grp_hbm.1, s32[8]{0:T(128)} %bin_hbm.1, bf16[8,4608]{1,0:T(8,128)(2,1)} %img_hbm.1, f32[16,16]{1,0:T(8,128)} %sig_hbm.1, ...), custom_call_target="tpu_custom_call" | custom-call | flops 4499999744 | bytes 13500000 | tf_op jit(solution)/shard_map/features_first/pallas_call | solution.py:376
  6.9 0.0 collective-permute-done
  6.9 0.0 copy-done
  6.9 1.6 %collective-permute-start.1 = (bf16[2,48,288]{2,1,0:T(8,128)(2,1)S(1)}, bf16[2,48,288]{2,1,0:T(8,128)(2,1)S(1)}, u32[]{:S(2)}, u32[]{:S(2)}) collective-permute-start(bf16[2,48,288]{2,1,0:T(8,128)(2,1)S(1)} %pad_maximum_fusion.near_ref), channel_id=1, source_target_pairs={{0,2},{1,3},{2,0},{3,1},{4,6},{5,7},{6,4},{7,5},{8,10},{9,11},{10,... | collective-permute-start | bytes 165896 | tf_op jit(solution)/shard_map/ppermute | solution.py:704
  8.5 1.6 %collective-permute-start.2 = (bf16[2,48,288]{2,1,0:T(8,128)(2,1)S(1)}, bf16[2,48,288]{2,1,0:T(8,128)(2,1)S(1)}, u32[]{:S(2)}, u32[]{:S(2)}) collective-permute-start(bf16[2,48,288]{2,1,0:T(8,128)(2,1)S(1)} %pad_maximum_fusion.near_ref), channel_id=1, source_target_pairs={{0,4},{1,5},{2,6},{3,7},{4,0},{5,1},{6,2},{7,3},{8,12},{9,13},{10,... | collective-permute-start | bytes 165896 | tf_op jit(solution)/shard_map/ppermute | solution.py:704
  10.1 0.4 collective-permute-start.3
  10.5 3.5 %features_second.1 = (bf16[19,416,256]{2,1,0:T(8,128)(2,1)S(1)}, f8e5m2[19,416,256]{2,1,0:T(32,128)(4,1)S(1)}, bf16[2,304,288]{2,1,0:T(8,128)(2,1)S(1)}, bf16[4,160,288]{2,1,0:T(8,128)(2,1)S(1)}) custom-call(bf16[19,416,256]{2,1,0:T(8,128)(2,1)S(1)} %get-tuple-element.22.fh_in, ...), custom_call_target="tpu_custom_call", output_to_operand_aliasing={{0}: (0, {}), {1}: (1, {})} | custom-call | flops 2500000000 | bytes 7500000 | tf_op jit(solution)/shard_map/features_second/pallas_call | solution.py:411
  14.0 0.0 collective-permute-done.1
  14.0 0.0 collective-permute-done.2
  14.0 1.3 %collective-permute-done.3 = bf16[2,48,288]{2,1,0:T(8,128)(2,1)S(1)} collective-permute-done((bf16[2,48,288]{2,1,0:T(8,128)(2,1)S(1)}, bf16[2,48,288]{2,1,0:T(8,128)(2,1)S(1)}, u32[]{:S(2)}, u32[]{:S(2)}) %collective-permute-start.3) | collective-permute-done | bytes 55328 | tf_op jit(solution)/shard_map/ppermute | solution.py:704
  15.4 0.1 collective-permute-start.5
  15.5 0.5 %collective-permute-start.4 = (bf16[2,48,288]{2,1,0:T(8,128)(2,1)S(1)}, bf16[2,48,288]{2,1,0:T(8,128)(2,1)S(1)}, u32[]{:S(2)}, u32[]{:S(2)}) collective-permute-start(bf16[2,48,288]{2,1,0:T(8,128)(2,1)S(1)} %pad_maximum_fusion.near_ref), channel_id=1, source_target_pairs={{0,1},{1,0},{2,3},{3,2},{4,5},{5,4},{6,7},{7,6},{8,9},{9,8},{10,11... | collective-permute-start | bytes 165896 | tf_op jit(solution)/shard_map/ppermute | solution.py:704
  16.0 1.1 %collective-permute-done.4.near1_ref = bf16[2,48,288]{2,1,0:T(8,128)(2,1)S(1)} collective-permute-done((bf16[2,48,288]{2,1,0:T(8,128)(2,1)S(1)}, bf16[2,48,288]{2,1,0:T(8,128)(2,1)S(1)}, u32[]{:S(2)}, u32[]{:S(2)}) %collective-permute-start.4) | collective-permute-done | bytes 55328 | tf_op jit(solution)/shard_map/ppermute | solution.py:704
  17.0 0.0 collective-permute-done.5.rest1_ref
  17.0 7.3 %posterior.1 = bf16[2,8,120,128]{3,2,1,0:T(8,128)(2,1)S(1)} custom-call(bf16[2,48,288]{2,1,0:T(8,128)(2,1)S(1)} %pad_maximum_fusion.near_ref, bf16[6,48,288]{2,1,0:T(8,128)(2,1)S(1)} %constant_dynamic-update-slice_fusion.rest_ref, bf16[2,48,288]{2,1,0:T(8,128)(2,1)S(1)} %collective-permute-done.4.near1_ref, ...), custom_call_target="tpu_custom_call" | custom-call | flops 10000000000 | bytes 30000000 | tf_op jit(solution)/shard_map/posterior/pallas_call | solution.py:637
  24.4 0.3 collective-permute-start.6
  24.7 1.3 %collective-permute-done.6 = bf16[8,120,128]{2,1,0:T(8,128)(2,1)S(1)} collective-permute-done((bf16[8,120,128]{2,1,0:T(8,128)(2,1)S(1)}, bf16[8,120,128]{2,1,0:T(8,128)(2,1)S(1)}, u32[]{:S(2)}, u32[]{:S(2)}) %collective-permute-start.6) | collective-permute-done | bytes 245792 | tf_op jit(solution)/shard_map/ppermute | solution.py:704
  26.0 0.1 fusion.3
  26.1 0.6 %collective-permute-start.7 = (bf16[2,120,128]{2,1,0:T(8,128)(2,1)S(1)}, bf16[2,120,128]{2,1,0:T(8,128)(2,1)S(1)}, u32[]{:S(2)}, u32[]{:S(2)}) collective-permute-start(bf16[2,120,128]{2,1,0:T(8,128)(2,1)S(1)} %get-tuple-element.37), channel_id=1, source_target_pairs={{0,2},{1,3},{2,0},{3,1},{4,6},{5,7},{6,4},{7,5},{8,10},{9,11},{10,... | collective-permute-start | bytes 184328 | tf_op jit(solution)/shard_map/ppermute | solution.py:704
  26.7 1.3 %collective-permute-start.8 = (bf16[2,120,128]{2,1,0:T(8,128)(2,1)S(1)}, bf16[2,120,128]{2,1,0:T(8,128)(2,1)S(1)}, u32[]{:S(2)}, u32[]{:S(2)}) collective-permute-start(bf16[2,120,128]{2,1,0:T(8,128)(2,1)S(1)} %get-tuple-element.39), channel_id=1, source_target_pairs={{0,4},{1,5},{2,6},{3,7},{4,0},{5,1},{6,2},{7,3},{8,12},{9,13},{10,... | collective-permute-start | bytes 184328 | tf_op jit(solution)/shard_map/ppermute | solution.py:704
  28.0 1.7 %collective-permute-start.9 = (bf16[2,120,128]{2,1,0:T(8,128)(2,1)S(1)}, bf16[2,120,128]{2,1,0:T(8,128)(2,1)S(1)}, u32[]{:S(2)}, u32[]{:S(2)}) collective-permute-start(bf16[2,120,128]{2,1,0:T(8,128)(2,1)S(1)} %get-tuple-element.38), channel_id=1, source_target_pairs={{0,6},{1,7},{2,4},{3,5},{4,2},{5,3},{6,0},{7,1},{8,14},{9,15},{10,... | collective-permute-start | bytes 184328 | tf_op jit(solution)/shard_map/ppermute | solution.py:704
  29.7 0.7 %collective-permute-done.7 = bf16[2,120,128]{2,1,0:T(8,128)(2,1)S(1)} collective-permute-done((bf16[2,120,128]{2,1,0:T(8,128)(2,1)S(1)}, bf16[2,120,128]{2,1,0:T(8,128)(2,1)S(1)}, u32[]{:S(2)}, u32[]{:S(2)}) %collective-permute-start.7) | collective-permute-done | bytes 61472 | tf_op jit(solution)/shard_map/ppermute | solution.py:704
  30.4 1.1 %collective-permute-done.8 = bf16[2,120,128]{2,1,0:T(8,128)(2,1)S(1)} collective-permute-done((bf16[2,120,128]{2,1,0:T(8,128)(2,1)S(1)}, bf16[2,120,128]{2,1,0:T(8,128)(2,1)S(1)}, u32[]{:S(2)}, u32[]{:S(2)}) %collective-permute-start.8) | collective-permute-done | bytes 61472 | tf_op jit(solution)/shard_map/ppermute | solution.py:704
  31.5 1.6 %collective-permute-done.9 = bf16[2,120,128]{2,1,0:T(8,128)(2,1)S(1)} collective-permute-done((bf16[2,120,128]{2,1,0:T(8,128)(2,1)S(1)}, bf16[2,120,128]{2,1,0:T(8,128)(2,1)S(1)}, u32[]{:S(2)}, u32[]{:S(2)}) %collective-permute-start.9) | collective-permute-done | bytes 61472 | tf_op jit(solution)/shard_map/ppermute | solution.py:704
  33.2 2.6 %collective-permute-start.10 = (bf16[120,128]{1,0:T(8,128)(2,1)S(1)}, bf16[120,128]{1,0:T(8,128)(2,1)S(1)}, u32[]{:S(2)}, u32[]{:S(2)}) collective-permute-start(bf16[120,128]{1,0:T(8,128)(2,1)S(1)} %fusion.2), channel_id=1, source_target_pairs={{0,8},{1,9},{2,10},{3,11},{4,12},{5,13},{6,14},{7,15},{8,0},{9,1},... | collective-permute-start | bytes 92168 | tf_op jit(solution)/shard_map/ppermute | solution.py:704
  35.7 2.6 %collective-permute-done.10.got_ref = bf16[120,128]{1,0:T(8,128)(2,1)S(1)} collective-permute-done((bf16[120,128]{1,0:T(8,128)(2,1)S(1)}, bf16[120,128]{1,0:T(8,128)(2,1)S(1)}, u32[]{:S(2)}, u32[]{:S(2)}) %collective-permute-start.10) | collective-permute-done | bytes 30752 | tf_op jit(solution)/shard_map/ppermute | solution.py:704
  38.3 1.1 %finish.1 = f32[48,288]{1,0:T(8,128)} custom-call(f32[120,128]{1,0:T(8,128)S(1)} %slice_bitcast_fusion.2.keep_ref, bf16[120,128]{1,0:T(8,128)(2,1)S(1)} %collective-permute-done.10.got_ref, bf16[4,160,288]{2,1,0:T(8,128)(2,1)S(1)} %get-tuple-element.34.back_ref), custom_call_target="tpu_custom_call" | custom-call | flops 1000000000 | bytes 3000000 | tf_op jit(solution)/shard_map/finish/pallas_call | solution.py:691
  (9 shorter events, 0.1 us)
Async XLA Ops:
  0.0 6.9 %copy-start = (bf16[48,288]{1,0:T(8,128)(2,1)S(1)}, bf16[48,288]{1,0:T(8,128)(2,1)}, u32[]{:S(2)}) copy-start(bf16[48,288]{1,0:T(8,128)(2,1)} %param.12) | copy-start | bytes 82948
  0.0 6.9 %collective-permute-start = (bf16[48,288]{1,0:T(8,128)(2,1)}, bf16[48,288]{1,0:T(8,128)(2,1)S(1)}, u32[]{:S(2)}, u32[]{:S(2)}) collective-permute-start(bf16[48,288]{1,0:T(8,128)(2,1)} %param.12), channel_id=1, source_target_pairs={{0,8},{1,9},{2,10},{3,11},{4,12},{5,13},{6,14},{7,15},{8,0},{9,1},... | collective-permute-start | bytes 82952 | tf_op jit(solution)/shard_map/ppermute | solution.py:704
  6.9 7.1 %collective-permute-start.1 = (bf16[2,48,288]{2,1,0:T(8,128)(2,1)S(1)}, bf16[2,48,288]{2,1,0:T(8,128)(2,1)S(1)}, u32[]{:S(2)}, u32[]{:S(2)}) collective-permute-start(bf16[2,48,288]{2,1,0:T(8,128)(2,1)S(1)} %pad_maximum_fusion.near_ref), channel_id=1, source_target_pairs={{0,2},{1,3},{2,0},{3,1},{4,6},{5,7},{6,4},{7,5},{8,10},{9,11},{10,... | collective-permute-start | bytes 165896 | tf_op jit(solution)/shard_map/ppermute | solution.py:704
  8.5 5.5 %collective-permute-start.2 = (bf16[2,48,288]{2,1,0:T(8,128)(2,1)S(1)}, bf16[2,48,288]{2,1,0:T(8,128)(2,1)S(1)}, u32[]{:S(2)}, u32[]{:S(2)}) collective-permute-start(bf16[2,48,288]{2,1,0:T(8,128)(2,1)S(1)} %pad_maximum_fusion.near_ref), channel_id=1, source_target_pairs={{0,4},{1,5},{2,6},{3,7},{4,0},{5,1},{6,2},{7,3},{8,12},{9,13},{10,... | collective-permute-start | bytes 165896 | tf_op jit(solution)/shard_map/ppermute | solution.py:704
  10.1 5.3 %collective-permute-start.3 = (bf16[2,48,288]{2,1,0:T(8,128)(2,1)S(1)}, bf16[2,48,288]{2,1,0:T(8,128)(2,1)S(1)}, u32[]{:S(2)}, u32[]{:S(2)}) collective-permute-start(bf16[2,48,288]{2,1,0:T(8,128)(2,1)S(1)} %pad_maximum_fusion.near_ref), channel_id=1, source_target_pairs={{0,6},{1,7},{2,4},{3,5},{4,2},{5,3},{6,0},{7,1},{8,14},{9,15},{10,... | collective-permute-start | bytes 165896 | tf_op jit(solution)/shard_map/ppermute | solution.py:704
  15.4 1.7 %collective-permute-start.5 = (bf16[6,48,288]{2,1,0:T(8,128)(2,1)S(1)}, bf16[6,48,288]{2,1,0:T(8,128)(2,1)S(1)}, u32[]{:S(2)}, u32[]{:S(2)}) collective-permute-start(bf16[6,48,288]{2,1,0:T(8,128)(2,1)S(1)} %constant_dynamic-update-slice_fusion.rest_ref), channel_id=1, source_target_pairs={{0,1},{1,0},{2,3},{3,2},{4,5},{5,4},{6,7},{7,6},{8,9},{9,8},{10,11... | collective-permute-start | bytes 497672 | tf_op jit(solution)/shard_map/ppermute | solution.py:704
  15.5 1.6 %collective-permute-start.4 = (bf16[2,48,288]{2,1,0:T(8,128)(2,1)S(1)}, bf16[2,48,288]{2,1,0:T(8,128)(2,1)S(1)}, u32[]{:S(2)}, u32[]{:S(2)}) collective-permute-start(bf16[2,48,288]{2,1,0:T(8,128)(2,1)S(1)} %pad_maximum_fusion.near_ref), channel_id=1, source_target_pairs={{0,1},{1,0},{2,3},{3,2},{4,5},{5,4},{6,7},{7,6},{8,9},{9,8},{10,11... | collective-permute-start | bytes 165896 | tf_op jit(solution)/shard_map/ppermute | solution.py:704
  24.4 1.6 %collective-permute-start.6 = (bf16[8,120,128]{2,1,0:T(8,128)(2,1)S(1)}, bf16[8,120,128]{2,1,0:T(8,128)(2,1)S(1)}, u32[]{:S(2)}, u32[]{:S(2)}) collective-permute-start(bf16[8,120,128]{2,1,0:T(8,128)(2,1)S(1)} %slice_bitcast_fusion), channel_id=1, source_target_pairs={{0,1},{1,0},{2,3},{3,2},{4,5},{5,4},{6,7},{7,6},{8,9},{9,8},{10,11... | collective-permute-start | bytes 737288 | tf_op jit(solution)/shard_map/ppermute | solution.py:704
  26.1 4.3 %collective-permute-start.7 = (bf16[2,120,128]{2,1,0:T(8,128)(2,1)S(1)}, bf16[2,120,128]{2,1,0:T(8,128)(2,1)S(1)}, u32[]{:S(2)}, u32[]{:S(2)}) collective-permute-start(bf16[2,120,128]{2,1,0:T(8,128)(2,1)S(1)} %get-tuple-element.37), channel_id=1, source_target_pairs={{0,2},{1,3},{2,0},{3,1},{4,6},{5,7},{6,4},{7,5},{8,10},{9,11},{10,... | collective-permute-start | bytes 184328 | tf_op jit(solution)/shard_map/ppermute | solution.py:704
  26.7 4.8 %collective-permute-start.8 = (bf16[2,120,128]{2,1,0:T(8,128)(2,1)S(1)}, bf16[2,120,128]{2,1,0:T(8,128)(2,1)S(1)}, u32[]{:S(2)}, u32[]{:S(2)}) collective-permute-start(bf16[2,120,128]{2,1,0:T(8,128)(2,1)S(1)} %get-tuple-element.39), channel_id=1, source_target_pairs={{0,4},{1,5},{2,6},{3,7},{4,0},{5,1},{6,2},{7,3},{8,12},{9,13},{10,... | collective-permute-start | bytes 184328 | tf_op jit(solution)/shard_map/ppermute | solution.py:704
  28.0 5.1 %collective-permute-start.9 = (bf16[2,120,128]{2,1,0:T(8,128)(2,1)S(1)}, bf16[2,120,128]{2,1,0:T(8,128)(2,1)S(1)}, u32[]{:S(2)}, u32[]{:S(2)}) collective-permute-start(bf16[2,120,128]{2,1,0:T(8,128)(2,1)S(1)} %get-tuple-element.38), channel_id=1, source_target_pairs={{0,6},{1,7},{2,4},{3,5},{4,2},{5,3},{6,0},{7,1},{8,14},{9,15},{10,... | collective-permute-start | bytes 184328 | tf_op jit(solution)/shard_map/ppermute | solution.py:704
  33.2 5.2 %collective-permute-start.10 = (bf16[120,128]{1,0:T(8,128)(2,1)S(1)}, bf16[120,128]{1,0:T(8,128)(2,1)S(1)}, u32[]{:S(2)}, u32[]{:S(2)}) collective-permute-start(bf16[120,128]{1,0:T(8,128)(2,1)S(1)} %fusion.2), channel_id=1, source_target_pairs={{0,8},{1,9},{2,10},{3,11},{4,12},{5,13},{6,14},{7,15},{8,0},{9,1},... | collective-permute-start | bytes 92168 | tf_op jit(solution)/shard_map/ppermute | solution.py:704

commit v3 on v2

--- a/solution.py
+++ b/solution.py
@@ -298,10 +298,11 @@
         (table_hbm.at[pl.ds(S_STEP * STEPS_A, S_PAD - S_STEP * STEPS_A)], rest_ref),
     ]
     copies = [pltpu.make_async_copy(a, b, sems.at[i]) for i, (a, b) in enumerate(moves)]
-    for copy in copies:
+    for copy in copies[:8]:
         copy.start()
     for copy in copies[:7]:
         copy.wait()
+    copies[8].start()
     noise_ref[...] = jnp.dot(
         sig_ref[...], exp_ref[...], precision=lax.Precision.HIGHEST, preferred_element_type=F32
     )
@@ -431,7 +432,7 @@
 
 
 def posterior_kernel(
-    direct, near_ref, rest_ref, near1_ref, rest1_ref, fh_ref, fl_ref, mt_ref,
+    direct, r0_ref, r1_ref, r2_ref, r3_ref, s0_ref, s1_ref, s2_ref, s3_ref, fh_ref, fl_ref, mt_ref,
     out_ref, x_ref, d_ref, a_ref, e_ref, ca_ref, cb_ref, ct_ref, sa_ref, sb_ref, st_ref,
     pa_ref, pb_ref, pt_ref, q_ref, num_ref,
 ):
@@ -441,12 +442,11 @@
 
     me = lax.axis_index("img") if direct else 0
     blank = jnp.zeros((KPAD - CLASSES, BLOCK_COLS), BF)
-    for side, refs in enumerate(((near_ref, rest_ref), (near1_ref, rest1_ref))):
-        for entry in range(BLOCKS // 2):
-            values = refs[0][entry] if entry < 2 else refs[1][entry - 2]
-            block = me ^ (2 * (entry // 2) + 8 * (entry % 2) + side)
-            row = pl.multiple_of(block * KPAD, KPAD)
-            x_ref[pl.ds(row, KPAD), :] = jnp.concatenate([values, blank], axis=0)
+    for side, refs in enumerate(((r0_ref, r1_ref, r2_ref, r3_ref), (s0_ref, s1_ref, s2_ref, s3_ref))):
+        for g, pair in enumerate(refs):
+            for h in range(2):
+                row = pl.multiple_of((me ^ (2 * g + 8 * h + side)) * KPAD, KPAD)
+                x_ref[pl.ds(row, KPAD), :] = jnp.concatenate([pair[h], blank], axis=0)
     x = x_ref[...]
     d_ref[...] = nt(mt_ref[0], x) + nt(mt_ref[1], x)
 
@@ -637,7 +637,7 @@
     return pl.pallas_call(
         functools.partial(posterior_kernel, direct),
         out_shape=jax.ShapeDtypeStruct((2, BLOCKS // 2, PAY, LANES), BF),
-        in_specs=[VM] * 7,
+        in_specs=[VM] * 11,
         out_specs=VM,
         scratch_shapes=[
             pltpu.VMEM((BLOCKS * KPAD, BLOCK_COLS), BF),
@@ -724,9 +724,7 @@
     else:
         whole = lax.all_gather(class_refs, "img", axis=1, tiled=True)
         blocks = whole.reshape(CLASSES, BLOCKS, BLOCK_COLS).transpose(1, 0, 2)
-        order = [2 * (e // 2) + 8 * (e % 2) for e in range(BLOCKS // 2)]
-        sides = [jnp.stack([blocks[m + side] for m in order]) for side in range(2)]
-        refs = [part for side in sides for part in (side[:2], side[2:])]
+        refs = [jnp.stack([blocks[2 * g + s], blocks[2 * g + s + 8]]) for s in range(2) for g in range(4)]
     pay = None
     for first in range(0, images.shape[0], ROWS8):
         part = slice(first, first + ROWS8)
@@ -739,9 +737,12 @@
             rest = [swap(near, 2 * g) for g in (1, 2, 3)]
         hi, lo, mt, back = second_features(hi, lo, table, pix, slot)
         if direct and first == 0:
-            rest, hi = lax.optimization_barrier((rest, hi))
-            rest = jnp.concatenate(rest)
-            refs = [near, rest, swap(near, 1), swap(rest, 1)]
+            other = [swap(near, 1)]
+            other[0], hi = lax.optimization_barrier((other[0], hi))
+            for g in range(3):
+                rest[g], hi = lax.optimization_barrier((rest[g], hi))
+                other.append(swap(rest[g], 1))
+            refs = [near] + rest + other
         one = make_payload(direct, refs, hi, lo, mt)
         pay = one if pay is None else pay + one
     if direct:

time: 39.6 us -> 39.4 us (level)
  waiting for transfers between devices: 9.76 us -> 9.36 us
  Pallas kernels: 14.8 us -> 15.2 us
    ppermute x11 -> x13, waiting for transfers between devices: 9.76 us -> 9.36 us  [swap(): return lax.ppermute(value, 'img', pairs)]
    ppermute x11 -> x13, starting transfers between devices: 14.5 us -> 14.5 us  [swap(): return lax.ppermute(value, 'img', pairs)]
  transfers between devices with their start and end apart: 11 -> 13, of which waited for: 7 -> 9; matrix products, arithmetic and copies ran while one was open for 0% -> 0% of each run, Pallas kernels for 16% -> 17%
where the time goes in v3:
time: 39.4 us; the launch traced here: 39.3 us
  Pallas kernels  15.2 us (39%)
  starting transfers between devices  14.5 us (37%)
  waiting for transfers between devices  9.36 us (24%)
    ppermute x13, starting transfers between devices, swap(): return lax.ppermute(value, 'img', pairs)  14.5 us
    ppermute x13, waiting for transfers between devices, swap(): return lax.ppermute(value, 'img', pairs)  9.36 us
    pallas_call x1, Pallas kernels, make_payload(): pl.pallas_call(functools.partial(posterior_kernel, direct), out_shape=jax...  7.48 us
    pallas_call x1, Pallas kernels, second_features(): pl.pallas_call(second_kernel, out_shape=(jax.ShapeDtypeStruct(hi.shape, B...  3.75 us
    pallas_call x1, Pallas kernels, first_features(): pl.pallas_call(first_kernel, out_shape=(jax.ShapeDtypeStruct(feat, BF), j...  2.85 us
    pallas_call x1, Pallas kernels, finish(): pl.pallas_call(final_kernel, out_shape=jax.ShapeDtypeStruct((CLASSES, BLO...  1.08 us
  transfers between devices with their start and end apart: 13, of which 9 were waited for; matrix products, arithmetic and copies ran while one was open for 0% of the time, Pallas kernels for 17%

profile of v3, /device:TPU:0, one launch (start us, length us, event | category | flops | bytes accessed | tf_op | source)
XLA Modules:
  0.0 39.3 jit_solution(18261228425033779926)
XLA Ops:
  0.0 0.0 copy-start
  0.0 4.0 %collective-permute-start = (bf16[48,288]{1,0:T(8,128)(2,1)}, bf16[48,288]{1,0:T(8,128)(2,1)S(1)}, u32[]{:S(2)}, u32[]{:S(2)}) collective-permute-start(bf16[48,288]{1,0:T(8,128)(2,1)} %param.12), channel_id=1, source_target_pairs={{0,8},{1,9},{2,10},{3,11},{4,12},{5,13},{6,14},{7,15},{8,0},{9,1},... | collective-permute-start | bytes 82952 | tf_op jit(solution)/shard_map/ppermute | solution.py:704
  4.0 2.8 %features_first.1 = (bf16[19,416,256]{2,1,0:T(8,128)(2,1)S(1)}, f8e5m2[19,416,256]{2,1,0:T(32,128)(4,1)S(1)}, f32[2,36,8,128]{3,2,1,0:T(8,128)S(1)}, f32[8,128]{1,0:T(8,128)S(1)}, f32[40,72,128]{2,1,0:T(8,128)S(1)}) custom-call(s32[8]{0:T(128)} %grp_hbm.1, s32[8]{0:T(128)} %bin_hbm.1, bf16[8,4608]{1,0:T(8,128)(2,1)} %img_hbm.1, f32[16,16]{1,0:T(8,128)} %sig_hbm.1, ...), custom_call_target="tpu_custom_call" | custom-call | flops 4499999744 | bytes 13500000 | tf_op jit(solution)/shard_map/features_first/pallas_call | solution.py:377
  6.9 0.0 collective-permute-done
  6.9 0.0 copy-done
  6.9 0.1 collective-permute-start.2
  7.0 1.6 %collective-permute-start.1 = (bf16[2,48,288]{2,1,0:T(8,128)(2,1)S(1)}, bf16[2,48,288]{2,1,0:T(8,128)(2,1)S(1)}, u32[]{:S(2)}, u32[]{:S(2)}) collective-permute-start(bf16[2,48,288]{2,1,0:T(8,128)(2,1)S(1)} %pad_maximum_fusion.r0_ref), channel_id=1, source_target_pairs={{0,2},{1,3},{2,0},{3,1},{4,6},{5,7},{6,4},{7,5},{8,10},{9,11},{10,... | collective-permute-start | bytes 165896 | tf_op jit(solution)/shard_map/ppermute | solution.py:704
  8.6 1.6 %collective-permute-start.3 = (bf16[2,48,288]{2,1,0:T(8,128)(2,1)S(1)}, bf16[2,48,288]{2,1,0:T(8,128)(2,1)S(1)}, u32[]{:S(2)}, u32[]{:S(2)}) collective-permute-start(bf16[2,48,288]{2,1,0:T(8,128)(2,1)S(1)} %pad_maximum_fusion.r0_ref), channel_id=1, source_target_pairs={{0,4},{1,5},{2,6},{3,7},{4,0},{5,1},{6,2},{7,3},{8,12},{9,13},{10,... | collective-permute-start | bytes 165896 | tf_op jit(solution)/shard_map/ppermute | solution.py:704
  10.2 0.4 %collective-permute-start.4 = (bf16[2,48,288]{2,1,0:T(8,128)(2,1)S(1)}, bf16[2,48,288]{2,1,0:T(8,128)(2,1)S(1)}, u32[]{:S(2)}, u32[]{:S(2)}) collective-permute-start(bf16[2,48,288]{2,1,0:T(8,128)(2,1)S(1)} %pad_maximum_fusion.r0_ref), channel_id=1, source_target_pairs={{0,6},{1,7},{2,4},{3,5},{4,2},{5,3},{6,0},{7,1},{8,14},{9,15},{10,... | collective-permute-start | bytes 165896 | tf_op jit(solution)/shard_map/ppermute | solution.py:704
  10.6 3.8 %features_second.1 = (bf16[19,416,256]{2,1,0:T(8,128)(2,1)S(1)}, f8e5m2[19,416,256]{2,1,0:T(32,128)(4,1)S(1)}, bf16[2,304,288]{2,1,0:T(8,128)(2,1)S(1)}, bf16[4,160,288]{2,1,0:T(8,128)(2,1)S(1)}) custom-call(bf16[19,416,256]{2,1,0:T(8,128)(2,1)S(1)} %get-tuple-element.26.fh_in, ...), custom_call_target="tpu_custom_call", output_to_operand_aliasing={{0}: (0, {}), {1}: (1, {})} | custom-call | flops 2500000000 | bytes 7500000 | tf_op jit(solution)/shard_map/features_second/pallas_call | solution.py:412
  14.3 0.0 collective-permute-done.2.s0_ref
  14.3 0.0 collective-permute-done.1.r1_ref
  14.4 0.0 collective-permute-done.3.r2_ref
  14.4 1.1 %collective-permute-done.4.r3_ref = bf16[2,48,288]{2,1,0:T(8,128)(2,1)S(1)} collective-permute-done((bf16[2,48,288]{2,1,0:T(8,128)(2,1)S(1)}, bf16[2,48,288]{2,1,0:T(8,128)(2,1)S(1)}, u32[]{:S(2)}, u32[]{:S(2)}) %collective-permute-start.4) | collective-permute-done | bytes 55328 | tf_op jit(solution)/shard_map/ppermute | solution.py:704
  15.4 0.0 collective-permute-start.7
  15.4 0.5 %collective-permute-start.6 = (bf16[2,48,288]{2,1,0:T(8,128)(2,1)S(1)}, bf16[2,48,288]{2,1,0:T(8,128)(2,1)S(1)}, u32[]{:S(2)}, u32[]{:S(2)}) collective-permute-start(bf16[2,48,288]{2,1,0:T(8,128)(2,1)S(1)} %collective-permute-done.3.r2_ref), channel_id=1, source_target_pairs={{0,1},{1,0},{2,3},{3,2},{4,5},{5,4},{6,7},{7,6},{8,9},{9,8},{10,11... | collective-permute-start | bytes 165896 | tf_op jit(solution)/shard_map/ppermute | solution.py:704
  15.9 0.0 collective-permute-start.5
  15.9 0.8 %collective-permute-done.7.s3_ref = bf16[2,48,288]{2,1,0:T(8,128)(2,1)S(1)} collective-permute-done((bf16[2,48,288]{2,1,0:T(8,128)(2,1)S(1)}, bf16[2,48,288]{2,1,0:T(8,128)(2,1)S(1)}, u32[]{:S(2)}, u32[]{:S(2)}) %collective-permute-start.7) | collective-permute-done | bytes 55328 | tf_op jit(solution)/shard_map/ppermute | solution.py:704
  16.7 0.2 collective-permute-done.6.s2_ref
  16.9 0.4 collective-permute-done.5.s1_ref
  17.2 7.5 %posterior.1 = bf16[2,8,120,128]{3,2,1,0:T(8,128)(2,1)S(1)} custom-call(bf16[2,48,288]{2,1,0:T(8,128)(2,1)S(1)} %pad_maximum_fusion.r0_ref, bf16[2,48,288]{2,1,0:T(8,128)(2,1)S(1)} %collective-permute-done.1.r1_ref, bf16[2,48,288]{2,1,0:T(8,128)(2,1)S(1)} %collective-permute-done.3.r2_ref, bf16[2,48,288]{2,1,0:T(8,128)(2,1)S(1)} %collective-permute-done.4.r3_ref, ...), custom_call_target="tpu_custom_call" | custom-call | flops 10000000000 | bytes 30000000 | tf_op jit(solution)/shard_map/posterior/pallas_call | solution.py:637
  24.7 0.2 collective-permute-start.8
  24.9 1.4 %collective-permute-done.8 = bf16[8,120,128]{2,1,0:T(8,128)(2,1)S(1)} collective-permute-done((bf16[8,120,128]{2,1,0:T(8,128)(2,1)S(1)}, bf16[8,120,128]{2,1,0:T(8,128)(2,1)S(1)}, u32[]{:S(2)}, u32[]{:S(2)}) %collective-permute-start.8) | collective-permute-done | bytes 245792 | tf_op jit(solution)/shard_map/ppermute | solution.py:704
  26.3 0.1 fusion.3
  26.4 0.7 %collective-permute-start.10 = (bf16[2,120,128]{2,1,0:T(8,128)(2,1)S(1)}, bf16[2,120,128]{2,1,0:T(8,128)(2,1)S(1)}, u32[]{:S(2)}, u32[]{:S(2)}) collective-permute-start(bf16[2,120,128]{2,1,0:T(8,128)(2,1)S(1)} %get-tuple-element.47), channel_id=1, source_target_pairs={{0,4},{1,5},{2,6},{3,7},{4,0},{5,1},{6,2},{7,3},{8,12},{9,13},{10,... | collective-permute-start | bytes 184328 | tf_op jit(solution)/shard_map/ppermute | solution.py:704
  27.1 1.4 %collective-permute-start.11 = (bf16[2,120,128]{2,1,0:T(8,128)(2,1)S(1)}, bf16[2,120,128]{2,1,0:T(8,128)(2,1)S(1)}, u32[]{:S(2)}, u32[]{:S(2)}) collective-permute-start(bf16[2,120,128]{2,1,0:T(8,128)(2,1)S(1)} %get-tuple-element.46), channel_id=1, source_target_pairs={{0,6},{1,7},{2,4},{3,5},{4,2},{5,3},{6,0},{7,1},{8,14},{9,15},{10,... | collective-permute-start | bytes 184328 | tf_op jit(solution)/shard_map/ppermute | solution.py:704
  28.5 1.5 %collective-permute-start.9 = (bf16[2,120,128]{2,1,0:T(8,128)(2,1)S(1)}, bf16[2,120,128]{2,1,0:T(8,128)(2,1)S(1)}, u32[]{:S(2)}, u32[]{:S(2)}) collective-permute-start(bf16[2,120,128]{2,1,0:T(8,128)(2,1)S(1)} %get-tuple-element.45), channel_id=1, source_target_pairs={{0,2},{1,3},{2,0},{3,1},{4,6},{5,7},{6,4},{7,5},{8,10},{9,11},{10,... | collective-permute-start | bytes 184328 | tf_op jit(solution)/shard_map/ppermute | solution.py:704
  30.0 1.0 %collective-permute-done.10 = bf16[2,120,128]{2,1,0:T(8,128)(2,1)S(1)} collective-permute-done((bf16[2,120,128]{2,1,0:T(8,128)(2,1)S(1)}, bf16[2,120,128]{2,1,0:T(8,128)(2,1)S(1)}, u32[]{:S(2)}, u32[]{:S(2)}) %collective-permute-start.10) | collective-permute-done | bytes 61472 | tf_op jit(solution)/shard_map/ppermute | solution.py:704
  30.9 1.3 %collective-permute-done.11 = bf16[2,120,128]{2,1,0:T(8,128)(2,1)S(1)} collective-permute-done((bf16[2,120,128]{2,1,0:T(8,128)(2,1)S(1)}, bf16[2,120,128]{2,1,0:T(8,128)(2,1)S(1)}, u32[]{:S(2)}, u32[]{:S(2)}) %collective-permute-start.11) | collective-permute-done | bytes 61472 | tf_op jit(solution)/shard_map/ppermute | solution.py:704
  32.3 0.9 %collective-permute-done.9 = bf16[2,120,128]{2,1,0:T(8,128)(2,1)S(1)} collective-permute-done((bf16[2,120,128]{2,1,0:T(8,128)(2,1)S(1)}, bf16[2,120,128]{2,1,0:T(8,128)(2,1)S(1)}, u32[]{:S(2)}, u32[]{:S(2)}) %collective-permute-start.9) | collective-permute-done | bytes 61472 | tf_op jit(solution)/shard_map/ppermute | solution.py:704
  33.2 2.5 %collective-permute-start.12 = (bf16[120,128]{1,0:T(8,128)(2,1)S(1)}, bf16[120,128]{1,0:T(8,128)(2,1)S(1)}, u32[]{:S(2)}, u32[]{:S(2)}) collective-permute-start(bf16[120,128]{1,0:T(8,128)(2,1)S(1)} %fusion.2), channel_id=1, source_target_pairs={{0,8},{1,9},{2,10},{3,11},{4,12},{5,13},{6,14},{7,15},{8,0},{9,1},... | collective-permute-start | bytes 92168 | tf_op jit(solution)/shard_map/ppermute | solution.py:704
  35.7 2.5 %collective-permute-done.12.got_ref = bf16[120,128]{1,0:T(8,128)(2,1)S(1)} collective-permute-done((bf16[120,128]{1,0:T(8,128)(2,1)S(1)}, bf16[120,128]{1,0:T(8,128)(2,1)S(1)}, u32[]{:S(2)}, u32[]{:S(2)}) %collective-permute-start.12) | collective-permute-done | bytes 30752 | tf_op jit(solution)/shard_map/ppermute | solution.py:704
  38.2 1.1 %finish.1 = f32[48,288]{1,0:T(8,128)} custom-call(f32[120,128]{1,0:T(8,128)S(1)} %slice_bitcast_fusion.2.keep_ref, bf16[120,128]{1,0:T(8,128)(2,1)S(1)} %collective-permute-done.12.got_ref, bf16[4,160,288]{2,1,0:T(8,128)(2,1)S(1)} %get-tuple-element.42.back_ref), custom_call_target="tpu_custom_call" | custom-call | flops 1000000000 | bytes 3000000 | tf_op jit(solution)/shard_map/finish/pallas_call | solution.py:691
  (6 shorter events, 0.1 us)
Async XLA Ops:
  0.0 6.9 %copy-start = (bf16[48,288]{1,0:T(8,128)(2,1)S(1)}, bf16[48,288]{1,0:T(8,128)(2,1)}, u32[]{:S(2)}) copy-start(bf16[48,288]{1,0:T(8,128)(2,1)} %param.12) | copy-start | bytes 82948
  0.0 6.9 %collective-permute-start = (bf16[48,288]{1,0:T(8,128)(2,1)}, bf16[48,288]{1,0:T(8,128)(2,1)S(1)}, u32[]{:S(2)}, u32[]{:S(2)}) collective-permute-start(bf16[48,288]{1,0:T(8,128)(2,1)} %param.12), channel_id=1, source_target_pairs={{0,8},{1,9},{2,10},{3,11},{4,12},{5,13},{6,14},{7,15},{8,0},{9,1},... | collective-permute-start | bytes 82952 | tf_op jit(solution)/shard_map/ppermute | solution.py:704
  6.9 7.4 %collective-permute-start.2 = (bf16[2,48,288]{2,1,0:T(8,128)(2,1)S(1)}, bf16[2,48,288]{2,1,0:T(8,128)(2,1)S(1)}, u32[]{:S(2)}, u32[]{:S(2)}) collective-permute-start(bf16[2,48,288]{2,1,0:T(8,128)(2,1)S(1)} %pad_maximum_fusion.r0_ref), channel_id=1, source_target_pairs={{0,1},{1,0},{2,3},{3,2},{4,5},{5,4},{6,7},{7,6},{8,9},{9,8},{10,11... | collective-permute-start | bytes 165896 | tf_op jit(solution)/shard_map/ppermute | solution.py:704
  7.0 7.3 %collective-permute-start.1 = (bf16[2,48,288]{2,1,0:T(8,128)(2,1)S(1)}, bf16[2,48,288]{2,1,0:T(8,128)(2,1)S(1)}, u32[]{:S(2)}, u32[]{:S(2)}) collective-permute-start(bf16[2,48,288]{2,1,0:T(8,128)(2,1)S(1)} %pad_maximum_fusion.r0_ref), channel_id=1, source_target_pairs={{0,2},{1,3},{2,0},{3,1},{4,6},{5,7},{6,4},{7,5},{8,10},{9,11},{10,... | collective-permute-start | bytes 165896 | tf_op jit(solution)/shard_map/ppermute | solution.py:704
  8.6 5.8 %collective-permute-start.3 = (bf16[2,48,288]{2,1,0:T(8,128)(2,1)S(1)}, bf16[2,48,288]{2,1,0:T(8,128)(2,1)S(1)}, u32[]{:S(2)}, u32[]{:S(2)}) collective-permute-start(bf16[2,48,288]{2,1,0:T(8,128)(2,1)S(1)} %pad_maximum_fusion.r0_ref), channel_id=1, source_target_pairs={{0,4},{1,5},{2,6},{3,7},{4,0},{5,1},{6,2},{7,3},{8,12},{9,13},{10,... | collective-permute-start | bytes 165896 | tf_op jit(solution)/shard_map/ppermute | solution.py:704
  10.2 5.3 %collective-permute-start.4 = (bf16[2,48,288]{2,1,0:T(8,128)(2,1)S(1)}, bf16[2,48,288]{2,1,0:T(8,128)(2,1)S(1)}, u32[]{:S(2)}, u32[]{:S(2)}) collective-permute-start(bf16[2,48,288]{2,1,0:T(8,128)(2,1)S(1)} %pad_maximum_fusion.r0_ref), channel_id=1, source_target_pairs={{0,6},{1,7},{2,4},{3,5},{4,2},{5,3},{6,0},{7,1},{8,14},{9,15},{10,... | collective-permute-start | bytes 165896 | tf_op jit(solution)/shard_map/ppermute | solution.py:704
  15.4 1.3 %collective-permute-start.7 = (bf16[2,48,288]{2,1,0:T(8,128)(2,1)S(1)}, bf16[2,48,288]{2,1,0:T(8,128)(2,1)S(1)}, u32[]{:S(2)}, u32[]{:S(2)}) collective-permute-start(bf16[2,48,288]{2,1,0:T(8,128)(2,1)S(1)} %collective-permute-done.4.r3_ref), channel_id=1, source_target_pairs={{0,1},{1,0},{2,3},{3,2},{4,5},{5,4},{6,7},{7,6},{8,9},{9,8},{10,11... | collective-permute-start | bytes 165896 | tf_op jit(solution)/shard_map/ppermute | solution.py:704
  15.4 1.4 %collective-permute-start.6 = (bf16[2,48,288]{2,1,0:T(8,128)(2,1)S(1)}, bf16[2,48,288]{2,1,0:T(8,128)(2,1)S(1)}, u32[]{:S(2)}, u32[]{:S(2)}) collective-permute-start(bf16[2,48,288]{2,1,0:T(8,128)(2,1)S(1)} %collective-permute-done.3.r2_ref), channel_id=1, source_target_pairs={{0,1},{1,0},{2,3},{3,2},{4,5},{5,4},{6,7},{7,6},{8,9},{9,8},{10,11... | collective-permute-start | bytes 165896 | tf_op jit(solution)/shard_map/ppermute | solution.py:704
  15.9 1.3 %collective-permute-start.5 = (bf16[2,48,288]{2,1,0:T(8,128)(2,1)S(1)}, bf16[2,48,288]{2,1,0:T(8,128)(2,1)S(1)}, u32[]{:S(2)}, u32[]{:S(2)}) collective-permute-start(bf16[2,48,288]{2,1,0:T(8,128)(2,1)S(1)} %collective-permute-done.1.r1_ref), channel_id=1, source_target_pairs={{0,1},{1,0},{2,3},{3,2},{4,5},{5,4},{6,7},{7,6},{8,9},{9,8},{10,11... | collective-permute-start | bytes 165896 | tf_op jit(solution)/shard_map/ppermute | solution.py:704
  24.7 1.6 %collective-permute-start.8 = (bf16[8,120,128]{2,1,0:T(8,128)(2,1)S(1)}, bf16[8,120,128]{2,1,0:T(8,128)(2,1)S(1)}, u32[]{:S(2)}, u32[]{:S(2)}) collective-permute-start(bf16[8,120,128]{2,1,0:T(8,128)(2,1)S(1)} %slice_bitcast_fusion), channel_id=1, source_target_pairs={{0,1},{1,0},{2,3},{3,2},{4,5},{5,4},{6,7},{7,6},{8,9},{9,8},{10,11... | collective-permute-start | bytes 737288 | tf_op jit(solution)/shard_map/ppermute | solution.py:704
  26.4 4.5 %collective-permute-start.10 = (bf16[2,120,128]{2,1,0:T(8,128)(2,1)S(1)}, bf16[2,120,128]{2,1,0:T(8,128)(2,1)S(1)}, u32[]{:S(2)}, u32[]{:S(2)}) collective-permute-start(bf16[2,120,128]{2,1,0:T(8,128)(2,1)S(1)} %get-tuple-element.47), channel_id=1, source_target_pairs={{0,4},{1,5},{2,6},{3,7},{4,0},{5,1},{6,2},{7,3},{8,12},{9,13},{10,... | collective-permute-start | bytes 184328 | tf_op jit(solution)/shard_map/ppermute | solution.py:704
  27.1 5.2 %collective-permute-start.11 = (bf16[2,120,128]{2,1,0:T(8,128)(2,1)S(1)}, bf16[2,120,128]{2,1,0:T(8,128)(2,1)S(1)}, u32[]{:S(2)}, u32[]{:S(2)}) collective-permute-start(bf16[2,120,128]{2,1,0:T(8,128)(2,1)S(1)} %get-tuple-element.46), channel_id=1, source_target_pairs={{0,6},{1,7},{2,4},{3,5},{4,2},{5,3},{6,0},{7,1},{8,14},{9,15},{10,... | collective-permute-start | bytes 184328 | tf_op jit(solution)/shard_map/ppermute | solution.py:704
  28.5 4.7 %collective-permute-start.9 = (bf16[2,120,128]{2,1,0:T(8,128)(2,1)S(1)}, bf16[2,120,128]{2,1,0:T(8,128)(2,1)S(1)}, u32[]{:S(2)}, u32[]{:S(2)}) collective-permute-start(bf16[2,120,128]{2,1,0:T(8,128)(2,1)S(1)} %get-tuple-element.45), channel_id=1, source_target_pairs={{0,2},{1,3},{2,0},{3,1},{4,6},{5,7},{6,4},{7,5},{8,10},{9,11},{10,... | collective-permute-start | bytes 184328 | tf_op jit(solution)/shard_map/ppermute | solution.py:704
  33.2 5.0 %collective-permute-start.12 = (bf16[120,128]{1,0:T(8,128)(2,1)S(1)}, bf16[120,128]{1,0:T(8,128)(2,1)S(1)}, u32[]{:S(2)}, u32[]{:S(2)}) collective-permute-start(bf16[120,128]{1,0:T(8,128)(2,1)S(1)} %fusion.2), channel_id=1, source_target_pairs={{0,8},{1,9},{2,10},{3,11},{4,12},{5,13},{6,14},{7,15},{8,0},{9,1},... | collective-permute-start | bytes 92168 | tf_op jit(solution)/shard_map/ppermute | solution.py:704

commit v4 on v3

--- a/solution.py
+++ b/solution.py
@@ -560,27 +560,20 @@
     operand(0)
     for q in range(FREQS):
         cross_first(q)
+        cross_second(q)
     tiles_a = tiles_of(ca_ref, sa_ref, pa_ref)
-    top_a = total_a = None
-    todo = list(range(FREQS))
-    for step, where in enumerate(tiles_a):
-        top_a = to_scores(where, top_a)
-        while todo and todo[0] * 2 * len(tiles_a) < (step + 1) * FREQS:
-            cross_second(todo.pop(0))
-    top_a = fold(top_a, jnp.maximum)
-    for step, where in enumerate(tiles_a):
-        total_a = to_posterior(where, top_a, total_a)
-        while todo and todo[0] * 2 * len(tiles_a) < (len(tiles_a) + step + 1) * FREQS:
-            cross_second(todo.pop(0))
-    for q in todo:
-        cross_second(q)
     tiles_b = tiles_of(cb_ref, sb_ref, pb_ref) + tiles_of(ct_ref, st_ref, pt_ref)
-    top_b = total_b = None
+    top_a = total_a = top_b = total_b = None
     for where in tiles_b:
         top_b = to_scores(where, top_b)
     top_b = fold(top_b, jnp.maximum)
     for where in tiles_b:
         total_b = to_posterior(where, top_b, total_b)
+    for where in tiles_a:
+        top_a = to_scores(where, top_a)
+    top_a = fold(top_a, jnp.maximum)
+    for where in tiles_a:
+        total_a = to_posterior(where, top_a, total_a)
     top = jnp.maximum(top_a, top_b)
     part_a, part_b = jnp.exp(top_a - top), jnp.exp(top_b - top)
     inverse = 1.0 / (part_a * fold(total_a, jnp.add) + part_b * fold(total_b, jnp.add))

time: 39.4 us -> 39.3 us (level)
  no operation moved by 1% of the time
where the time goes in v4:
time: 39.3 us; the launch traced here: 39.1 us
  Pallas kernels  15 us (38%)
  starting transfers between devices  14.5 us (37%)
  waiting for transfers between devices  9.37 us (24%)
    ppermute x13, starting transfers between devices, swap(): return lax.ppermute(value, 'img', pairs)  14.5 us
    ppermute x13, waiting for transfers between devices, swap(): return lax.ppermute(value, 'img', pairs)  9.37 us
    pallas_call x1, Pallas kernels, make_payload(): pl.pallas_call(functools.partial(posterior_kernel, direct), out_shape=jax...  7.31 us
    pallas_call x1, Pallas kernels, second_features(): pl.pallas_call(second_kernel, out_shape=(jax.ShapeDtypeStruct(hi.shape, B...  3.75 us
    pallas_call x1, Pallas kernels, first_features(): pl.pallas_call(first_kernel, out_shape=(jax.ShapeDtypeStruct(feat, BF), j...  2.84 us
    pallas_call x1, Pallas kernels, finish(): pl.pallas_call(final_kernel, out_shape=jax.ShapeDtypeStruct((CLASSES, BLO...  1.1 us
  transfers between devices with their start and end apart: 13, of which 9 were waited for; matrix products, arithmetic and copies ran while one was open for 0% of the time, Pallas kernels for 17%

profile of v4, /device:TPU:0, one launch (start us, length us, event | category | flops | bytes accessed | tf_op | source)
XLA Modules:
  0.0 39.1 jit_solution(9941184840155922331)
XLA Ops:
  0.0 0.0 copy-start
  0.0 4.0 %collective-permute-start = (bf16[48,288]{1,0:T(8,128)(2,1)}, bf16[48,288]{1,0:T(8,128)(2,1)S(1)}, u32[]{:S(2)}, u32[]{:S(2)}) collective-permute-start(bf16[48,288]{1,0:T(8,128)(2,1)} %param.12), channel_id=1, source_target_pairs={{0,8},{1,9},{2,10},{3,11},{4,12},{5,13},{6,14},{7,15},{8,0},{9,1},... | collective-permute-start | bytes 82952 | tf_op jit(solution)/shard_map/ppermute | solution.py:697
  4.0 2.8 %features_first.1 = (bf16[19,416,256]{2,1,0:T(8,128)(2,1)S(1)}, f8e5m2[19,416,256]{2,1,0:T(32,128)(4,1)S(1)}, f32[2,36,8,128]{3,2,1,0:T(8,128)S(1)}, f32[8,128]{1,0:T(8,128)S(1)}, f32[40,72,128]{2,1,0:T(8,128)S(1)}) custom-call(s32[8]{0:T(128)} %grp_hbm.1, s32[8]{0:T(128)} %bin_hbm.1, bf16[8,4608]{1,0:T(8,128)(2,1)} %img_hbm.1, f32[16,16]{1,0:T(8,128)} %sig_hbm.1, ...), custom_call_target="tpu_custom_call" | custom-call | flops 4499999744 | bytes 13500000 | tf_op jit(solution)/shard_map/features_first/pallas_call | solution.py:377
  6.9 0.0 collective-permute-done
  6.9 0.0 copy-done
  6.9 0.1 collective-permute-start.2
  7.0 1.6 %collective-permute-start.1 = (bf16[2,48,288]{2,1,0:T(8,128)(2,1)S(1)}, bf16[2,48,288]{2,1,0:T(8,128)(2,1)S(1)}, u32[]{:S(2)}, u32[]{:S(2)}) collective-permute-start(bf16[2,48,288]{2,1,0:T(8,128)(2,1)S(1)} %pad_maximum_fusion.r0_ref), channel_id=1, source_target_pairs={{0,2},{1,3},{2,0},{3,1},{4,6},{5,7},{6,4},{7,5},{8,10},{9,11},{10,... | collective-permute-start | bytes 165896 | tf_op jit(solution)/shard_map/ppermute | solution.py:697
  8.6 1.6 %collective-permute-start.3 = (bf16[2,48,288]{2,1,0:T(8,128)(2,1)S(1)}, bf16[2,48,288]{2,1,0:T(8,128)(2,1)S(1)}, u32[]{:S(2)}, u32[]{:S(2)}) collective-permute-start(bf16[2,48,288]{2,1,0:T(8,128)(2,1)S(1)} %pad_maximum_fusion.r0_ref), channel_id=1, source_target_pairs={{0,4},{1,5},{2,6},{3,7},{4,0},{5,1},{6,2},{7,3},{8,12},{9,13},{10,... | collective-permute-start | bytes 165896 | tf_op jit(solution)/shard_map/ppermute | solution.py:697
  10.2 0.4 %collective-permute-start.4 = (bf16[2,48,288]{2,1,0:T(8,128)(2,1)S(1)}, bf16[2,48,288]{2,1,0:T(8,128)(2,1)S(1)}, u32[]{:S(2)}, u32[]{:S(2)}) collective-permute-start(bf16[2,48,288]{2,1,0:T(8,128)(2,1)S(1)} %pad_maximum_fusion.r0_ref), channel_id=1, source_target_pairs={{0,6},{1,7},{2,4},{3,5},{4,2},{5,3},{6,0},{7,1},{8,14},{9,15},{10,... | collective-permute-start | bytes 165896 | tf_op jit(solution)/shard_map/ppermute | solution.py:697
  10.6 3.8 %features_second.1 = (bf16[19,416,256]{2,1,0:T(8,128)(2,1)S(1)}, f8e5m2[19,416,256]{2,1,0:T(32,128)(4,1)S(1)}, bf16[2,304,288]{2,1,0:T(8,128)(2,1)S(1)}, bf16[4,160,288]{2,1,0:T(8,128)(2,1)S(1)}) custom-call(bf16[19,416,256]{2,1,0:T(8,128)(2,1)S(1)} %get-tuple-element.26.fh_in, ...), custom_call_target="tpu_custom_call", output_to_operand_aliasing={{0}: (0, {}), {1}: (1, {})} | custom-call | flops 2500000000 | bytes 7500000 | tf_op jit(solution)/shard_map/features_second/pallas_call | solution.py:412
  14.3 0.0 collective-permute-done.2.s0_ref
  14.3 0.0 collective-permute-done.1.r1_ref
  14.4 0.0 collective-permute-done.3.r2_ref
  14.4 1.1 %collective-permute-done.4.r3_ref = bf16[2,48,288]{2,1,0:T(8,128)(2,1)S(1)} collective-permute-done((bf16[2,48,288]{2,1,0:T(8,128)(2,1)S(1)}, bf16[2,48,288]{2,1,0:T(8,128)(2,1)S(1)}, u32[]{:S(2)}, u32[]{:S(2)}) %collective-permute-start.4) | collective-permute-done | bytes 55328 | tf_op jit(solution)/shard_map/ppermute | solution.py:697
  15.4 0.0 collective-permute-start.7
  15.4 0.5 %collective-permute-start.6 = (bf16[2,48,288]{2,1,0:T(8,128)(2,1)S(1)}, bf16[2,48,288]{2,1,0:T(8,128)(2,1)S(1)}, u32[]{:S(2)}, u32[]{:S(2)}) collective-permute-start(bf16[2,48,288]{2,1,0:T(8,128)(2,1)S(1)} %collective-permute-done.3.r2_ref), channel_id=1, source_target_pairs={{0,1},{1,0},{2,3},{3,2},{4,5},{5,4},{6,7},{7,6},{8,9},{9,8},{10,11... | collective-permute-start | bytes 165896 | tf_op jit(solution)/shard_map/ppermute | solution.py:697
  15.9 0.0 collective-permute-start.5
  15.9 0.8 %collective-permute-done.7.s3_ref = bf16[2,48,288]{2,1,0:T(8,128)(2,1)S(1)} collective-permute-done((bf16[2,48,288]{2,1,0:T(8,128)(2,1)S(1)}, bf16[2,48,288]{2,1,0:T(8,128)(2,1)S(1)}, u32[]{:S(2)}, u32[]{:S(2)}) %collective-permute-start.7) | collective-permute-done | bytes 55328 | tf_op jit(solution)/shard_map/ppermute | solution.py:697
  16.7 0.2 collective-permute-done.6.s2_ref
  16.9 0.4 collective-permute-done.5.s1_ref
  17.2 7.3 %posterior.1 = bf16[2,8,120,128]{3,2,1,0:T(8,128)(2,1)S(1)} custom-call(bf16[2,48,288]{2,1,0:T(8,128)(2,1)S(1)} %pad_maximum_fusion.r0_ref, bf16[2,48,288]{2,1,0:T(8,128)(2,1)S(1)} %collective-permute-done.1.r1_ref, bf16[2,48,288]{2,1,0:T(8,128)(2,1)S(1)} %collective-permute-done.3.r2_ref, bf16[2,48,288]{2,1,0:T(8,128)(2,1)S(1)} %collective-permute-done.4.r3_ref, ...), custom_call_target="tpu_custom_call" | custom-call | flops 10000000000 | bytes 30000000 | tf_op jit(solution)/shard_map/posterior/pallas_call | solution.py:630
  24.5 0.2 collective-permute-start.8
  24.8 1.4 %collective-permute-done.8 = bf16[8,120,128]{2,1,0:T(8,128)(2,1)S(1)} collective-permute-done((bf16[8,120,128]{2,1,0:T(8,128)(2,1)S(1)}, bf16[8,120,128]{2,1,0:T(8,128)(2,1)S(1)}, u32[]{:S(2)}, u32[]{:S(2)}) %collective-permute-start.8) | collective-permute-done | bytes 245792 | tf_op jit(solution)/shard_map/ppermute | solution.py:697
  26.1 0.1 fusion.3
  26.2 0.7 %collective-permute-start.10 = (bf16[2,120,128]{2,1,0:T(8,128)(2,1)S(1)}, bf16[2,120,128]{2,1,0:T(8,128)(2,1)S(1)}, u32[]{:S(2)}, u32[]{:S(2)}) collective-permute-start(bf16[2,120,128]{2,1,0:T(8,128)(2,1)S(1)} %get-tuple-element.47), channel_id=1, source_target_pairs={{0,4},{1,5},{2,6},{3,7},{4,0},{5,1},{6,2},{7,3},{8,12},{9,13},{10,... | collective-permute-start | bytes 184328 | tf_op jit(solution)/shard_map/ppermute | solution.py:697
  26.9 1.4 %collective-permute-start.11 = (bf16[2,120,128]{2,1,0:T(8,128)(2,1)S(1)}, bf16[2,120,128]{2,1,0:T(8,128)(2,1)S(1)}, u32[]{:S(2)}, u32[]{:S(2)}) collective-permute-start(bf16[2,120,128]{2,1,0:T(8,128)(2,1)S(1)} %get-tuple-element.46), channel_id=1, source_target_pairs={{0,6},{1,7},{2,4},{3,5},{4,2},{5,3},{6,0},{7,1},{8,14},{9,15},{10,... | collective-permute-start | bytes 184328 | tf_op jit(solution)/shard_map/ppermute | solution.py:697
  28.3 1.5 %collective-permute-start.9 = (bf16[2,120,128]{2,1,0:T(8,128)(2,1)S(1)}, bf16[2,120,128]{2,1,0:T(8,128)(2,1)S(1)}, u32[]{:S(2)}, u32[]{:S(2)}) collective-permute-start(bf16[2,120,128]{2,1,0:T(8,128)(2,1)S(1)} %get-tuple-element.45), channel_id=1, source_target_pairs={{0,2},{1,3},{2,0},{3,1},{4,6},{5,7},{6,4},{7,5},{8,10},{9,11},{10,... | collective-permute-start | bytes 184328 | tf_op jit(solution)/shard_map/ppermute | solution.py:697
  29.8 1.0 %collective-permute-done.10 = bf16[2,120,128]{2,1,0:T(8,128)(2,1)S(1)} collective-permute-done((bf16[2,120,128]{2,1,0:T(8,128)(2,1)S(1)}, bf16[2,120,128]{2,1,0:T(8,128)(2,1)S(1)}, u32[]{:S(2)}, u32[]{:S(2)}) %collective-permute-start.10) | collective-permute-done | bytes 61472 | tf_op jit(solution)/shard_map/ppermute | solution.py:697
  30.8 1.3 %collective-permute-done.11 = bf16[2,120,128]{2,1,0:T(8,128)(2,1)S(1)} collective-permute-done((bf16[2,120,128]{2,1,0:T(8,128)(2,1)S(1)}, bf16[2,120,128]{2,1,0:T(8,128)(2,1)S(1)}, u32[]{:S(2)}, u32[]{:S(2)}) %collective-permute-start.11) | collective-permute-done | bytes 61472 | tf_op jit(solution)/shard_map/ppermute | solution.py:697
  32.1 0.9 %collective-permute-done.9 = bf16[2,120,128]{2,1,0:T(8,128)(2,1)S(1)} collective-permute-done((bf16[2,120,128]{2,1,0:T(8,128)(2,1)S(1)}, bf16[2,120,128]{2,1,0:T(8,128)(2,1)S(1)}, u32[]{:S(2)}, u32[]{:S(2)}) %collective-permute-start.9) | collective-permute-done | bytes 61472 | tf_op jit(solution)/shard_map/ppermute | solution.py:697
  33.0 2.5 %collective-permute-start.12 = (bf16[120,128]{1,0:T(8,128)(2,1)S(1)}, bf16[120,128]{1,0:T(8,128)(2,1)S(1)}, u32[]{:S(2)}, u32[]{:S(2)}) collective-permute-start(bf16[120,128]{1,0:T(8,128)(2,1)S(1)} %fusion.2), channel_id=1, source_target_pairs={{0,8},{1,9},{2,10},{3,11},{4,12},{5,13},{6,14},{7,15},{8,0},{9,1},... | collective-permute-start | bytes 92168 | tf_op jit(solution)/shard_map/ppermute | solution.py:697
  35.6 2.5 %collective-permute-done.12.got_ref = bf16[120,128]{1,0:T(8,128)(2,1)S(1)} collective-permute-done((bf16[120,128]{1,0:T(8,128)(2,1)S(1)}, bf16[120,128]{1,0:T(8,128)(2,1)S(1)}, u32[]{:S(2)}, u32[]{:S(2)}) %collective-permute-start.12) | collective-permute-done | bytes 30752 | tf_op jit(solution)/shard_map/ppermute | solution.py:697
  38.0 1.1 %finish.1 = f32[48,288]{1,0:T(8,128)} custom-call(f32[120,128]{1,0:T(8,128)S(1)} %slice_bitcast_fusion.2.keep_ref, bf16[120,128]{1,0:T(8,128)(2,1)S(1)} %collective-permute-done.12.got_ref, bf16[4,160,288]{2,1,0:T(8,128)(2,1)S(1)} %get-tuple-element.42.back_ref), custom_call_target="tpu_custom_call" | custom-call | flops 1000000000 | bytes 3000000 | tf_op jit(solution)/shard_map/finish/pallas_call | solution.py:684
  (6 shorter events, 0.1 us)
Async XLA Ops:
  0.0 6.9 %copy-start = (bf16[48,288]{1,0:T(8,128)(2,1)S(1)}, bf16[48,288]{1,0:T(8,128)(2,1)}, u32[]{:S(2)}) copy-start(bf16[48,288]{1,0:T(8,128)(2,1)} %param.12) | copy-start | bytes 82948
  0.0 6.9 %collective-permute-start = (bf16[48,288]{1,0:T(8,128)(2,1)}, bf16[48,288]{1,0:T(8,128)(2,1)S(1)}, u32[]{:S(2)}, u32[]{:S(2)}) collective-permute-start(bf16[48,288]{1,0:T(8,128)(2,1)} %param.12), channel_id=1, source_target_pairs={{0,8},{1,9},{2,10},{3,11},{4,12},{5,13},{6,14},{7,15},{8,0},{9,1},... | collective-permute-start | bytes 82952 | tf_op jit(solution)/shard_map/ppermute | solution.py:697
  6.9 7.4 %collective-permute-start.2 = (bf16[2,48,288]{2,1,0:T(8,128)(2,1)S(1)}, bf16[2,48,288]{2,1,0:T(8,128)(2,1)S(1)}, u32[]{:S(2)}, u32[]{:S(2)}) collective-permute-start(bf16[2,48,288]{2,1,0:T(8,128)(2,1)S(1)} %pad_maximum_fusion.r0_ref), channel_id=1, source_target_pairs={{0,1},{1,0},{2,3},{3,2},{4,5},{5,4},{6,7},{7,6},{8,9},{9,8},{10,11... | collective-permute-start | bytes 165896 | tf_op jit(solution)/shard_map/ppermute | solution.py:697
  7.0 7.3 %collective-permute-start.1 = (bf16[2,48,288]{2,1,0:T(8,128)(2,1)S(1)}, bf16[2,48,288]{2,1,0:T(8,128)(2,1)S(1)}, u32[]{:S(2)}, u32[]{:S(2)}) collective-permute-start(bf16[2,48,288]{2,1,0:T(8,128)(2,1)S(1)} %pad_maximum_fusion.r0_ref), channel_id=1, source_target_pairs={{0,2},{1,3},{2,0},{3,1},{4,6},{5,7},{6,4},{7,5},{8,10},{9,11},{10,... | collective-permute-start | bytes 165896 | tf_op jit(solution)/shard_map/ppermute | solution.py:697
  8.6 5.8 %collective-permute-start.3 = (bf16[2,48,288]{2,1,0:T(8,128)(2,1)S(1)}, bf16[2,48,288]{2,1,0:T(8,128)(2,1)S(1)}, u32[]{:S(2)}, u32[]{:S(2)}) collective-permute-start(bf16[2,48,288]{2,1,0:T(8,128)(2,1)S(1)} %pad_maximum_fusion.r0_ref), channel_id=1, source_target_pairs={{0,4},{1,5},{2,6},{3,7},{4,0},{5,1},{6,2},{7,3},{8,12},{9,13},{10,... | collective-permute-start | bytes 165896 | tf_op jit(solution)/shard_map/ppermute | solution.py:697
  10.2 5.3 %collective-permute-start.4 = (bf16[2,48,288]{2,1,0:T(8,128)(2,1)S(1)}, bf16[2,48,288]{2,1,0:T(8,128)(2,1)S(1)}, u32[]{:S(2)}, u32[]{:S(2)}) collective-permute-start(bf16[2,48,288]{2,1,0:T(8,128)(2,1)S(1)} %pad_maximum_fusion.r0_ref), channel_id=1, source_target_pairs={{0,6},{1,7},{2,4},{3,5},{4,2},{5,3},{6,0},{7,1},{8,14},{9,15},{10,... | collective-permute-start | bytes 165896 | tf_op jit(solution)/shard_map/ppermute | solution.py:697
  15.4 1.3 %collective-permute-start.7 = (bf16[2,48,288]{2,1,0:T(8,128)(2,1)S(1)}, bf16[2,48,288]{2,1,0:T(8,128)(2,1)S(1)}, u32[]{:S(2)}, u32[]{:S(2)}) collective-permute-start(bf16[2,48,288]{2,1,0:T(8,128)(2,1)S(1)} %collective-permute-done.4.r3_ref), channel_id=1, source_target_pairs={{0,1},{1,0},{2,3},{3,2},{4,5},{5,4},{6,7},{7,6},{8,9},{9,8},{10,11... | collective-permute-start | bytes 165896 | tf_op jit(solution)/shard_map/ppermute | solution.py:697
  15.4 1.4 %collective-permute-start.6 = (bf16[2,48,288]{2,1,0:T(8,128)(2,1)S(1)}, bf16[2,48,288]{2,1,0:T(8,128)(2,1)S(1)}, u32[]{:S(2)}, u32[]{:S(2)}) collective-permute-start(bf16[2,48,288]{2,1,0:T(8,128)(2,1)S(1)} %collective-permute-done.3.r2_ref), channel_id=1, source_target_pairs={{0,1},{1,0},{2,3},{3,2},{4,5},{5,4},{6,7},{7,6},{8,9},{9,8},{10,11... | collective-permute-start | bytes 165896 | tf_op jit(solution)/shard_map/ppermute | solution.py:697
  15.9 1.3 %collective-permute-start.5 = (bf16[2,48,288]{2,1,0:T(8,128)(2,1)S(1)}, bf16[2,48,288]{2,1,0:T(8,128)(2,1)S(1)}, u32[]{:S(2)}, u32[]{:S(2)}) collective-permute-start(bf16[2,48,288]{2,1,0:T(8,128)(2,1)S(1)} %collective-permute-done.1.r1_ref), channel_id=1, source_target_pairs={{0,1},{1,0},{2,3},{3,2},{4,5},{5,4},{6,7},{7,6},{8,9},{9,8},{10,11... | collective-permute-start | bytes 165896 | tf_op jit(solution)/shard_map/ppermute | solution.py:697
  24.5 1.6 %collective-permute-start.8 = (bf16[8,120,128]{2,1,0:T(8,128)(2,1)S(1)}, bf16[8,120,128]{2,1,0:T(8,128)(2,1)S(1)}, u32[]{:S(2)}, u32[]{:S(2)}) collective-permute-start(bf16[8,120,128]{2,1,0:T(8,128)(2,1)S(1)} %slice_bitcast_fusion), channel_id=1, source_target_pairs={{0,1},{1,0},{2,3},{3,2},{4,5},{5,4},{6,7},{7,6},{8,9},{9,8},{10,11... | collective-permute-start | bytes 737288 | tf_op jit(solution)/shard_map/ppermute | solution.py:697
  26.2 4.5 %collective-permute-start.10 = (bf16[2,120,128]{2,1,0:T(8,128)(2,1)S(1)}, bf16[2,120,128]{2,1,0:T(8,128)(2,1)S(1)}, u32[]{:S(2)}, u32[]{:S(2)}) collective-permute-start(bf16[2,120,128]{2,1,0:T(8,128)(2,1)S(1)} %get-tuple-element.47), channel_id=1, source_target_pairs={{0,4},{1,5},{2,6},{3,7},{4,0},{5,1},{6,2},{7,3},{8,12},{9,13},{10,... | collective-permute-start | bytes 184328 | tf_op jit(solution)/shard_map/ppermute | solution.py:697
  26.9 5.2 %collective-permute-start.11 = (bf16[2,120,128]{2,1,0:T(8,128)(2,1)S(1)}, bf16[2,120,128]{2,1,0:T(8,128)(2,1)S(1)}, u32[]{:S(2)}, u32[]{:S(2)}) collective-permute-start(bf16[2,120,128]{2,1,0:T(8,128)(2,1)S(1)} %get-tuple-element.46), channel_id=1, source_target_pairs={{0,6},{1,7},{2,4},{3,5},{4,2},{5,3},{6,0},{7,1},{8,14},{9,15},{10,... | collective-permute-start | bytes 184328 | tf_op jit(solution)/shard_map/ppermute | solution.py:697
  28.3 4.7 %collective-permute-start.9 = (bf16[2,120,128]{2,1,0:T(8,128)(2,1)S(1)}, bf16[2,120,128]{2,1,0:T(8,128)(2,1)S(1)}, u32[]{:S(2)}, u32[]{:S(2)}) collective-permute-start(bf16[2,120,128]{2,1,0:T(8,128)(2,1)S(1)} %get-tuple-element.45), channel_id=1, source_target_pairs={{0,2},{1,3},{2,0},{3,1},{4,6},{5,7},{6,4},{7,5},{8,10},{9,11},{10,... | collective-permute-start | bytes 184328 | tf_op jit(solution)/shard_map/ppermute | solution.py:697
  33.0 5.0 %collective-permute-start.12 = (bf16[120,128]{1,0:T(8,128)(2,1)S(1)}, bf16[120,128]{1,0:T(8,128)(2,1)S(1)}, u32[]{:S(2)}, u32[]{:S(2)}) collective-permute-start(bf16[120,128]{1,0:T(8,128)(2,1)S(1)} %fusion.2), channel_id=1, source_target_pairs={{0,8},{1,9},{2,10},{3,11},{4,12},{5,13},{6,14},{7,15},{8,0},{9,1},... | collective-permute-start | bytes 92168 | tf_op jit(solution)/shard_map/ppermute | solution.py:697

commit v5 on v4

--- a/solution.py
+++ b/solution.py
@@ -30,7 +30,8 @@
 ROWS = S_PAD * ROWS8
 LIVE = SHIFTS * ROWS8
 COLS = 512
-STEPS_A = 3
+STEPS_A = 2
+STEPS_B = 5
 GROUP = 256
 TAIL = 3 * LANES
 TAIL_ROWS = 16
@@ -295,7 +296,7 @@
         (grp_hbm, grp_ref), (bin_hbm, bin_ref), (img_hbm, img_ref), (sig_hbm, sig_ref),
         (ctf_hbm, ctf_ref), (exp_hbm, exp_ref), (perm_hbm, perm_ref),
         (table_hbm.at[pl.ds(0, S_STEP * STEPS_A)], table_ref),
-        (table_hbm.at[pl.ds(S_STEP * STEPS_A, S_PAD - S_STEP * STEPS_A)], rest_ref),
+        (table_hbm.at[pl.ds(S_STEP * STEPS_A, S_STEP * STEPS_B)], rest_ref),
     ]
     copies = [pltpu.make_async_copy(a, b, sems.at[i]) for i, (a, b) in enumerate(moves)]
     for copy in copies[:8]:
@@ -342,20 +343,22 @@
 
 
 def second_kernel(
-    fh_in, fl_in, table_ref, pix_ref, slot_ref, mt_hbm, back_hbm,
-    fh_ref, fl_ref, mt_ref, back_ref, sems,
+    fh_in, fl_in, table_ref, pix_ref, slot_ref, table_hbm, mt_hbm, back_hbm,
+    fh_ref, fl_ref, mt_ref, back_ref, late_ref, sems,
 ):
     del fh_in, fl_in
-    copies = [
-        pltpu.make_async_copy(mt_hbm, mt_ref, sems.at[0]),
-        pltpu.make_async_copy(back_hbm, back_ref, sems.at[1]),
-    ]
+    early = STEPS_A + STEPS_B
+    late = table_hbm.at[pl.ds(S_STEP * early, S_PAD - S_STEP * early)]
+    moves = [(late, late_ref), (mt_hbm, mt_ref), (back_hbm, back_ref)]
+    copies = [pltpu.make_async_copy(a, b, sems.at[i]) for i, (a, b) in enumerate(moves)]
     for copy in copies:
         copy.start()
+    transform_steps(table_ref, pix_ref, slot_ref, fh_ref, fl_ref, STEPS_A, STEPS_B)
+    copies[0].wait()
     transform_steps(
-        table_ref, pix_ref, slot_ref, fh_ref, fl_ref, STEPS_A, S_PAD // S_STEP - STEPS_A
-    )
-    for copy in copies:
+        late_ref, pix_ref, slot_ref, fh_ref, fl_ref, early, S_PAD // S_STEP - early
+    )
+    for copy in copies[1:]:
         copy.wait()
 
 
@@ -373,7 +376,6 @@
 
 def first_features(images, sigma2, ctf_group, defocus_bin):
     feat = (FREQS, ROWS, 2 * LANES)
-    tail = S_PAD - S_STEP * STEPS_A
     return pl.pallas_call(
         first_kernel,
         out_shape=(
@@ -381,7 +383,7 @@
             jax.ShapeDtypeStruct(feat, F8),
             jax.ShapeDtypeStruct((2, ROT, ROWS8, LANES), F32),
             jax.ShapeDtypeStruct((ROWS8, LANES), F32),
-            jax.ShapeDtypeStruct((tail, 2 * ROT, LANES), F32),
+            jax.ShapeDtypeStruct((S_STEP * STEPS_B, 2 * ROT, LANES), F32),
         ),
         in_specs=[HB] * 8,
         out_specs=[VM] * 5,
@@ -417,14 +419,20 @@
             jax.ShapeDtypeStruct(mt.shape, BF),
             jax.ShapeDtypeStruct(back.shape, BF),
         ),
-        in_specs=[VM] * 5 + [HB] * 2,
+        in_specs=[VM] * 5 + [HB] * 3,
         out_specs=[VM] * 4,
-        scratch_shapes=[pltpu.SemaphoreType.DMA((2,))],
+        scratch_shapes=[
+            pltpu.VMEM((S_PAD - S_STEP * (STEPS_A + STEPS_B), 2 * ROT, LANES), F32),
+            pltpu.SemaphoreType.DMA((3,)),
+        ],
         input_output_aliases={0: 0, 1: 1},
         compiler_params=pltpu.CompilerParams(vmem_limit_bytes=16 * MIB),
         cost_estimate=cost(2.5),
         name="features_second",
-    )(hi, lo, table, pix, slot, *in_hbm(jnp.asarray(mt), jnp.asarray(back)))
+    )(
+        hi, lo, table, pix, slot,
+        *in_hbm(jnp.asarray(phase_lanes()), jnp.asarray(mt), jnp.asarray(back)),
+    )
 
 
 def nt(left, right):

time: 39.3 us -> 39 us (level)
  transfers between devices with their start and end apart: 13 -> 13, of which waited for: 9 -> 10; matrix products, arithmetic and copies ran while one was open for 0% -> 0% of each run, Pallas kernels for 17% -> 17%
where the time goes in v5:
time: 39 us; the launch traced here: 38.8 us
  Pallas kernels  14.7 us (38%)
  starting transfers between devices  14.6 us (37%)
  waiting for transfers between devices  9.25 us (24%)
    ppermute x13, starting transfers between devices, swap(): return lax.ppermute(value, 'img', pairs)  14.6 us
    ppermute x13, waiting for transfers between devices, swap(): return lax.ppermute(value, 'img', pairs)  9.25 us
    pallas_call x1, Pallas kernels, make_payload(): pl.pallas_call(functools.partial(posterior_kernel, direct), out_shape=jax...  7.13 us
    pallas_call x1, Pallas kernels, second_features(): pl.pallas_call(second_kernel, out_shape=(jax.ShapeDtypeStruct(hi.shape, B...  4.04 us
    pallas_call x1, Pallas kernels, first_features(): pl.pallas_call(first_kernel, out_shape=(jax.ShapeDtypeStruct(feat, BF), j...  2.45 us
    pallas_call x1, Pallas kernels, finish(): pl.pallas_call(final_kernel, out_shape=jax.ShapeDtypeStruct((CLASSES, BLO...  1.08 us
  transfers between devices with their start and end apart: 13, of which 10 were waited for; matrix products, arithmetic and copies ran while one was open for 0% of the time, Pallas kernels for 17%

profile of v5, /device:TPU:0, one launch (start us, length us, event | category | flops | bytes accessed | tf_op | source)
XLA Modules:
  0.0 38.8 jit_solution(17407441177463456377)
XLA Ops:
  0.0 0.0 copy-start
  0.0 4.0 %collective-permute-start = (bf16[48,288]{1,0:T(8,128)(2,1)}, bf16[48,288]{1,0:T(8,128)(2,1)S(1)}, u32[]{:S(2)}, u32[]{:S(2)}) collective-permute-start(bf16[48,288]{1,0:T(8,128)(2,1)} %param.13), channel_id=1, source_target_pairs={{0,8},{1,9},{2,10},{3,11},{4,12},{5,13},{6,14},{7,15},{8,0},{9,1},... | collective-permute-start | bytes 82952 | tf_op jit(solution)/shard_map/ppermute | solution.py:705
  4.0 2.5 %features_first.1 = (bf16[19,416,256]{2,1,0:T(8,128)(2,1)S(1)}, f8e5m2[19,416,256]{2,1,0:T(32,128)(4,1)S(1)}, f32[2,36,8,128]{3,2,1,0:T(8,128)S(1)}, f32[8,128]{1,0:T(8,128)S(1)}, f32[20,72,128]{2,1,0:T(8,128)S(1)}) custom-call(s32[8]{0:T(128)} %grp_hbm.1, s32[8]{0:T(128)} %bin_hbm.1, bf16[8,4608]{1,0:T(8,128)(2,1)} %img_hbm.1, f32[16,16]{1,0:T(8,128)} %sig_hbm.1, ...), custom_call_target="tpu_custom_call" | custom-call | flops 4499999744 | bytes 13500000 | tf_op jit(solution)/shard_map/features_first/pallas_call | solution.py:379
  6.5 0.2 collective-permute-done
  6.7 0.0 copy-done
  6.7 0.1 collective-permute-start.2
  6.8 1.7 %collective-permute-start.1 = (bf16[2,48,288]{2,1,0:T(8,128)(2,1)S(1)}, bf16[2,48,288]{2,1,0:T(8,128)(2,1)S(1)}, u32[]{:S(2)}, u32[]{:S(2)}) collective-permute-start(bf16[2,48,288]{2,1,0:T(8,128)(2,1)S(1)} %pad_maximum_fusion.r0_ref), channel_id=1, source_target_pairs={{0,2},{1,3},{2,0},{3,1},{4,6},{5,7},{6,4},{7,5},{8,10},{9,11},{10,... | collective-permute-start | bytes 165896 | tf_op jit(solution)/shard_map/ppermute | solution.py:705
  8.5 1.3 %collective-permute-start.3 = (bf16[2,48,288]{2,1,0:T(8,128)(2,1)S(1)}, bf16[2,48,288]{2,1,0:T(8,128)(2,1)S(1)}, u32[]{:S(2)}, u32[]{:S(2)}) collective-permute-start(bf16[2,48,288]{2,1,0:T(8,128)(2,1)S(1)} %pad_maximum_fusion.r0_ref), channel_id=1, source_target_pairs={{0,4},{1,5},{2,6},{3,7},{4,0},{5,1},{6,2},{7,3},{8,12},{9,13},{10,... | collective-permute-start | bytes 165896 | tf_op jit(solution)/shard_map/ppermute | solution.py:705
  9.8 0.5 %collective-permute-start.4 = (bf16[2,48,288]{2,1,0:T(8,128)(2,1)S(1)}, bf16[2,48,288]{2,1,0:T(8,128)(2,1)S(1)}, u32[]{:S(2)}, u32[]{:S(2)}) collective-permute-start(bf16[2,48,288]{2,1,0:T(8,128)(2,1)S(1)} %pad_maximum_fusion.r0_ref), channel_id=1, source_target_pairs={{0,6},{1,7},{2,4},{3,5},{4,2},{5,3},{6,0},{7,1},{8,14},{9,15},{10,... | collective-permute-start | bytes 165896 | tf_op jit(solution)/shard_map/ppermute | solution.py:705
  10.3 4.0 %features_second.1 = (bf16[19,416,256]{2,1,0:T(8,128)(2,1)S(1)}, f8e5m2[19,416,256]{2,1,0:T(32,128)(4,1)S(1)}, bf16[2,304,288]{2,1,0:T(8,128)(2,1)S(1)}, bf16[4,160,288]{2,1,0:T(8,128)(2,1)S(1)}) custom-call(bf16[19,416,256]{2,1,0:T(8,128)(2,1)S(1)} %get-tuple-element.26.fh_in, ...), custom_call_target="tpu_custom_call", output_to_operand_aliasing={{0}: (0, {}), {1}: (1, {})} | custom-call | flops 2500000000 | bytes 7500000 | tf_op jit(solution)/shard_map/features_second/pallas_call | solution.py:414
  14.4 0.0 collective-permute-done.2.s0_ref
  14.4 0.0 collective-permute-done.1.r1_ref
  14.4 0.0 collective-permute-done.3.r2_ref
  14.4 0.7 %collective-permute-done.4.r3_ref = bf16[2,48,288]{2,1,0:T(8,128)(2,1)S(1)} collective-permute-done((bf16[2,48,288]{2,1,0:T(8,128)(2,1)S(1)}, bf16[2,48,288]{2,1,0:T(8,128)(2,1)S(1)}, u32[]{:S(2)}, u32[]{:S(2)}) %collective-permute-start.4) | collective-permute-done | bytes 55328 | tf_op jit(solution)/shard_map/ppermute | solution.py:705
  15.0 0.0 collective-permute-start.7
  15.0 0.5 %collective-permute-start.6 = (bf16[2,48,288]{2,1,0:T(8,128)(2,1)S(1)}, bf16[2,48,288]{2,1,0:T(8,128)(2,1)S(1)}, u32[]{:S(2)}, u32[]{:S(2)}) collective-permute-start(bf16[2,48,288]{2,1,0:T(8,128)(2,1)S(1)} %collective-permute-done.3.r2_ref), channel_id=1, source_target_pairs={{0,1},{1,0},{2,3},{3,2},{4,5},{5,4},{6,7},{7,6},{8,9},{9,8},{10,11... | collective-permute-start | bytes 165896 | tf_op jit(solution)/shard_map/ppermute | solution.py:705
  15.5 0.0 collective-permute-start.5
  15.6 0.8 %collective-permute-done.7.s3_ref = bf16[2,48,288]{2,1,0:T(8,128)(2,1)S(1)} collective-permute-done((bf16[2,48,288]{2,1,0:T(8,128)(2,1)S(1)}, bf16[2,48,288]{2,1,0:T(8,128)(2,1)S(1)}, u32[]{:S(2)}, u32[]{:S(2)}) %collective-permute-start.7) | collective-permute-done | bytes 55328 | tf_op jit(solution)/shard_map/ppermute | solution.py:705
  16.3 0.2 collective-permute-done.6.s2_ref
  16.5 0.4 collective-permute-done.5.s1_ref
  16.8 7.1 %posterior.1 = bf16[2,8,120,128]{3,2,1,0:T(8,128)(2,1)S(1)} custom-call(bf16[2,48,288]{2,1,0:T(8,128)(2,1)S(1)} %pad_maximum_fusion.r0_ref, bf16[2,48,288]{2,1,0:T(8,128)(2,1)S(1)} %collective-permute-done.1.r1_ref, bf16[2,48,288]{2,1,0:T(8,128)(2,1)S(1)} %collective-permute-done.3.r2_ref, bf16[2,48,288]{2,1,0:T(8,128)(2,1)S(1)} %collective-permute-done.4.r3_ref, ...), custom_call_target="tpu_custom_call" | custom-call | flops 10000000000 | bytes 30000000 | tf_op jit(solution)/shard_map/posterior/pallas_call | solution.py:638
  24.0 0.2 collective-permute-start.8
  24.2 1.4 %collective-permute-done.8 = bf16[8,120,128]{2,1,0:T(8,128)(2,1)S(1)} collective-permute-done((bf16[8,120,128]{2,1,0:T(8,128)(2,1)S(1)}, bf16[8,120,128]{2,1,0:T(8,128)(2,1)S(1)}, u32[]{:S(2)}, u32[]{:S(2)}) %collective-permute-start.8) | collective-permute-done | bytes 245792 | tf_op jit(solution)/shard_map/ppermute | solution.py:705
  25.6 0.1 fusion.3
  25.7 0.9 %collective-permute-start.10 = (bf16[2,120,128]{2,1,0:T(8,128)(2,1)S(1)}, bf16[2,120,128]{2,1,0:T(8,128)(2,1)S(1)}, u32[]{:S(2)}, u32[]{:S(2)}) collective-permute-start(bf16[2,120,128]{2,1,0:T(8,128)(2,1)S(1)} %get-tuple-element.47), channel_id=1, source_target_pairs={{0,4},{1,5},{2,6},{3,7},{4,0},{5,1},{6,2},{7,3},{8,12},{9,13},{10,... | collective-permute-start | bytes 184328 | tf_op jit(solution)/shard_map/ppermute | solution.py:705
  26.6 1.7 %collective-permute-start.11 = (bf16[2,120,128]{2,1,0:T(8,128)(2,1)S(1)}, bf16[2,120,128]{2,1,0:T(8,128)(2,1)S(1)}, u32[]{:S(2)}, u32[]{:S(2)}) collective-permute-start(bf16[2,120,128]{2,1,0:T(8,128)(2,1)S(1)} %get-tuple-element.46), channel_id=1, source_target_pairs={{0,6},{1,7},{2,4},{3,5},{4,2},{5,3},{6,0},{7,1},{8,14},{9,15},{10,... | collective-permute-start | bytes 184328 | tf_op jit(solution)/shard_map/ppermute | solution.py:705
  28.3 0.9 %collective-permute-start.9 = (bf16[2,120,128]{2,1,0:T(8,128)(2,1)S(1)}, bf16[2,120,128]{2,1,0:T(8,128)(2,1)S(1)}, u32[]{:S(2)}, u32[]{:S(2)}) collective-permute-start(bf16[2,120,128]{2,1,0:T(8,128)(2,1)S(1)} %get-tuple-element.45), channel_id=1, source_target_pairs={{0,2},{1,3},{2,0},{3,1},{4,6},{5,7},{6,4},{7,5},{8,10},{9,11},{10,... | collective-permute-start | bytes 184328 | tf_op jit(solution)/shard_map/ppermute | solution.py:705
  29.2 0.7 %collective-permute-done.10 = bf16[2,120,128]{2,1,0:T(8,128)(2,1)S(1)} collective-permute-done((bf16[2,120,128]{2,1,0:T(8,128)(2,1)S(1)}, bf16[2,120,128]{2,1,0:T(8,128)(2,1)S(1)}, u32[]{:S(2)}, u32[]{:S(2)}) %collective-permute-start.10) | collective-permute-done | bytes 61472 | tf_op jit(solution)/shard_map/ppermute | solution.py:705
  29.9 2.0 %collective-permute-done.11 = bf16[2,120,128]{2,1,0:T(8,128)(2,1)S(1)} collective-permute-done((bf16[2,120,128]{2,1,0:T(8,128)(2,1)S(1)}, bf16[2,120,128]{2,1,0:T(8,128)(2,1)S(1)}, u32[]{:S(2)}, u32[]{:S(2)}) %collective-permute-start.11) | collective-permute-done | bytes 61472 | tf_op jit(solution)/shard_map/ppermute | solution.py:705
  31.9 0.9 %collective-permute-done.9 = bf16[2,120,128]{2,1,0:T(8,128)(2,1)S(1)} collective-permute-done((bf16[2,120,128]{2,1,0:T(8,128)(2,1)S(1)}, bf16[2,120,128]{2,1,0:T(8,128)(2,1)S(1)}, u32[]{:S(2)}, u32[]{:S(2)}) %collective-permute-start.9) | collective-permute-done | bytes 61472 | tf_op jit(solution)/shard_map/ppermute | solution.py:705
  32.9 2.7 %collective-permute-start.12 = (bf16[120,128]{1,0:T(8,128)(2,1)S(1)}, bf16[120,128]{1,0:T(8,128)(2,1)S(1)}, u32[]{:S(2)}, u32[]{:S(2)}) collective-permute-start(bf16[120,128]{1,0:T(8,128)(2,1)S(1)} %fusion.2), channel_id=1, source_target_pairs={{0,8},{1,9},{2,10},{3,11},{4,12},{5,13},{6,14},{7,15},{8,0},{9,1},... | collective-permute-start | bytes 92168 | tf_op jit(solution)/shard_map/ppermute | solution.py:705
  35.6 2.2 %collective-permute-done.12.got_ref = bf16[120,128]{1,0:T(8,128)(2,1)S(1)} collective-permute-done((bf16[120,128]{1,0:T(8,128)(2,1)S(1)}, bf16[120,128]{1,0:T(8,128)(2,1)S(1)}, u32[]{:S(2)}, u32[]{:S(2)}) %collective-permute-start.12) | collective-permute-done | bytes 30752 | tf_op jit(solution)/shard_map/ppermute | solution.py:705
  37.8 1.1 %finish.1 = f32[48,288]{1,0:T(8,128)} custom-call(f32[120,128]{1,0:T(8,128)S(1)} %slice_bitcast_fusion.2.keep_ref, bf16[120,128]{1,0:T(8,128)(2,1)S(1)} %collective-permute-done.12.got_ref, bf16[4,160,288]{2,1,0:T(8,128)(2,1)S(1)} %get-tuple-element.42.back_ref), custom_call_target="tpu_custom_call" | custom-call | flops 1000000000 | bytes 3000000 | tf_op jit(solution)/shard_map/finish/pallas_call | solution.py:692
  (6 shorter events, 0.1 us)
Async XLA Ops:
  0.0 6.7 %copy-start = (bf16[48,288]{1,0:T(8,128)(2,1)S(1)}, bf16[48,288]{1,0:T(8,128)(2,1)}, u32[]{:S(2)}) copy-start(bf16[48,288]{1,0:T(8,128)(2,1)} %param.13) | copy-start | bytes 82948
  0.0 6.6 %collective-permute-start = (bf16[48,288]{1,0:T(8,128)(2,1)}, bf16[48,288]{1,0:T(8,128)(2,1)S(1)}, u32[]{:S(2)}, u32[]{:S(2)}) collective-permute-start(bf16[48,288]{1,0:T(8,128)(2,1)} %param.13), channel_id=1, source_target_pairs={{0,8},{1,9},{2,10},{3,11},{4,12},{5,13},{6,14},{7,15},{8,0},{9,1},... | collective-permute-start | bytes 82952 | tf_op jit(solution)/shard_map/ppermute | solution.py:705
  6.7 7.7 %collective-permute-start.2 = (bf16[2,48,288]{2,1,0:T(8,128)(2,1)S(1)}, bf16[2,48,288]{2,1,0:T(8,128)(2,1)S(1)}, u32[]{:S(2)}, u32[]{:S(2)}) collective-permute-start(bf16[2,48,288]{2,1,0:T(8,128)(2,1)S(1)} %pad_maximum_fusion.r0_ref), channel_id=1, source_target_pairs={{0,1},{1,0},{2,3},{3,2},{4,5},{5,4},{6,7},{7,6},{8,9},{9,8},{10,11... | collective-permute-start | bytes 165896 | tf_op jit(solution)/shard_map/ppermute | solution.py:705
  6.8 7.6 %collective-permute-start.1 = (bf16[2,48,288]{2,1,0:T(8,128)(2,1)S(1)}, bf16[2,48,288]{2,1,0:T(8,128)(2,1)S(1)}, u32[]{:S(2)}, u32[]{:S(2)}) collective-permute-start(bf16[2,48,288]{2,1,0:T(8,128)(2,1)S(1)} %pad_maximum_fusion.r0_ref), channel_id=1, source_target_pairs={{0,2},{1,3},{2,0},{3,1},{4,6},{5,7},{6,4},{7,5},{8,10},{9,11},{10,... | collective-permute-start | bytes 165896 | tf_op jit(solution)/shard_map/ppermute | solution.py:705
  8.5 5.9 %collective-permute-start.3 = (bf16[2,48,288]{2,1,0:T(8,128)(2,1)S(1)}, bf16[2,48,288]{2,1,0:T(8,128)(2,1)S(1)}, u32[]{:S(2)}, u32[]{:S(2)}) collective-permute-start(bf16[2,48,288]{2,1,0:T(8,128)(2,1)S(1)} %pad_maximum_fusion.r0_ref), channel_id=1, source_target_pairs={{0,4},{1,5},{2,6},{3,7},{4,0},{5,1},{6,2},{7,3},{8,12},{9,13},{10,... | collective-permute-start | bytes 165896 | tf_op jit(solution)/shard_map/ppermute | solution.py:705
  9.8 5.3 %collective-permute-start.4 = (bf16[2,48,288]{2,1,0:T(8,128)(2,1)S(1)}, bf16[2,48,288]{2,1,0:T(8,128)(2,1)S(1)}, u32[]{:S(2)}, u32[]{:S(2)}) collective-permute-start(bf16[2,48,288]{2,1,0:T(8,128)(2,1)S(1)} %pad_maximum_fusion.r0_ref), channel_id=1, source_target_pairs={{0,6},{1,7},{2,4},{3,5},{4,2},{5,3},{6,0},{7,1},{8,14},{9,15},{10,... | collective-permute-start | bytes 165896 | tf_op jit(solution)/shard_map/ppermute | solution.py:705
  15.0 1.3 %collective-permute-start.7 = (bf16[2,48,288]{2,1,0:T(8,128)(2,1)S(1)}, bf16[2,48,288]{2,1,0:T(8,128)(2,1)S(1)}, u32[]{:S(2)}, u32[]{:S(2)}) collective-permute-start(bf16[2,48,288]{2,1,0:T(8,128)(2,1)S(1)} %collective-permute-done.4.r3_ref), channel_id=1, source_target_pairs={{0,1},{1,0},{2,3},{3,2},{4,5},{5,4},{6,7},{7,6},{8,9},{9,8},{10,11... | collective-permute-start | bytes 165896 | tf_op jit(solution)/shard_map/ppermute | solution.py:705
  15.0 1.4 %collective-permute-start.6 = (bf16[2,48,288]{2,1,0:T(8,128)(2,1)S(1)}, bf16[2,48,288]{2,1,0:T(8,128)(2,1)S(1)}, u32[]{:S(2)}, u32[]{:S(2)}) collective-permute-start(bf16[2,48,288]{2,1,0:T(8,128)(2,1)S(1)} %collective-permute-done.3.r2_ref), channel_id=1, source_target_pairs={{0,1},{1,0},{2,3},{3,2},{4,5},{5,4},{6,7},{7,6},{8,9},{9,8},{10,11... | collective-permute-start | bytes 165896 | tf_op jit(solution)/shard_map/ppermute | solution.py:705
  15.5 1.3 %collective-permute-start.5 = (bf16[2,48,288]{2,1,0:T(8,128)(2,1)S(1)}, bf16[2,48,288]{2,1,0:T(8,128)(2,1)S(1)}, u32[]{:S(2)}, u32[]{:S(2)}) collective-permute-start(bf16[2,48,288]{2,1,0:T(8,128)(2,1)S(1)} %collective-permute-done.1.r1_ref), channel_id=1, source_target_pairs={{0,1},{1,0},{2,3},{3,2},{4,5},{5,4},{6,7},{7,6},{8,9},{9,8},{10,11... | collective-permute-start | bytes 165896 | tf_op jit(solution)/shard_map/ppermute | solution.py:705
  24.0 1.6 %collective-permute-start.8 = (bf16[8,120,128]{2,1,0:T(8,128)(2,1)S(1)}, bf16[8,120,128]{2,1,0:T(8,128)(2,1)S(1)}, u32[]{:S(2)}, u32[]{:S(2)}) collective-permute-start(bf16[8,120,128]{2,1,0:T(8,128)(2,1)S(1)} %slice_bitcast_fusion), channel_id=1, source_target_pairs={{0,1},{1,0},{2,3},{3,2},{4,5},{5,4},{6,7},{7,6},{8,9},{9,8},{10,11... | collective-permute-start | bytes 737288 | tf_op jit(solution)/shard_map/ppermute | solution.py:705
  25.7 4.3 %collective-permute-start.10 = (bf16[2,120,128]{2,1,0:T(8,128)(2,1)S(1)}, bf16[2,120,128]{2,1,0:T(8,128)(2,1)S(1)}, u32[]{:S(2)}, u32[]{:S(2)}) collective-permute-start(bf16[2,120,128]{2,1,0:T(8,128)(2,1)S(1)} %get-tuple-element.47), channel_id=1, source_target_pairs={{0,4},{1,5},{2,6},{3,7},{4,0},{5,1},{6,2},{7,3},{8,12},{9,13},{10,... | collective-permute-start | bytes 184328 | tf_op jit(solution)/shard_map/ppermute | solution.py:705
  26.6 5.3 %collective-permute-start.11 = (bf16[2,120,128]{2,1,0:T(8,128)(2,1)S(1)}, bf16[2,120,128]{2,1,0:T(8,128)(2,1)S(1)}, u32[]{:S(2)}, u32[]{:S(2)}) collective-permute-start(bf16[2,120,128]{2,1,0:T(8,128)(2,1)S(1)} %get-tuple-element.46), channel_id=1, source_target_pairs={{0,6},{1,7},{2,4},{3,5},{4,2},{5,3},{6,0},{7,1},{8,14},{9,15},{10,... | collective-permute-start | bytes 184328 | tf_op jit(solution)/shard_map/ppermute | solution.py:705
  28.3 4.6 %collective-permute-start.9 = (bf16[2,120,128]{2,1,0:T(8,128)(2,1)S(1)}, bf16[2,120,128]{2,1,0:T(8,128)(2,1)S(1)}, u32[]{:S(2)}, u32[]{:S(2)}) collective-permute-start(bf16[2,120,128]{2,1,0:T(8,128)(2,1)S(1)} %get-tuple-element.45), channel_id=1, source_target_pairs={{0,2},{1,3},{2,0},{3,1},{4,6},{5,7},{6,4},{7,5},{8,10},{9,11},{10,... | collective-permute-start | bytes 184328 | tf_op jit(solution)/shard_map/ppermute | solution.py:705
  32.9 4.9 %collective-permute-start.12 = (bf16[120,128]{1,0:T(8,128)(2,1)S(1)}, bf16[120,128]{1,0:T(8,128)(2,1)S(1)}, u32[]{:S(2)}, u32[]{:S(2)}) collective-permute-start(bf16[120,128]{1,0:T(8,128)(2,1)S(1)} %fusion.2), channel_id=1, source_target_pairs={{0,8},{1,9},{2,10},{3,11},{4,12},{5,13},{6,14},{7,15},{8,0},{9,1},... | collective-permute-start | bytes 92168 | tf_op jit(solution)/shard_map/ppermute | solution.py:705

commit v6 on v5

--- a/solution.py
+++ b/solution.py
@@ -131,8 +131,12 @@
                 real[q, cc, d, cc, STEP * b + d] = scale * np.cos(turn)
                 if q not in (0, ROT // 2):
                     imag[q, cc, d, cc, STEP * b + d] = -scale * np.sin(turn)
-    shape = (QUADS, 4, ROWS8, BLOCK_COLS)
-    return [t.reshape(shape).transpose(1, 0, 2, 3).reshape(4 * QUADS * ROWS8, BLOCK_COLS) for t in (real, imag)]
+    rows = []
+    for slots in (slice(0, 3), slice(3, 4)):
+        for t in (real, imag):
+            part = t.reshape(QUADS, 4, ROWS8, BLOCK_COLS)[:, slots].transpose(1, 0, 2, 3).reshape(-1, BLOCK_COLS)
+            rows.append(np.pad(part, ((0, LANES - len(part)), (0, 0))))
+    return np.concatenate(rows)
 
 
 def split(table):
@@ -410,7 +414,7 @@
 
 def second_features(hi, lo, table, pix, slot):
     mt = np.stack(split(refs_transform()))
-    back = np.stack([half for part in inverse_transform() for half in split(part)])
+    back = np.stack(split(inverse_transform()))
     return pl.pallas_call(
         second_kernel,
         out_shape=(
@@ -665,22 +669,21 @@
 
 def final_kernel(keep_ref, got_ref, back_ref, out_ref):
     total = keep_ref[...] + got_ref[...].astype(F32)
+    total = jnp.concatenate([total, jnp.zeros((LANES - PAY, LANES), F32)], axis=0)
     turned = total.T
     width = QUADS * ROWS8
-    third = 2 * CLASSES // 3
-    last = jnp.concatenate(
-        [turned[2 * CLASSES :, slot * width : (slot + 1) * width] for slot in range(3)], axis=0
-    )
-    numer = jnp.zeros((CLASSES, BLOCK_COLS), F32)
-    for part in range(2):
-        rows = slice(part * CLASSES, (part + 1) * CLASSES)
-        for value, first in ((turned[rows], 0), (last[rows], 3 * width)):
-            span = slice(first, first + value.shape[1])
-            hi = value.astype(BF)
-            lo = (value - hi.astype(F32)).astype(BF)
-            dot = functools.partial(jnp.dot, preferred_element_type=F32)
-            table_hi, table_lo = back_ref[2 * part, span], back_ref[2 * part + 1, span]
-            numer += dot(hi, table_hi) + dot(lo, table_hi) + dot(hi, table_lo)
+    rest = turned[2 * CLASSES :]
+    last = [rest] + [pltpu.roll(rest, LANES - slot * width, 1) for slot in (1, 2)]
+    last = jnp.concatenate(last, axis=0)
+    column = lax.broadcasted_iota(jnp.int32, last.shape, 1)
+    last = jnp.where(column < width, last, 0.0)
+    parts = [v[rows] for v in (turned, last) for rows in (slice(0, CLASSES), slice(CLASSES, 2 * CLASSES))]
+    value = jnp.concatenate(parts, axis=1)
+    hi = value.astype(BF)
+    lo = (value - hi.astype(F32)).astype(BF)
+    dot = functools.partial(jnp.dot, preferred_element_type=F32)
+    both = dot(jnp.concatenate([hi, lo], axis=0), back_ref[0])
+    numer = both[:CLASSES] + both[CLASSES:] + dot(hi, back_ref[1])
     weights = turned[CLASSES : 2 * CLASSES]
     column = lax.broadcasted_iota(jnp.int32, (CLASSES, BLOCK_COLS), 1)
     first = weights[:, 0:1] + weights[:, 1:2]

time: 39 us -> 39 us (level)
  no operation moved by 1% of the time
where the time goes in v6:
time: 39 us; the launch traced here: 38.8 us
  Pallas kernels  14.7 us (38%)
  starting transfers between devices  14.6 us (37%)
  waiting for transfers between devices  9.25 us (24%)
    ppermute x13, starting transfers between devices, swap(): return lax.ppermute(value, 'img', pairs)  14.6 us
    ppermute x13, waiting for transfers between devices, swap(): return lax.ppermute(value, 'img', pairs)  9.25 us
    pallas_call x1, Pallas kernels, make_payload(): pl.pallas_call(functools.partial(posterior_kernel, direct), out_shape=jax...  7.13 us
    pallas_call x1, Pallas kernels, second_features(): pl.pallas_call(second_kernel, out_shape=(jax.ShapeDtypeStruct(hi.shape, B...  4.04 us
    pallas_call x1, Pallas kernels, first_features(): pl.pallas_call(first_kernel, out_shape=(jax.ShapeDtypeStruct(feat, BF), j...  2.45 us
    pallas_call x1, Pallas kernels, finish(): pl.pallas_call(final_kernel, out_shape=jax.ShapeDtypeStruct((CLASSES, BLO...  1.05 us
  transfers between devices with their start and end apart: 13, of which 10 were waited for; matrix products, arithmetic and copies ran while one was open for 0% of the time, Pallas kernels for 17%

profile of v6, /device:TPU:0, one launch (start us, length us, event | category | flops | bytes accessed | tf_op | source)
XLA Modules:
  0.0 38.8 jit_solution(14141693371175458634)
XLA Ops:
  0.0 0.0 copy-start
  0.0 4.0 %collective-permute-start = (bf16[48,288]{1,0:T(8,128)(2,1)}, bf16[48,288]{1,0:T(8,128)(2,1)S(1)}, u32[]{:S(2)}, u32[]{:S(2)}) collective-permute-start(bf16[48,288]{1,0:T(8,128)(2,1)} %param.13), channel_id=1, source_target_pairs={{0,8},{1,9},{2,10},{3,11},{4,12},{5,13},{6,14},{7,15},{8,0},{9,1},... | collective-permute-start | bytes 82952 | tf_op jit(solution)/shard_map/ppermute | solution.py:708
  4.0 2.5 %features_first.1 = (bf16[19,416,256]{2,1,0:T(8,128)(2,1)S(1)}, f8e5m2[19,416,256]{2,1,0:T(32,128)(4,1)S(1)}, f32[2,36,8,128]{3,2,1,0:T(8,128)S(1)}, f32[8,128]{1,0:T(8,128)S(1)}, f32[20,72,128]{2,1,0:T(8,128)S(1)}) custom-call(s32[8]{0:T(128)} %grp_hbm.1, s32[8]{0:T(128)} %bin_hbm.1, bf16[8,4608]{1,0:T(8,128)(2,1)} %img_hbm.1, f32[16,16]{1,0:T(8,128)} %sig_hbm.1, ...), custom_call_target="tpu_custom_call" | custom-call | flops 4499999744 | bytes 13500000 | tf_op jit(solution)/shard_map/features_first/pallas_call | solution.py:383
  6.5 0.2 collective-permute-done
  6.7 0.0 copy-done
  6.7 0.1 collective-permute-start.2
  6.8 1.7 %collective-permute-start.1 = (bf16[2,48,288]{2,1,0:T(8,128)(2,1)S(1)}, bf16[2,48,288]{2,1,0:T(8,128)(2,1)S(1)}, u32[]{:S(2)}, u32[]{:S(2)}) collective-permute-start(bf16[2,48,288]{2,1,0:T(8,128)(2,1)S(1)} %pad_maximum_fusion.r0_ref), channel_id=1, source_target_pairs={{0,2},{1,3},{2,0},{3,1},{4,6},{5,7},{6,4},{7,5},{8,10},{9,11},{10,... | collective-permute-start | bytes 165896 | tf_op jit(solution)/shard_map/ppermute | solution.py:708
  8.5 1.3 %collective-permute-start.3 = (bf16[2,48,288]{2,1,0:T(8,128)(2,1)S(1)}, bf16[2,48,288]{2,1,0:T(8,128)(2,1)S(1)}, u32[]{:S(2)}, u32[]{:S(2)}) collective-permute-start(bf16[2,48,288]{2,1,0:T(8,128)(2,1)S(1)} %pad_maximum_fusion.r0_ref), channel_id=1, source_target_pairs={{0,4},{1,5},{2,6},{3,7},{4,0},{5,1},{6,2},{7,3},{8,12},{9,13},{10,... | collective-permute-start | bytes 165896 | tf_op jit(solution)/shard_map/ppermute | solution.py:708
  9.8 0.5 %collective-permute-start.4 = (bf16[2,48,288]{2,1,0:T(8,128)(2,1)S(1)}, bf16[2,48,288]{2,1,0:T(8,128)(2,1)S(1)}, u32[]{:S(2)}, u32[]{:S(2)}) collective-permute-start(bf16[2,48,288]{2,1,0:T(8,128)(2,1)S(1)} %pad_maximum_fusion.r0_ref), channel_id=1, source_target_pairs={{0,6},{1,7},{2,4},{3,5},{4,2},{5,3},{6,0},{7,1},{8,14},{9,15},{10,... | collective-permute-start | bytes 165896 | tf_op jit(solution)/shard_map/ppermute | solution.py:708
  10.3 4.0 %features_second.1 = (bf16[19,416,256]{2,1,0:T(8,128)(2,1)S(1)}, f8e5m2[19,416,256]{2,1,0:T(32,128)(4,1)S(1)}, bf16[2,304,288]{2,1,0:T(8,128)(2,1)S(1)}, bf16[2,512,288]{2,1,0:T(8,128)(2,1)S(1)}) custom-call(bf16[19,416,256]{2,1,0:T(8,128)(2,1)S(1)} %get-tuple-element.26.fh_in, ...), custom_call_target="tpu_custom_call", output_to_operand_aliasing={{0}: (0, {}), {1}: (1, {})} | custom-call | flops 2500000000 | bytes 7500000 | tf_op jit(solution)/shard_map/features_second/pallas_call | solution.py:418
  14.4 0.0 collective-permute-done.2.s0_ref
  14.4 0.0 collective-permute-done.1.r1_ref
  14.4 0.0 collective-permute-done.3.r2_ref
  14.4 0.7 %collective-permute-done.4.r3_ref = bf16[2,48,288]{2,1,0:T(8,128)(2,1)S(1)} collective-permute-done((bf16[2,48,288]{2,1,0:T(8,128)(2,1)S(1)}, bf16[2,48,288]{2,1,0:T(8,128)(2,1)S(1)}, u32[]{:S(2)}, u32[]{:S(2)}) %collective-permute-start.4) | collective-permute-done | bytes 55328 | tf_op jit(solution)/shard_map/ppermute | solution.py:708
  15.0 0.0 collective-permute-start.7
  15.0 0.5 %collective-permute-start.6 = (bf16[2,48,288]{2,1,0:T(8,128)(2,1)S(1)}, bf16[2,48,288]{2,1,0:T(8,128)(2,1)S(1)}, u32[]{:S(2)}, u32[]{:S(2)}) collective-permute-start(bf16[2,48,288]{2,1,0:T(8,128)(2,1)S(1)} %collective-permute-done.3.r2_ref), channel_id=1, source_target_pairs={{0,1},{1,0},{2,3},{3,2},{4,5},{5,4},{6,7},{7,6},{8,9},{9,8},{10,11... | collective-permute-start | bytes 165896 | tf_op jit(solution)/shard_map/ppermute | solution.py:708
  15.6 0.0 collective-permute-start.5
  15.6 0.8 %collective-permute-done.7.s3_ref = bf16[2,48,288]{2,1,0:T(8,128)(2,1)S(1)} collective-permute-done((bf16[2,48,288]{2,1,0:T(8,128)(2,1)S(1)}, bf16[2,48,288]{2,1,0:T(8,128)(2,1)S(1)}, u32[]{:S(2)}, u32[]{:S(2)}) %collective-permute-start.7) | collective-permute-done | bytes 55328 | tf_op jit(solution)/shard_map/ppermute | solution.py:708
  16.3 0.2 collective-permute-done.6.s2_ref
  16.5 0.4 collective-permute-done.5.s1_ref
  16.8 7.1 %posterior.1 = bf16[2,8,120,128]{3,2,1,0:T(8,128)(2,1)S(1)} custom-call(bf16[2,48,288]{2,1,0:T(8,128)(2,1)S(1)} %pad_maximum_fusion.r0_ref, bf16[2,48,288]{2,1,0:T(8,128)(2,1)S(1)} %collective-permute-done.1.r1_ref, bf16[2,48,288]{2,1,0:T(8,128)(2,1)S(1)} %collective-permute-done.3.r2_ref, bf16[2,48,288]{2,1,0:T(8,128)(2,1)S(1)} %collective-permute-done.4.r3_ref, ...), custom_call_target="tpu_custom_call" | custom-call | flops 10000000000 | bytes 30000000 | tf_op jit(solution)/shard_map/posterior/pallas_call | solution.py:642
  24.0 0.2 collective-permute-start.8
  24.2 1.4 %collective-permute-done.8 = bf16[8,120,128]{2,1,0:T(8,128)(2,1)S(1)} collective-permute-done((bf16[8,120,128]{2,1,0:T(8,128)(2,1)S(1)}, bf16[8,120,128]{2,1,0:T(8,128)(2,1)S(1)}, u32[]{:S(2)}, u32[]{:S(2)}) %collective-permute-start.8) | collective-permute-done | bytes 245792 | tf_op jit(solution)/shard_map/ppermute | solution.py:708
  25.6 0.1 fusion.3
  25.7 0.9 %collective-permute-start.10 = (bf16[2,120,128]{2,1,0:T(8,128)(2,1)S(1)}, bf16[2,120,128]{2,1,0:T(8,128)(2,1)S(1)}, u32[]{:S(2)}, u32[]{:S(2)}) collective-permute-start(bf16[2,120,128]{2,1,0:T(8,128)(2,1)S(1)} %get-tuple-element.47), channel_id=1, source_target_pairs={{0,4},{1,5},{2,6},{3,7},{4,0},{5,1},{6,2},{7,3},{8,12},{9,13},{10,... | collective-permute-start | bytes 184328 | tf_op jit(solution)/shard_map/ppermute | solution.py:708
  26.6 1.7 %collective-permute-start.11 = (bf16[2,120,128]{2,1,0:T(8,128)(2,1)S(1)}, bf16[2,120,128]{2,1,0:T(8,128)(2,1)S(1)}, u32[]{:S(2)}, u32[]{:S(2)}) collective-permute-start(bf16[2,120,128]{2,1,0:T(8,128)(2,1)S(1)} %get-tuple-element.46), channel_id=1, source_target_pairs={{0,6},{1,7},{2,4},{3,5},{4,2},{5,3},{6,0},{7,1},{8,14},{9,15},{10,... | collective-permute-start | bytes 184328 | tf_op jit(solution)/shard_map/ppermute | solution.py:708
  28.3 0.9 %collective-permute-start.9 = (bf16[2,120,128]{2,1,0:T(8,128)(2,1)S(1)}, bf16[2,120,128]{2,1,0:T(8,128)(2,1)S(1)}, u32[]{:S(2)}, u32[]{:S(2)}) collective-permute-start(bf16[2,120,128]{2,1,0:T(8,128)(2,1)S(1)} %get-tuple-element.45), channel_id=1, source_target_pairs={{0,2},{1,3},{2,0},{3,1},{4,6},{5,7},{6,4},{7,5},{8,10},{9,11},{10,... | collective-permute-start | bytes 184328 | tf_op jit(solution)/shard_map/ppermute | solution.py:708
  29.2 0.7 %collective-permute-done.10 = bf16[2,120,128]{2,1,0:T(8,128)(2,1)S(1)} collective-permute-done((bf16[2,120,128]{2,1,0:T(8,128)(2,1)S(1)}, bf16[2,120,128]{2,1,0:T(8,128)(2,1)S(1)}, u32[]{:S(2)}, u32[]{:S(2)}) %collective-permute-start.10) | collective-permute-done | bytes 61472 | tf_op jit(solution)/shard_map/ppermute | solution.py:708
  29.9 2.0 %collective-permute-done.11 = bf16[2,120,128]{2,1,0:T(8,128)(2,1)S(1)} collective-permute-done((bf16[2,120,128]{2,1,0:T(8,128)(2,1)S(1)}, bf16[2,120,128]{2,1,0:T(8,128)(2,1)S(1)}, u32[]{:S(2)}, u32[]{:S(2)}) %collective-permute-start.11) | collective-permute-done | bytes 61472 | tf_op jit(solution)/shard_map/ppermute | solution.py:708
  31.9 0.9 %collective-permute-done.9 = bf16[2,120,128]{2,1,0:T(8,128)(2,1)S(1)} collective-permute-done((bf16[2,120,128]{2,1,0:T(8,128)(2,1)S(1)}, bf16[2,120,128]{2,1,0:T(8,128)(2,1)S(1)}, u32[]{:S(2)}, u32[]{:S(2)}) %collective-permute-start.9) | collective-permute-done | bytes 61472 | tf_op jit(solution)/shard_map/ppermute | solution.py:708
  32.9 2.7 %collective-permute-start.12 = (bf16[120,128]{1,0:T(8,128)(2,1)S(1)}, bf16[120,128]{1,0:T(8,128)(2,1)S(1)}, u32[]{:S(2)}, u32[]{:S(2)}) collective-permute-start(bf16[120,128]{1,0:T(8,128)(2,1)S(1)} %fusion.2), channel_id=1, source_target_pairs={{0,8},{1,9},{2,10},{3,11},{4,12},{5,13},{6,14},{7,15},{8,0},{9,1},... | collective-permute-start | bytes 92168 | tf_op jit(solution)/shard_map/ppermute | solution.py:708
  35.6 2.2 %collective-permute-done.12.got_ref = bf16[120,128]{1,0:T(8,128)(2,1)S(1)} collective-permute-done((bf16[120,128]{1,0:T(8,128)(2,1)S(1)}, bf16[120,128]{1,0:T(8,128)(2,1)S(1)}, u32[]{:S(2)}, u32[]{:S(2)}) %collective-permute-start.12) | collective-permute-done | bytes 30752 | tf_op jit(solution)/shard_map/ppermute | solution.py:708
  37.8 1.0 %finish.1 = f32[48,288]{1,0:T(8,128)} custom-call(f32[120,128]{1,0:T(8,128)S(1)} %slice_bitcast_fusion.2.keep_ref, bf16[120,128]{1,0:T(8,128)(2,1)S(1)} %collective-permute-done.12.got_ref, bf16[2,512,288]{2,1,0:T(8,128)(2,1)S(1)} %get-tuple-element.42.back_ref), custom_call_target="tpu_custom_call" | custom-call | flops 1000000000 | bytes 3000000 | tf_op jit(solution)/shard_map/finish/pallas_call | solution.py:695
  (6 shorter events, 0.1 us)
Async XLA Ops:
  0.0 6.7 %copy-start = (bf16[48,288]{1,0:T(8,128)(2,1)S(1)}, bf16[48,288]{1,0:T(8,128)(2,1)}, u32[]{:S(2)}) copy-start(bf16[48,288]{1,0:T(8,128)(2,1)} %param.13) | copy-start | bytes 82948
  0.0 6.6 %collective-permute-start = (bf16[48,288]{1,0:T(8,128)(2,1)}, bf16[48,288]{1,0:T(8,128)(2,1)S(1)}, u32[]{:S(2)}, u32[]{:S(2)}) collective-permute-start(bf16[48,288]{1,0:T(8,128)(2,1)} %param.13), channel_id=1, source_target_pairs={{0,8},{1,9},{2,10},{3,11},{4,12},{5,13},{6,14},{7,15},{8,0},{9,1},... | collective-permute-start | bytes 82952 | tf_op jit(solution)/shard_map/ppermute | solution.py:708
  6.7 7.7 %collective-permute-start.2 = (bf16[2,48,288]{2,1,0:T(8,128)(2,1)S(1)}, bf16[2,48,288]{2,1,0:T(8,128)(2,1)S(1)}, u32[]{:S(2)}, u32[]{:S(2)}) collective-permute-start(bf16[2,48,288]{2,1,0:T(8,128)(2,1)S(1)} %pad_maximum_fusion.r0_ref), channel_id=1, source_target_pairs={{0,1},{1,0},{2,3},{3,2},{4,5},{5,4},{6,7},{7,6},{8,9},{9,8},{10,11... | collective-permute-start | bytes 165896 | tf_op jit(solution)/shard_map/ppermute | solution.py:708
  6.8 7.6 %collective-permute-start.1 = (bf16[2,48,288]{2,1,0:T(8,128)(2,1)S(1)}, bf16[2,48,288]{2,1,0:T(8,128)(2,1)S(1)}, u32[]{:S(2)}, u32[]{:S(2)}) collective-permute-start(bf16[2,48,288]{2,1,0:T(8,128)(2,1)S(1)} %pad_maximum_fusion.r0_ref), channel_id=1, source_target_pairs={{0,2},{1,3},{2,0},{3,1},{4,6},{5,7},{6,4},{7,5},{8,10},{9,11},{10,... | collective-permute-start | bytes 165896 | tf_op jit(solution)/shard_map/ppermute | solution.py:708
  8.5 5.9 %collective-permute-start.3 = (bf16[2,48,288]{2,1,0:T(8,128)(2,1)S(1)}, bf16[2,48,288]{2,1,0:T(8,128)(2,1)S(1)}, u32[]{:S(2)}, u32[]{:S(2)}) collective-permute-start(bf16[2,48,288]{2,1,0:T(8,128)(2,1)S(1)} %pad_maximum_fusion.r0_ref), channel_id=1, source_target_pairs={{0,4},{1,5},{2,6},{3,7},{4,0},{5,1},{6,2},{7,3},{8,12},{9,13},{10,... | collective-permute-start | bytes 165896 | tf_op jit(solution)/shard_map/ppermute | solution.py:708
  9.8 5.3 %collective-permute-start.4 = (bf16[2,48,288]{2,1,0:T(8,128)(2,1)S(1)}, bf16[2,48,288]{2,1,0:T(8,128)(2,1)S(1)}, u32[]{:S(2)}, u32[]{:S(2)}) collective-permute-start(bf16[2,48,288]{2,1,0:T(8,128)(2,1)S(1)} %pad_maximum_fusion.r0_ref), channel_id=1, source_target_pairs={{0,6},{1,7},{2,4},{3,5},{4,2},{5,3},{6,0},{7,1},{8,14},{9,15},{10,... | collective-permute-start | bytes 165896 | tf_op jit(solution)/shard_map/ppermute | solution.py:708
  15.0 1.3 %collective-permute-start.7 = (bf16[2,48,288]{2,1,0:T(8,128)(2,1)S(1)}, bf16[2,48,288]{2,1,0:T(8,128)(2,1)S(1)}, u32[]{:S(2)}, u32[]{:S(2)}) collective-permute-start(bf16[2,48,288]{2,1,0:T(8,128)(2,1)S(1)} %collective-permute-done.4.r3_ref), channel_id=1, source_target_pairs={{0,1},{1,0},{2,3},{3,2},{4,5},{5,4},{6,7},{7,6},{8,9},{9,8},{10,11... | collective-permute-start | bytes 165896 | tf_op jit(solution)/shard_map/ppermute | solution.py:708
  15.0 1.4 %collective-permute-start.6 = (bf16[2,48,288]{2,1,0:T(8,128)(2,1)S(1)}, bf16[2,48,288]{2,1,0:T(8,128)(2,1)S(1)}, u32[]{:S(2)}, u32[]{:S(2)}) collective-permute-start(bf16[2,48,288]{2,1,0:T(8,128)(2,1)S(1)} %collective-permute-done.3.r2_ref), channel_id=1, source_target_pairs={{0,1},{1,0},{2,3},{3,2},{4,5},{5,4},{6,7},{7,6},{8,9},{9,8},{10,11... | collective-permute-start | bytes 165896 | tf_op jit(solution)/shard_map/ppermute | solution.py:708
  15.6 1.3 %collective-permute-start.5 = (bf16[2,48,288]{2,1,0:T(8,128)(2,1)S(1)}, bf16[2,48,288]{2,1,0:T(8,128)(2,1)S(1)}, u32[]{:S(2)}, u32[]{:S(2)}) collective-permute-start(bf16[2,48,288]{2,1,0:T(8,128)(2,1)S(1)} %collective-permute-done.1.r1_ref), channel_id=1, source_target_pairs={{0,1},{1,0},{2,3},{3,2},{4,5},{5,4},{6,7},{7,6},{8,9},{9,8},{10,11... | collective-permute-start | bytes 165896 | tf_op jit(solution)/shard_map/ppermute | solution.py:708
  24.0 1.6 %collective-permute-start.8 = (bf16[8,120,128]{2,1,0:T(8,128)(2,1)S(1)}, bf16[8,120,128]{2,1,0:T(8,128)(2,1)S(1)}, u32[]{:S(2)}, u32[]{:S(2)}) collective-permute-start(bf16[8,120,128]{2,1,0:T(8,128)(2,1)S(1)} %slice_bitcast_fusion), channel_id=1, source_target_pairs={{0,1},{1,0},{2,3},{3,2},{4,5},{5,4},{6,7},{7,6},{8,9},{9,8},{10,11... | collective-permute-start | bytes 737288 | tf_op jit(solution)/shard_map/ppermute | solution.py:708
  25.7 4.3 %collective-permute-start.10 = (bf16[2,120,128]{2,1,0:T(8,128)(2,1)S(1)}, bf16[2,120,128]{2,1,0:T(8,128)(2,1)S(1)}, u32[]{:S(2)}, u32[]{:S(2)}) collective-permute-start(bf16[2,120,128]{2,1,0:T(8,128)(2,1)S(1)} %get-tuple-element.47), channel_id=1, source_target_pairs={{0,4},{1,5},{2,6},{3,7},{4,0},{5,1},{6,2},{7,3},{8,12},{9,13},{10,... | collective-permute-start | bytes 184328 | tf_op jit(solution)/shard_map/ppermute | solution.py:708
  26.6 5.3 %collective-permute-start.11 = (bf16[2,120,128]{2,1,0:T(8,128)(2,1)S(1)}, bf16[2,120,128]{2,1,0:T(8,128)(2,1)S(1)}, u32[]{:S(2)}, u32[]{:S(2)}) collective-permute-start(bf16[2,120,128]{2,1,0:T(8,128)(2,1)S(1)} %get-tuple-element.46), channel_id=1, source_target_pairs={{0,6},{1,7},{2,4},{3,5},{4,2},{5,3},{6,0},{7,1},{8,14},{9,15},{10,... | collective-permute-start | bytes 184328 | tf_op jit(solution)/shard_map/ppermute | solution.py:708
  28.3 4.6 %collective-permute-start.9 = (bf16[2,120,128]{2,1,0:T(8,128)(2,1)S(1)}, bf16[2,120,128]{2,1,0:T(8,128)(2,1)S(1)}, u32[]{:S(2)}, u32[]{:S(2)}) collective-permute-start(bf16[2,120,128]{2,1,0:T(8,128)(2,1)S(1)} %get-tuple-element.45), channel_id=1, source_target_pairs={{0,2},{1,3},{2,0},{3,1},{4,6},{5,7},{6,4},{7,5},{8,10},{9,11},{10,... | collective-permute-start | bytes 184328 | tf_op jit(solution)/shard_map/ppermute | solution.py:708
  32.9 4.9 %collective-permute-start.12 = (bf16[120,128]{1,0:T(8,128)(2,1)S(1)}, bf16[120,128]{1,0:T(8,128)(2,1)S(1)}, u32[]{:S(2)}, u32[]{:S(2)}) collective-permute-start(bf16[120,128]{1,0:T(8,128)(2,1)S(1)} %fusion.2), channel_id=1, source_target_pairs={{0,8},{1,9},{2,10},{3,11},{4,12},{5,13},{6,14},{7,15},{8,0},{9,1},... | collective-permute-start | bytes 92168 | tf_op jit(solution)/shard_map/ppermute | solution.py:708
